TPU v7x, 256 devices: a whole 4x4x8 slice. The times are simulated.
256 devices in a mesh: section: 8 (over y_lo, x), dp: 32 (over y_hi, z, core).
Axes of the slice: x: 4, y: 4 (y_hi: 2, y_lo: 2; y = y_hi * 2 + y_lo), z: 8, core: 2. Of those that a mesh axis runs over, the one named last changes fastest.
Arguments:
- arriving: bfloat16 [8, 32, 128, 8192], P('section', 'dp'), may hold values from -6 to 6
- returning: bfloat16 [8, 32, 128, 8192], P('section', 'dp'), may hold values from -6 to 6
- gain: float32 [8, 8192], P('section'), may hold values from 0.1 to 1.9
- section_down_weight: bfloat16 [8, 128, 8192], P('section', None, 'dp'), may hold values from -0.0625 to 0.0625
- section_up_weight: bfloat16 [8, 128, 8192], P('section', None, 'dp'), may hold values from -0.5 to 0.5
- failed: int32 [8], replicated, may hold values from 0 to 31
- route: int32 [8, 32], replicated, may hold values from 0 to 31, each once within a row
Outputs:
- forward_out: bfloat16 [8, 32, 128, 8192], P('section', 'dp')
- backward_out: bfloat16 [8, 32, 128, 8192], P('section', 'dp')
- rerouted_forward: bfloat16 [8, 128, 8192], P('section', 'dp')
- rerouted_backward: bfloat16 [8, 128, 8192], P('section', 'dp')
- grad_down: float32 [8, 128, 8192], P('section', None, 'dp')
- grad_up: float32 [8, 128, 8192], P('section', None, 'dp')
All inputs are finite; a program needn't handle non-finite values.
Results may differ from a plain program's by a relative error of at most 0.005.
Values may be sent and summed in bfloat16 or wider, within the bound.
No kernel may reach another device: no remote copies, remote signals or barrier semaphores. Data moves between devices by JAX's collectives and lax.ppermute only.
A program may use at most 128 MiB of HBM per device.

v0:
```python
import jax
import jax.numpy as jnp
from jax import lax
from jax.sharding import PartitionSpec as P

eps = 1e-05


def from_behind(block, axis, distance):
    devices = range(lax.axis_size(axis))
    route = [((i - distance) % len(devices), i) for i in devices]
    return lax.ppermute(block, axis, route)


def from_root(block, axis, source):
    block = jnp.where(lax.axis_index(axis) == source, block, jnp.zeros_like(block))
    return lax.psum(block, axis)


def body(arriving, returning, gain, section_down_weight, section_up_weight, failed, route):
    section = lax.axis_index("section")
    rank = lax.axis_index("dp")
    replicas = lax.axis_size("dp")
    count = arriving.shape[2]
    width = arriving.shape[3]
    share = count // replicas
    half_rows = count // 2
    lost = failed[section]
    order = route[section]
    block_start = order[rank] * share
    near_helper = (lost + 1) % replicas
    far_helper = (lost + replicas // 2) % replicas
    inbound = from_behind(arriving, "section", 1)
    upstream = from_behind(returning, "section", -1)
    own_x = inbound[0, 0]
    own_g = upstream[0, 0]
    moved_x, moved_g = (from_root(own_x, "dp", lost), from_root(own_g, "dp", lost))
    keeps = rank != lost
    blank = jnp.zeros((count, width), jnp.bfloat16)
    blank_half = jnp.zeros((half_rows, width), jnp.bfloat16)
    is_near = rank == near_helper
    is_far = rank == far_helper
    extra_x = jnp.where(
        is_near, moved_x[:half_rows], jnp.where(is_far, moved_x[half_rows:], blank_half)
    )
    extra_g = jnp.where(
        is_near, moved_g[:half_rows], jnp.where(is_far, moved_g[half_rows:], blank_half)
    )
    acts = jnp.concatenate([jnp.where(keeps, own_x, blank), extra_x], axis=0)
    grads = jnp.concatenate([jnp.where(keeps, own_g, blank), extra_g], axis=0)
    down_full, up_full = (
        lax.all_gather(section_down_weight, "dp", axis=2, tiled=True),
        lax.all_gather(section_up_weight, "dp", axis=2, tiled=True),
    )
    down_weight = down_full[0]
    up_weight = up_full[0]
    scale = gain[0]
    act32 = acts.astype(jnp.float32)

    def normalize(rows):
        inv = lax.rsqrt(jnp.mean(rows * rows, axis=-1, keepdims=True) + eps)
        return rows * inv * scale

    normed32, pull = jax.vjp(normalize, act32)
    normed = normed32.astype(jnp.bfloat16)
    low = lax.dot_general(
        normed, down_weight, (((1,), (1,)), ((), ())), preferred_element_type=jnp.float32
    ).astype(jnp.bfloat16)
    lifted = jnp.dot(low, up_weight, preferred_element_type=jnp.float32)
    outputs = (act32 + lifted).astype(jnp.bfloat16)
    back_low = lax.dot_general(
        grads, up_weight, (((1,), (1,)), ((), ())), preferred_element_type=jnp.float32
    ).astype(jnp.bfloat16)
    back_norm = jnp.dot(back_low, down_weight, preferred_element_type=jnp.float32)
    back_x = (grads.astype(jnp.float32) + pull(back_norm)[0]).astype(jnp.bfloat16)
    contract_rows = (((0,), (0,)), ((), ()))
    part_down = lax.dot_general(normed, back_low, contract_rows, preferred_element_type=jnp.float32)
    part_up = lax.dot_general(grads, low, contract_rows, preferred_element_type=jnp.float32)
    summed = lax.psum_scatter(
        jnp.concatenate([part_down, part_up], axis=1), "dp", scatter_dimension=0, tiled=True
    )
    rank_width = low.shape[1]
    grad_down = (summed[:, :rank_width].T / replicas)[None]
    grad_up = (summed[:, rank_width:].T / replicas)[None]
    forward_out = outputs[:count].reshape(1, 1, count, width)
    backward_out = back_x[:count].reshape(1, 1, count, width)
    pieces = []
    for helper_rank in (near_helper, far_helper):
        pieces.append(
            (
                from_root(outputs[count:], "dp", helper_rank),
                from_root(back_x[count:], "dp", helper_rank),
            )
        )
    whole_f = jnp.concatenate([pieces[0][0], pieces[1][0]], axis=0)
    whole_b = jnp.concatenate([pieces[0][1], pieces[1][1]], axis=0)
    rerouted_f = lax.dynamic_slice_in_dim(whole_f, block_start, share, 0)
    rerouted_b = lax.dynamic_slice_in_dim(whole_b, block_start, share, 0)
    return (forward_out, backward_out, rerouted_f[None], rerouted_b[None], grad_down, grad_up)


def solution(mesh):
    return jax.shard_map(
        body,
        mesh=mesh,
        in_specs=(
            P("section", "dp", None, None),
            P("section", "dp", None, None),
            P("section", None),
            P("section", None, "dp"),
            P("section", None, "dp"),
            P(),
            P(),
        ),
        out_specs=(
            P("section", "dp", None, None),
            P("section", "dp", None, None),
            P("section", "dp", None),
            P("section", "dp", None),
            P("section", None, "dp"),
            P("section", None, "dp"),
        ),
        check_vma=False,
    )
```

profile of v0, /device:TPU:6, one launch (start us, length us, event | category | flops | bytes accessed | tf_op | source)
XLA Modules:
  0.0 951.2 jit_solution(2313549252625182807)
XLA Ops:
  7.2 0.9 collective-permute-start.1
  8.1 3.3 collective-permute-start
  11.4 1.2 dynamic_slice.13
  14.0 43.0 %collective-permute-done.1 = bf16[1,1,128,8192]{3,2,1,0:T(8,128)(2,1)S(1)} collective-permute-done((bf16[1,1,128,8192]{3,2,1,0:T(8,128)(2,1)}, bf16[1,1,128,8192]{3,2,1,0:T(8,128)(2,1)S(1)}, u32[]{:S(2)}, u32[]{:S(2)}) %collective-permute-start.1) | collective-permute-done | bytes 2097184 | tf_op jit(solution)/shard_map/ppermute | solution.py:12
  57.0 2.3 select_bitcast_fusion.1
  59.3 3.2 select_bitcast_fusion.3
  62.5 0.7 all-gather.5.cloned.1.call-update
  63.2 0.7 all-gather.3.cloned.1.call-update
  65.3 278.1 %all-reduce.7.cloned.1.call-done = (bf16[128,8192]{1,0:T(8,128)(2,1)}, bf16[128,8192]{1,0:T(8,128)(2,1)}) async-done(((bf16[128,8192]{1,0:T(8,128)(2,1)}, bf16[128,8192]{1,0:T(8,128)(2,1)}), (bf16[128,8192]{1,0:T(8,128)(2,1)}, bf16[128,8192]{1,0:T(8,128)(2,1)})) %all-reduce.7.cloned.1.call-update) | async-done | bytes 4194320 | tf_op jit(solution)/shard_map/psum | solution.py:17
  343.5 1.7 fusion.19
  345.1 76.9 %all-gather.5.cloned.1.call-done = bf16[1,128,8192]{2,1,0:T(8,128)(2,1)} async-done(((bf16[1,128,256]{2,1,0:T(8,128)(2,1)}), bf16[1,128,8192]{2,1,0:T(8,128)(2,1)}) %all-gather.5.cloned.1.call-update) | async-done | bytes 2097168 | tf_op jit(solution)/shard_map/all_gather | solution.py:53
  422.1 3.3 fusion.16
  425.4 0.1 fusion.20
  425.6 72.5 %all-gather.3.cloned.1.call-done = bf16[1,128,8192]{2,1,0:T(8,128)(2,1)} async-done(((bf16[1,128,256]{2,1,0:T(8,128)(2,1)}), bf16[1,128,8192]{2,1,0:T(8,128)(2,1)}) %all-gather.3.cloned.1.call-update) | async-done | bytes 2097168 | tf_op jit(solution)/shard_map/all_gather | solution.py:52
  498.0 3.3 fusion.6
  501.4 2.3 fusion.2
  503.7 1.1 fusion.13
  504.8 1.6 copy-done.7
  506.4 1.0 fusion
  507.4 2.1 broadcast_select_fusion.2
  509.6 0.8 copy-done.2
  510.4 0.0 reduce-scatter.2.cloned.1.call-start
  510.5 2.7 fusion.21
  513.1 1.0 fusion.22
  514.2 3.8 pad_maximum_fusion
  518.0 1.4 dynamic_slice.14
  520.1 3.9 slice_bitcast_fusion
  524.1 261.6 %all-reduce.5.cloned.1.call-done = (bf16[64,8192]{1,0:T(8,128)(2,1)}, bf16[64,8192]{1,0:T(8,128)(2,1)}, bf16[64,8192]{1,0:T(8,128)(2,1)}, bf16[64,8192]{1,0:T(8,128)(2,1)}) async-done(((bf16[64,8192]{1,0:T(8,128)(2,1)}, bf16[64,8192]{1,0:T(8,128)(2,1)}, bf16[64,8192]{1,0:T(8,128)(2,1)}, bf16[64,8192]{1,0:T(8,128)(2,1)}), (bf16[64,8192]{1,0:T(8,128)(2,1)}, bf16[64,8192]{1,0:T(8,128)(2,1)}, ...) | async-done | bytes 4194320 | tf_op jit(solution)/shard_map/psum | solution.py:17
  785.7 1.6 fusion.29
  787.3 1.6 fusion.30
  788.9 154.0 %reduce-scatter.2.cloned.1.call-done = f32[256,256]{0,1:T(8,128)} async-done(((f32[8192,256]{0,1:T(8,128)}), f32[256,256]{0,1:T(8,128)}) %reduce-scatter.2.cloned.1.call-update) | async-done | bytes 262160 | tf_op jit(solution)/shard_map/reduce_scatter | solution.py:79
  943.0 1.7 fusion.25
  (27 shorter events, 0.3 us)
Async XLA Ops:
  7.2 336.3 %all-reduce.7.cloned.1.call-start = ((), (), s32[]{:S(2)}) async-start(), calls=%async_computation.5 | async-start | bytes 8388608 | tf_op jit(solution)/shard_map/psum | solution.py:17
  7.2 49.8 %collective-permute-start.1 = (bf16[1,1,128,8192]{3,2,1,0:T(8,128)(2,1)}, bf16[1,1,128,8192]{3,2,1,0:T(8,128)(2,1)S(1)}, u32[]{:S(2)}, u32[]{:S(2)}) collective-permute-start(bf16[1,1,128,8192]{3,2,1,0:T(8,128)(2,1)} %param.8), channel_id=1, source_target_pairs={{32,0},{64,32},{96,64},{128,96},{160,128},{192,160},{224,192},{0,2... | collective-permute-start | bytes 6291464 | tf_op jit(solution)/shard_map/ppermute | solution.py:12
  8.1 51.1 %collective-permute-start = (bf16[1,1,128,8192]{3,2,1,0:T(8,128)(2,1)}, bf16[1,1,128,8192]{3,2,1,0:T(8,128)(2,1)}, u32[]{:S(2)}, u32[]{:S(2)}) collective-permute-start(bf16[1,1,128,8192]{3,2,1,0:T(8,128)(2,1)} %param.7), channel_id=1, source_target_pairs={{224,0},{0,32},{32,64},{64,96},{96,128},{128,160},{160,192},{192,2... | collective-permute-start | bytes 6291464 | tf_op jit(solution)/shard_map/ppermute | solution.py:12
  62.4 359.6 %all-gather.5.cloned.1.call-start = ((), (), s32[]{:S(2)}) async-start(), calls=%async_computation.2 | async-start | bytes 2162688 | tf_op jit(solution)/shard_map/all_gather | solution.py:53
  63.2 434.8 %all-gather.3.cloned.1.call-start = ((), (), s32[]{:S(2)}) async-start(), calls=%async_computation.1 | async-start | bytes 2162688 | tf_op jit(solution)/shard_map/all_gather | solution.py:52
  63.9 721.8 %all-reduce.5.cloned.1.call-start = ((), (), s32[]{:S(2)}) async-start(), calls=%async_computation.4 | async-start | bytes 8388608 | tf_op jit(solution)/shard_map/psum | solution.py:17
  345.1 80.3 %copy-start.4 = (bf16[64,8192]{1,0:T(8,128)(2,1)}, bf16[64,8192]{1,0:T(8,128)(2,1)S(1)}, u32[]{:S(2)}) copy-start(bf16[64,8192]{1,0:T(8,128)(2,1)S(1)} %fusion.19) | copy-start | bytes 3145732
  422.1 3.4 copy-start.6
  425.4 72.6 %copy-start.9 = (f32[1,8192]{1,0:T(1,128)S(1)}, f32[1,8192]{1,0:T(1,128)}, u32[]{:S(2)}) copy-start(f32[1,8192]{1,0:T(1,128)} %param.9) | copy-start | bytes 98308
  498.0 3.3 copy-start.3
  498.0 3.3 copy-start.5
  501.4 2.3 copy-start.8
  503.7 3.7 copy-start
  503.7 2.7 copy-start.7
  507.4 3.0 copy-start.2
  510.4 432.6 %reduce-scatter.2.cloned.1.call-start = ((), (), s32[]{:S(2)}) async-start(), calls=%async_computation.3 | async-start | bytes 8650752 | tf_op jit(solution)/shard_map/reduce_scatter | solution.py:79
  518.0 2.1 copy-start.1
Sparse Core Ops, SparseCore 0:
  62.6 280.8 all-reduce.6
  346.0 75.9 all-gather.4
  424.6 73.3 all-gather.2
  510.5 275.1 all-reduce.4
  789.9 152.9 reduce-scatter.1
where the time goes:
time: 952 us; the launch traced here: 951 us
  waiting for transfers between devices  888 us (93%)
  other arithmetic  20.4 us (2%)
  between operations  17.3 us (2%)
  matrix products  12.4 us (1%)
    psum x2, waiting for transfers between devices, from_root(): return lax.psum(block, axis)  540 us
    reduce_scatter x1, waiting for transfers between devices, body(): lax.psum_scatter(jnp.concatenate([part_down, part_up], axis=1), 'dp', sca...  154 us
    all_gather x1, waiting for transfers between devices, body(): lax.all_gather(section_up_weight, 'dp', axis=2, tiled=True)  76.9 us
    all_gather x1, waiting for transfers between devices, body(): lax.all_gather(section_down_weight, 'dp', axis=2, tiled=True)  72.5 us
    ppermute x2, waiting for transfers between devices, from_behind(): return lax.ppermute(block, axis, route)  43 us
  transfers between devices with their start and end apart: 7, of which 6 were waited for; matrix products, arithmetic and copies ran while one was open for 3% of the time, Pallas kernels for 0%

commit v1 on v0

v1 whole, which is shorter than its diff:
```python
import jax
import jax.numpy as jnp
from jax import lax
from jax.experimental import pallas as pl
from jax.experimental.pallas import tpu as pltpu
from jax.sharding import PartitionSpec as P

eps = 1e-05
N_Z = 8
N_DP = 32
BLOCK = 256
F32 = jnp.float32
BF16 = jnp.bfloat16


def place(y, z, c):
    return (y * N_Z + z) * 2 + c


PLACES = [(y, z, c) for y in range(2) for z in range(N_Z) for c in range(2)]
TO_CORE = [(place(y, z, c), place(y, z, 1 - c)) for y, z, c in PLACES]
TO_Y = [(place(y, z, c), place(1 - y, z, c)) for y, z, c in PLACES]
TO_UP = [(place(y, z, c), place(y, (z + 1) % N_Z, c)) for y, z, c in PLACES]
TO_DOWN = [(place(y, z, c), place(y, (z - 1) % N_Z, c)) for y, z, c in PLACES]
Z_GROUPS = [[place(y, z, c) for z in range(N_Z)] for y in range(2) for c in range(2)]


def over_dp(block, pairs):
    return lax.ppermute(block, "dp", pairs)


def over_section(block, distance):
    n = lax.axis_size("section")
    return lax.ppermute(block, "section", [(i, (i + distance) % n) for i in range(n)])


def ring_sum(own, half, narrow):
    first, second = half(own(4))
    up, down = over_dp(narrow(first), TO_UP), over_dp(narrow(second), TO_DOWN)
    f0, f1 = half(own(3))
    g0, g1 = half(own(5))
    up = jnp.concatenate([f0 + up.astype(F32), f1], axis=0)
    down = jnp.concatenate([g0, g1 + down.astype(F32)], axis=0)
    up, down = over_dp(narrow(up), TO_UP), over_dp(narrow(down), TO_DOWN)
    for k in (2, 1):
        up = over_dp(narrow(own(k) + up.astype(F32)), TO_UP)
        down = over_dp(narrow(own(8 - k) + down.astype(F32)), TO_DOWN)
    return own(0) + up.astype(F32) + down.astype(F32)


def terms_kernel(
    at, x_ref, g_ref, gain_ref, w0_ref, w1_ref,
    keep_d, keep_u, send_d, send_u, low_ref, back_ref, inv_ref, dot_ref, normed,
):
    rows, width = x_ref.shape
    z = at[32]

    def square(i, total):
        part = x_ref[:, pl.ds(pl.multiple_of(i * 512, 512), 512)].astype(F32)
        part = part * part
        return total + (part[:, :128] + part[:, 128:256]) + (part[:, 256:384] + part[:, 384:])

    total = lax.fori_loop(0, width // 512, square, jnp.zeros((rows, 128), F32))
    inv = lax.rsqrt(jnp.sum(total, axis=1, keepdims=True) * (1.0 / width) + eps)
    trans = (((1,), (1,)), ((), ()))

    def lows(k, sums):
        low, back = sums
        spot = lax.rem(z + k, N_Z)
        for c, w_ref in enumerate((w0_ref, w1_ref)):
            for y in range(2):
                off = pl.multiple_of(at[(c * N_Z + k) * 2 + y], BLOCK)
                part = x_ref[:, pl.ds(off, BLOCK)].astype(F32)
                norm = (part * inv * gain_ref[:, pl.ds(off, BLOCK)]).astype(BF16)
                normed[(c * N_Z + k) * 2 + y] = norm
                low += lax.dot_general(norm, w_ref[spot, y, 0], trans, preferred_element_type=F32)
                back += lax.dot_general(
                    g_ref[:, pl.ds(off, BLOCK)], w_ref[spot, y, 1], trans, preferred_element_type=F32
                )
        return low, back

    zero = jnp.zeros((rows, low_ref.shape[1]), F32)
    low, back = lax.fori_loop(0, N_Z, lows, (zero, zero))
    low16, back16 = low.astype(BF16), back.astype(BF16)
    low_ref[...] = low16
    back_ref[...] = back16
    inv_ref[...] = jnp.broadcast_to(inv, inv_ref.shape)
    dots = jnp.sum(back16.astype(F32) * low, axis=1, keepdims=True)
    dot_ref[...] = jnp.broadcast_to(dots, dot_ref.shape)
    low_t, back_t = low16.T, back16.T

    def terms(k, carry):
        for c in range(2):
            for y in range(2):
                spot = (c * N_Z + k) * 2 + y
                off = pl.multiple_of(at[spot], BLOCK)
                down = jnp.dot(back_t, normed[spot], preferred_element_type=F32)
                up = jnp.dot(low_t, g_ref[:, pl.ds(off, BLOCK)], preferred_element_type=F32)
                if c == 0:
                    keep_d[k, y] = down
                    keep_u[k, y] = up
                else:
                    send_d[k, y] = down.astype(BF16)
                    send_u[k, y] = up.astype(BF16)
        return carry

    lax.fori_loop(0, N_Z, terms, 0)


def outputs_kernel(
    at, x_ref, g_ref, gain_ref, w0_ref, w1_ref, low_ref, back_ref, inv_ref, dot_ref, xe_ref, ge_ref,
    fwd, bwd, fwd_e, bwd_e,
):
    rows, width = x_ref.shape
    z = at[32]
    keeps = at[33] == 1
    trans = (((1,), (1,)), ((), ()))
    extra = xe_ref.shape[0]

    def square(i, total):
        part = xe_ref[:, pl.ds(pl.multiple_of(i * 128, 128), 128)].astype(F32)
        return total + part * part

    total = lax.fori_loop(0, width // 128, square, jnp.zeros((extra, 128), F32))
    inv_e = lax.rsqrt(jnp.sum(total, axis=1, keepdims=True) * (1.0 / width) + eps)

    def lows(k, sums):
        low, back = sums
        spot = lax.rem(z + k, N_Z)
        for c, w_ref in enumerate((w0_ref, w1_ref)):
            for y in range(2):
                off = pl.multiple_of(at[(c * N_Z + k) * 2 + y], BLOCK)
                part = xe_ref[:, pl.ds(off, BLOCK)].astype(F32)
                norm = (part * inv_e * gain_ref[:, pl.ds(off, BLOCK)]).astype(BF16)
                low += lax.dot_general(norm, w_ref[spot, y, 0], trans, preferred_element_type=F32)
                back += lax.dot_general(
                    ge_ref[:, pl.ds(off, BLOCK)], w_ref[spot, y, 1], trans, preferred_element_type=F32
                )
        return low, back

    zero = jnp.zeros((extra, low_ref.shape[1]), F32)
    low_e, back_e = lax.fori_loop(0, N_Z, lows, (zero, zero))
    low_e16, back_e16 = low_e.astype(BF16), back_e.astype(BF16)
    dots_e = jnp.sum(back_e16.astype(F32) * low_e, axis=1, keepdims=True)
    low = jnp.concatenate([low_ref[...], low_e16], axis=0)
    back = jnp.concatenate([back_ref[...], back_e16], axis=0)
    inv = inv_ref[:, :1]
    slope = inv * inv * dot_ref[:, :1] * (1.0 / width)
    slope_e = inv_e * inv_e * dots_e * (1.0 / width)

    def outs(k, carry):
        spot = lax.rem(z + k, N_Z)
        for c, w_ref in enumerate((w0_ref, w1_ref)):
            for y in range(2):
                off = pl.multiple_of(at[(c * N_Z + k) * 2 + y], BLOCK)
                here = pl.ds(off, BLOCK)
                scale = gain_ref[:, here]
                lifted = jnp.dot(low, w_ref[spot, y, 1], preferred_element_type=F32)
                pulled = jnp.dot(back, w_ref[spot, y, 0], preferred_element_type=F32) * scale
                part = x_ref[:, here].astype(F32)
                part_e = xe_ref[:, here].astype(F32)
                out = (part + lifted[:rows]).astype(BF16)
                grad = g_ref[:, here].astype(F32) + (pulled[:rows] * inv - part * slope)
                fwd[:, here] = jnp.where(keeps, out, jnp.zeros_like(out))
                grad = grad.astype(BF16)
                bwd[:, here] = jnp.where(keeps, grad, jnp.zeros_like(grad))
                fwd_e[:, here] = (part_e + lifted[rows:]).astype(BF16)
                grad_e = ge_ref[:, here].astype(F32) + (pulled[rows:] * inv_e - part_e * slope_e)
                bwd_e[:, here] = grad_e.astype(BF16)
        return carry

    lax.fori_loop(0, N_Z, outs, 0)


def picks(route, lost, rank, y, z, c, c_rel, slot, count):
    share = count // N_DP
    row = jnp.arange(count)
    k, q = row // 16, row % 16
    y_to = jnp.where(q >= 8, 1 - y, y)
    c_to = c if c_rel == 0 else 1 - c
    to = place(y_to, (z + k) % N_Z, c_to)
    source = route[to] * share + q % share
    used = (rank == lost) & ((q // 4) % 2 == slot)
    return ((source[:, None] == jnp.arange(count)[None, :]) & used[:, None]).astype(BF16)


def body(arriving, returning, gain, section_down_weight, section_up_weight, failed, route):
    section = lax.axis_index("section")
    sections = lax.axis_size("section")
    rank = lax.axis_index("dp")
    y, z, c = rank // 16, (rank // 2) % N_Z, rank % 2
    count, width = arriving.shape[2], arriving.shape[3]
    depth = section_down_weight.shape[1]
    share = count // N_DP

    inbound = over_section(arriving, 1)[0, 0]
    upstream = over_section(returning, -1)[0, 0]

    shard = jnp.concatenate([section_down_weight, section_up_weight], axis=0)
    both = jnp.stack([shard, over_dp(shard, TO_Y)], axis=0)
    mine = lax.all_gather(both, "dp", axis=0, axis_index_groups=Z_GROUPS, tiled=False)
    theirs = over_dp(mine, TO_CORE)

    here_x, here_g = arriving[0, 0], returning[0, 0]
    after, before = (section + 1) % sections, (section - 1) % sections
    moved = []
    for c_rel in range(2):
        px = picks(route[after], failed[after], rank, y, z, c, c_rel, 0, count)
        pg = picks(route[before], failed[before], rank, y, z, c, c_rel, 1, count)
        rows = jnp.dot(px, here_x, preferred_element_type=F32) + jnp.dot(
            pg, here_g, preferred_element_type=F32
        )
        moved.append(rows.astype(BF16).reshape(N_Z, 16, width))
    crossed = over_dp(moved[1], TO_CORE)
    rows = ring_sum(
        lambda k: moved[0][k].astype(F32) + crossed[k].astype(F32),
        lambda v: (v[:8], v[8:]),
        lambda v: v.astype(BF16),
    ).astype(BF16)
    rows = rows[:8] + over_dp(rows[8:], TO_Y)
    extra_x = over_section(rows[:share], 1)
    extra_g = over_section(rows[share : 2 * share], -1)
    pad = ((0, 16 - share), (0, 0))
    extra_x, extra_g = jnp.pad(extra_x, pad), jnp.pad(extra_g, pad)

    offsets = [
        place(y if yr == 0 else 1 - y, (z + k) % N_Z, c if cr == 0 else 1 - c) * BLOCK
        for cr in range(2)
        for k in range(N_Z)
        for yr in range(2)
    ]
    at = jnp.stack(offsets + [z, (rank != failed[section]).astype(jnp.int32)]).astype(jnp.int32)
    smem = pl.BlockSpec(memory_space=pltpu.SMEM)
    vmem = pl.BlockSpec(memory_space=pltpu.VMEM)
    chunk = (N_Z, 2, depth, BLOCK)
    stat = jax.ShapeDtypeStruct((count, 128), F32)
    small = jax.ShapeDtypeStruct((count, depth), BF16)
    keep_d, keep_u, send_d, send_u, low, back, inv, dots = pl.pallas_call(
        terms_kernel,
        out_shape=[
            jax.ShapeDtypeStruct(chunk, F32),
            jax.ShapeDtypeStruct(chunk, F32),
            jax.ShapeDtypeStruct(chunk, BF16),
            jax.ShapeDtypeStruct(chunk, BF16),
            small,
            small,
            stat,
            stat,
        ],
        in_specs=[smem] + [vmem] * 5,
        out_specs=[vmem] * 8,
        scratch_shapes=[pltpu.VMEM((32, count, BLOCK), BF16)],
        compiler_params=pltpu.CompilerParams(vmem_limit_bytes=40 * 2**20),
        cost_estimate=pl.CostEstimate(
            flops=8 * count * width * depth, bytes_accessed=16 * 2**20, transcendentals=0
        ),
        name="terms",
    )(at, inbound, upstream, gain, mine, theirs)

    def reduced(keep, send):
        crossed = over_dp(send, TO_CORE)
        total = ring_sum(
            lambda k: keep[k] + crossed[k].astype(F32),
            lambda v: (v[:1], v[1:]),
            lambda v: v.astype(BF16),
        )
        other = over_dp(total[1].astype(BF16), TO_Y)
        return ((total[0] + other.astype(F32)) * (1.0 / N_DP))[None]

    grad_up = reduced(keep_u, send_u)
    grad_down = reduced(keep_d, send_d)

    wide = jax.ShapeDtypeStruct((count, width), BF16)
    thin = jax.ShapeDtypeStruct((16, width), BF16)
    forward_out, backward_out, rerouted_f, rerouted_b = pl.pallas_call(
        outputs_kernel,
        out_shape=[wide, wide, thin, thin],
        in_specs=[smem] + [vmem] * 11,
        out_specs=[vmem] * 4,
        compiler_params=pltpu.CompilerParams(vmem_limit_bytes=40 * 2**20),
        cost_estimate=pl.CostEstimate(
            flops=5 * count * width * depth, bytes_accessed=14 * 2**20, transcendentals=0
        ),
        name="outputs",
    )(at, inbound, upstream, gain, mine, theirs, low, back, inv, dots, extra_x, extra_g)
    return (
        forward_out[None, None],
        backward_out[None, None],
        rerouted_f[None, :share],
        rerouted_b[None, :share],
        grad_down,
        grad_up,
    )


def solution(mesh):
    return jax.shard_map(
        body,
        mesh=mesh,
        in_specs=(
            P("section", "dp", None, None),
            P("section", "dp", None, None),
            P("section", None),
            P("section", None, "dp"),
            P("section", None, "dp"),
            P(),
            P(),
        ),
        out_specs=(
            P("section", "dp", None, None),
            P("section", "dp", None, None),
            P("section", "dp", None),
            P("section", "dp", None),
            P("section", None, "dp"),
            P("section", None, "dp"),
        ),
        check_vma=False,
    )
```

time: 952 us -> 214 us (0.22)
  waiting for transfers between devices: 888 us -> 104 us
  starting transfers between devices: 4.41 us -> 47.4 us
  Pallas kernels: 0 us -> 17.8 us
  other arithmetic: 20.4 us -> 10.1 us
    psum x2 -> x0, waiting for transfers between devices: 540 us -> none  [from_root(): return lax.psum(block, axis)]
    reduce_scatter x1 -> x0, waiting for transfers between devices: 154 us -> none  [body(): lax.psum_scatter(jnp.concatenate([part_down, part_up], axis=1), 'dp', sca...]
    all_gather x2 -> x1, waiting for transfers between devices: 149 us -> 25.6 us  [body(): lax.all_gather(both, 'dp', axis=0, axis_index_groups=Z_GROUPS, tiled=False)]
    ppermute x2 -> x36, starting transfers between devices: 4.21 us -> 47.3 us  [the longest x32 43.2 us: over_dp(): return lax.ppermute(block, 'dp', pairs)]
    ppermute x2 -> x36, waiting for transfers between devices: 43 us -> 78.1 us  [the longest x32 74.4 us: over_dp(): return lax.ppermute(block, 'dp', pairs)]
    pallas_call x0 -> x2, Pallas kernels: none -> 17.8 us  [the longest x1 9.91 us: body(): pl.pallas_call(outputs_kernel, out_shape=[wide, wide, thin, thin], in_spe...]
  transfers between devices with their start and end apart: 7 -> 37, of which waited for: 6 -> 19; matrix products, arithmetic and copies ran while one was open for 3% -> 6% of each run, Pallas kernels for 0% -> 5%
where the time goes in v1:
time: 214 us
  waiting for transfers between devices  104 us (49%)
  starting transfers between devices  47.4 us (22%)
  Pallas kernels  17.8 us (8%)
  between operations  16.7 us (8%)
  local copies, waits for them, and re-layouts  10.3 us (5%)
  other arithmetic  10.1 us (5%)
  matrix products  7.8 us (4%)
    ppermute x32, waiting for transfers between devices, over_dp(): return lax.ppermute(block, 'dp', pairs)  74.4 us
    ppermute x32, starting transfers between devices, over_dp(): return lax.ppermute(block, 'dp', pairs)  43.2 us
    all_gather x1, waiting for transfers between devices, body(): lax.all_gather(both, 'dp', axis=0, axis_index_groups=Z_GROUPS, tiled=False)  25.6 us
    pallas_call x1, Pallas kernels, body(): pl.pallas_call(outputs_kernel, out_shape=[wide, wide, thin, thin], in_spe...  9.91 us
    pallas_call x1, Pallas kernels, body(): pl.pallas_call(terms_kernel, out_shape=[jax.ShapeDtypeStruct(chunk, F32),...  7.88 us
    gather x4, local copies, waits for them, and re-layouts, picks(): source = route[to] * share + q % share  4.9 us
    dot_general x2, matrix products, body(): jnp.dot(px, here_x, preferred_element_type=F32)  4.83 us
    convert_element_type x4, other arithmetic, body(): v.astype(BF16)  4.4 us
  transfers between devices with their start and end apart: 37, of which 19 were waited for; matrix products, arithmetic and copies ran while one was open for 6% of the time, Pallas kernels for 5%

profile of v1, /device:TPU:6, one launch (start us, length us, event | category | flops | bytes accessed | tf_op | source)
XLA Modules:
  0.0 213.8 jit_solution(16032525544910711999)
XLA Ops:
  13.3 2.5 %fusion.4 = f32[128,8192]{1,0:T(8,128)S(1)} fusion(bf16[1,1,128,8192]{3,2,1,0:T(8,128)(2,1)} %param.7, s32[128]{0:T(128)S(1)} %multiply_add_fusion.1, pred[128]{0:T(512)(128)(4,1)S(1)} %get-tuple-element.58), kind=kOutput, calls=%fused_computation.10 | convolution fusion | flops 268468224 | bytes 6292096 | tf_op jit(solution)/shard_map/dot_general | solution.py:210
  15.8 2.1 %fusion.1 = bf16[128,8192]{1,0:T(8,128)(2,1)} fusion(f32[128,8192]{1,0:T(8,128)S(1)} %fusion.4, bf16[1,1,128,8192]{3,2,1,0:T(8,128)(2,1)S(1)} %copy-done.2, s32[128]{0:T(128)S(1)} %multiply_add_fusion, pred[128]{0:T(512)(128)(4,1)S(1)} %get-tuple-element.57), kind=kOutput, calls=%fused_computation.7 | convolution fusion | flops 270565376 | bytes 8389248 | tf_op jit(solution)/shard_map/dot_general | solution.py:210
  20.5 2.3 %fusion.6 = f32[128,8192]{1,0:T(8,128)S(1)} fusion(bf16[1,1,128,8192]{3,2,1,0:T(8,128)(2,1)} %param.7, s32[128]{0:T(128)S(1)} %multiply_add_fusion.3, pred[128]{0:T(512)(128)(4,1)S(1)} %get-tuple-element.58), kind=kOutput, calls=%fused_computation.12 | convolution fusion | flops 268468224 | bytes 6292096 | tf_op jit(solution)/shard_map/dot_general | solution.py:210
  25.2 2.0 collective-permute-start.5
  27.3 8.1 %collective-permute-done.5 = bf16[8,8192]{1,0:T(8,128)(2,1)S(1)} collective-permute-done((bf16[8,8192]{1,0:T(8,128)(2,1)S(1)}, bf16[8,8192]{1,0:T(8,128)(2,1)S(1)}, u32[]{:S(2)}, u32[]{:S(2)}) %collective-permute-start.5) | collective-permute-done | bytes 131104 | tf_op jit(solution)/shard_map/ppermute | solution.py:29
  35.5 9.3 %collective-permute-done.6 = bf16[16,8192]{1,0:T(8,128)(2,1)S(1)} collective-permute-done((bf16[16,8192]{1,0:T(8,128)(2,1)S(1)}, bf16[16,8192]{1,0:T(8,128)(2,1)S(1)}, u32[]{:S(2)}, u32[]{:S(2)}) %collective-permute-start.6) | collective-permute-done | bytes 262176 | tf_op jit(solution)/shard_map/ppermute | solution.py:29
  46.0 3.2 %collective-permute-start.9 = (bf16[8,8192]{1,0:T(8,128)(2,1)S(1)}, bf16[8,8192]{1,0:T(8,128)(2,1)S(1)}, u32[]{:S(2)}, u32[]{:S(2)}) collective-permute-start(bf16[8,8192]{1,0:T(8,128)(2,1)S(1)} %get-tuple-element.45), channel_id=1, source_target_pairs={{0,14},{1,15},{2,0},{3,1},{4,2},{5,3},{6,4},{7,5},{8,6},{9,7},{10,... | collective-permute-start | bytes 393224 | tf_op jit(solution)/shard_map/ppermute | solution.py:29
  49.2 5.2 %collective-permute-done.7 = bf16[16,8192]{1,0:T(8,128)(2,1)S(1)} collective-permute-done((bf16[16,8192]{1,0:T(8,128)(2,1)S(1)}, bf16[16,8192]{1,0:T(8,128)(2,1)S(1)}, u32[]{:S(2)}, u32[]{:S(2)}) %collective-permute-start.7) | collective-permute-done | bytes 262176 | tf_op jit(solution)/shard_map/ppermute | solution.py:29
  55.8 6.3 %collective-permute-done.10 = bf16[16,8192]{1,0:T(8,128)(2,1)S(1)} collective-permute-done((bf16[16,8192]{1,0:T(8,128)(2,1)S(1)}, bf16[16,8192]{1,0:T(8,128)(2,1)S(1)}, u32[]{:S(2)}, u32[]{:S(2)}) %collective-permute-start.10) | collective-permute-done | bytes 262176 | tf_op jit(solution)/shard_map/ppermute | solution.py:29
  64.8 3.3 %collective-permute-start.2 = (bf16[2,128,256]{2,1,0:T(8,128)(2,1)S(1)}, bf16[2,128,256]{2,1,0:T(8,128)(2,1)S(1)}, u32[]{:S(2)}, u32[]{:S(2)}) collective-permute-start(bf16[2,128,256]{2,1,0:T(8,128)(2,1)S(1)} %constant_dynamic-update-slice_fusion), channel_id=1, source_target_pairs={{0,16},{1,17},{2,18},{3,19},{4,20},{5,21},{6,22},{7,23},{8,24},{9,... | collective-permute-start | bytes 393224 | tf_op jit(solution)/shard_map/ppermute | solution.py:29
  68.1 3.3 %collective-permute-done.2 = bf16[2,128,256]{2,1,0:T(8,128)(2,1)S(1)} collective-permute-done((bf16[2,128,256]{2,1,0:T(8,128)(2,1)S(1)}, bf16[2,128,256]{2,1,0:T(8,128)(2,1)S(1)}, u32[]{:S(2)}, u32[]{:S(2)}) %collective-permute-start.2) | collective-permute-done | bytes 131104 | tf_op jit(solution)/shard_map/ppermute | solution.py:29
  73.9 2.9 %collective-permute-start.12 = (bf16[16,8192]{1,0:T(8,128)(2,1)S(1)}, bf16[16,8192]{1,0:T(8,128)(2,1)S(1)}, u32[]{:S(2)}, u32[]{:S(2)}) collective-permute-start(bf16[16,8192]{1,0:T(8,128)(2,1)S(1)} %fusion.11), channel_id=1, source_target_pairs={{0,14},{1,15},{2,0},{3,1},{4,2},{5,3},{6,4},{7,5},{8,6},{9,7},{10,... | collective-permute-start | bytes 786440 | tf_op jit(solution)/shard_map/ppermute | solution.py:29
  76.8 3.0 %collective-permute-done.8 = bf16[16,8192]{1,0:T(8,128)(2,1)S(1)} collective-permute-done((bf16[16,8192]{1,0:T(8,128)(2,1)S(1)}, bf16[16,8192]{1,0:T(8,128)(2,1)S(1)}, u32[]{:S(2)}, u32[]{:S(2)}) %collective-permute-start.8) | collective-permute-done | bytes 262176 | tf_op jit(solution)/shard_map/ppermute | solution.py:29
  81.9 3.3 %collective-permute-start.13 = (bf16[8,8192]{1,0:T(8,128)(2,1)S(1)}, bf16[8,8192]{1,0:T(8,128)(2,1)S(1)}, u32[]{:S(2)}, u32[]{:S(2)}) collective-permute-start(bf16[8,8192]{1,0:T(8,128)(2,1)S(1)} %slice.393), channel_id=1, source_target_pairs={{0,16},{1,17},{2,18},{3,19},{4,20},{5,21},{6,22},{7,23},{8,24},{9,... | collective-permute-start | bytes 393224 | tf_op jit(solution)/shard_map/ppermute | solution.py:29
  87.2 25.6 %all-gather.3.cloned.1.call-done = bf16[16,2,128,256]{3,2,1,0:T(8,128)(2,1)} async-done(((bf16[2,2,128,256]{3,2,1,0:T(8,128)(2,1)}), bf16[16,2,128,256]{3,2,1,0:T(8,128)(2,1)}) %all-gather.3.cloned.1.call-update) | async-done | bytes 2097168 | tf_op jit(solution)/shard_map/all_gather | solution.py:201
  112.8 19.5 %collective-permute-done.13 = bf16[8,8192]{1,0:T(8,128)(2,1)S(1)} collective-permute-done((bf16[8,8192]{1,0:T(8,128)(2,1)S(1)}, bf16[8,8192]{1,0:T(8,128)(2,1)S(1)}, u32[]{:S(2)}, u32[]{:S(2)}) %collective-permute-start.13) | collective-permute-done | bytes 131104 | tf_op jit(solution)/shard_map/ppermute | solution.py:29
  132.4 2.0 collective-permute-start.15
  136.7 2.2 %collective-permute-done.15 = bf16[4,8192]{1,0:T(4,128)(2,1)S(1)} collective-permute-done((bf16[4,8192]{1,0:T(4,128)(2,1)S(1)}, bf16[4,8192]{1,0:T(4,128)(2,1)S(1)}, u32[]{:S(2)}, u32[]{:S(2)}) %collective-permute-start.15) | collective-permute-done | bytes 65568 | tf_op jit(solution)/shard_map/ppermute | solution.py:34
  140.6 7.9 %terms.1 = (f32[8,2,128,256]{3,2,1,0:T(8,128)S(1)}, f32[8,2,128,256]{3,2,1,0:T(8,128)S(1)}, bf16[8,2,128,256]{3,2,1,0:T(8,128)(2,1)S(1)}, bf16[8,2,128,256]{3,2,...) custom-call(s32[34]{0:T(128)S(1)} %stack.152.at, ...), custom_call_target="tpu_custom_call" | custom-call | flops 1073741824 | bytes 16777216 | tf_op jit(solution)/shard_map/terms/pallas_call | solution.py:238
  149.1 9.9 %outputs.1 = (bf16[128,8192]{1,0:T(8,128)(2,1)}, bf16[128,8192]{1,0:T(8,128)(2,1)}, bf16[16,8192]{1,0:T(8,128)(2,1)S(1)}, bf16[16,8192]{1,0:T(8,128)(2,1)S(1)}) custom-call(s32[34]{0:T(128)S(1)} %stack.152.at, bf16[128,8192]{1,0:T(8,128)(2,1)S(1)} %bitcast.215, bf16[128,8192]{1,0:T(8,128)(2,1)} %bitcast.36.g_ref, f32[1,8192]{1,0:T(1,128)S(1)} %copy-done.1, ...), custom_call_target="tpu_custom_call" | custom-call | flops 671088640 | bytes 14680064 | tf_op jit(solution)/shard_map/outputs/pallas_call | solution.py:275
  160.4 3.5 %collective-permute-start.31 = (bf16[1,128,256]{2,1,0:T(8,128)(2,1)S(1)}, bf16[1,128,256]{2,1,0:T(8,128)(2,1)S(1)}, u32[]{:S(2)}, u32[]{:S(2)}) collective-permute-start(bf16[1,128,256]{2,1,0:T(8,128)(2,1)S(1)} %get-tuple-element.47), channel_id=1, source_target_pairs={{0,14},{1,15},{2,0},{3,1},{4,2},{5,3},{6,4},{7,5},{8,6},{9,7},{10,... | collective-permute-start | bytes 196616 | tf_op jit(solution)/shard_map/ppermute | solution.py:29
  164.0 3.3 %collective-permute-start.21 = (bf16[1,128,256]{2,1,0:T(8,128)(2,1)S(1)}, bf16[1,128,256]{2,1,0:T(8,128)(2,1)S(1)}, u32[]{:S(2)}, u32[]{:S(2)}) collective-permute-start(bf16[1,128,256]{2,1,0:T(8,128)(2,1)S(1)} %get-tuple-element.49), channel_id=1, source_target_pairs={{0,14},{1,15},{2,0},{3,1},{4,2},{5,3},{6,4},{7,5},{8,6},{9,7},{10,... | collective-permute-start | bytes 196616 | tf_op jit(solution)/shard_map/ppermute | solution.py:29
  167.5 3.3 %collective-permute-start.32 = (bf16[2,128,256]{2,1,0:T(8,128)(2,1)S(1)}, bf16[2,128,256]{2,1,0:T(8,128)(2,1)S(1)}, u32[]{:S(2)}, u32[]{:S(2)}) collective-permute-start(bf16[2,128,256]{2,1,0:T(8,128)(2,1)S(1)} %pad_maximum_fusion.6), channel_id=1, source_target_pairs={{0,14},{1,15},{2,0},{3,1},{4,2},{5,3},{6,4},{7,5},{8,6},{9,7},{10,... | collective-permute-start | bytes 393224 | tf_op jit(solution)/shard_map/ppermute | solution.py:29
  171.0 3.5 %collective-permute-start.22 = (bf16[2,128,256]{2,1,0:T(8,128)(2,1)S(1)}, bf16[2,128,256]{2,1,0:T(8,128)(2,1)S(1)}, u32[]{:S(2)}, u32[]{:S(2)}) collective-permute-start(bf16[2,128,256]{2,1,0:T(8,128)(2,1)S(1)} %pad_maximum_fusion.4), channel_id=1, source_target_pairs={{0,14},{1,15},{2,0},{3,1},{4,2},{5,3},{6,4},{7,5},{8,6},{9,7},{10,... | collective-permute-start | bytes 393224 | tf_op jit(solution)/shard_map/ppermute | solution.py:29
  174.6 3.0 %collective-permute-done.28 = bf16[2,128,256]{2,1,0:T(8,128)(2,1)S(1)} collective-permute-done((bf16[2,128,256]{2,1,0:T(8,128)(2,1)S(1)}, bf16[2,128,256]{2,1,0:T(8,128)(2,1)S(1)}, u32[]{:S(2)}, u32[]{:S(2)}) %collective-permute-start.28) | collective-permute-done | bytes 131104 | tf_op jit(solution)/shard_map/ppermute | solution.py:29
  177.8 3.6 %collective-permute-done.18 = bf16[2,128,256]{2,1,0:T(8,128)(2,1)S(1)} collective-permute-done((bf16[2,128,256]{2,1,0:T(8,128)(2,1)S(1)}, bf16[2,128,256]{2,1,0:T(8,128)(2,1)S(1)}, u32[]{:S(2)}, u32[]{:S(2)}) %collective-permute-start.18) | collective-permute-done | bytes 131104 | tf_op jit(solution)/shard_map/ppermute | solution.py:29
  181.5 3.5 %collective-permute-done.29 = bf16[2,128,256]{2,1,0:T(8,128)(2,1)S(1)} collective-permute-done((bf16[2,128,256]{2,1,0:T(8,128)(2,1)S(1)}, bf16[2,128,256]{2,1,0:T(8,128)(2,1)S(1)}, u32[]{:S(2)}, u32[]{:S(2)}) %collective-permute-start.29) | collective-permute-done | bytes 131104 | tf_op jit(solution)/shard_map/ppermute | solution.py:29
  185.2 2.0 collective-permute-start.30
  192.1 2.3 %collective-permute-done.23 = bf16[2,128,256]{2,1,0:T(8,128)(2,1)S(1)} collective-permute-done((bf16[2,128,256]{2,1,0:T(8,128)(2,1)S(1)}, bf16[2,128,256]{2,1,0:T(8,128)(2,1)S(1)}, u32[]{:S(2)}, u32[]{:S(2)}) %collective-permute-start.23) | collective-permute-done | bytes 131104 | tf_op jit(solution)/shard_map/ppermute | solution.py:29
  196.8 3.5 %collective-permute-start.35 = (bf16[128,256]{1,0:T(8,128)(2,1)S(1)}, bf16[128,256]{1,0:T(8,128)(2,1)S(1)}, u32[]{:S(2)}, u32[]{:S(2)}) collective-permute-start(bf16[128,256]{1,0:T(8,128)(2,1)S(1)} %fusion.51), channel_id=1, source_target_pairs={{0,16},{1,17},{2,18},{3,19},{4,20},{5,21},{6,22},{7,23},{8,24},{9,... | collective-permute-start | bytes 196616 | tf_op jit(solution)/shard_map/ppermute | solution.py:29
  200.4 2.7 %collective-permute-start.25 = (bf16[128,256]{1,0:T(8,128)(2,1)S(1)}, bf16[128,256]{1,0:T(8,128)(2,1)S(1)}, u32[]{:S(2)}, u32[]{:S(2)}) collective-permute-start(bf16[128,256]{1,0:T(8,128)(2,1)S(1)} %fusion.48), channel_id=1, source_target_pairs={{0,16},{1,17},{2,18},{3,19},{4,20},{5,21},{6,22},{7,23},{8,24},{9,... | collective-permute-start | bytes 196616 | tf_op jit(solution)/shard_map/ppermute | solution.py:29
  203.8 2.5 %collective-permute-done.25 = bf16[128,256]{1,0:T(8,128)(2,1)S(1)} collective-permute-done((bf16[128,256]{1,0:T(8,128)(2,1)S(1)}, bf16[128,256]{1,0:T(8,128)(2,1)S(1)}, u32[]{:S(2)}, u32[]{:S(2)}) %collective-permute-start.25) | collective-permute-done | bytes 65568 | tf_op jit(solution)/shard_map/ppermute | solution.py:29
  (127 shorter events, 36.3 us)
Async XLA Ops:
  7.2 105.6 %all-gather.3.cloned.1.call-start = ((), (), s32[]{:S(2)}) async-start(), calls=%async_computation | async-start | bytes 2359296 | tf_op jit(solution)/shard_map/all_gather | solution.py:201
  25.2 10.1 %collective-permute-start.5 = (bf16[8,8192]{1,0:T(8,128)(2,1)S(1)}, bf16[8,8192]{1,0:T(8,128)(2,1)S(1)}, u32[]{:S(2)}, u32[]{:S(2)}) collective-permute-start(bf16[8,8192]{1,0:T(8,128)(2,1)S(1)} %get-tuple-element.44), channel_id=1, source_target_pairs={{0,2},{1,3},{2,4},{3,5},{4,6},{5,7},{6,8},{7,9},{8,10},{9,11},{10,... | collective-permute-start | bytes 393224 | tf_op jit(solution)/shard_map/ppermute | solution.py:29
  35.4 9.4 %collective-permute-start.6 = (bf16[16,8192]{1,0:T(8,128)(2,1)S(1)}, bf16[16,8192]{1,0:T(8,128)(2,1)S(1)}, u32[]{:S(2)}, u32[]{:S(2)}) collective-permute-start(bf16[16,8192]{1,0:T(8,128)(2,1)S(1)} %pad_maximum_fusion.1), channel_id=1, source_target_pairs={{0,2},{1,3},{2,4},{3,5},{4,6},{5,7},{6,8},{7,9},{8,10},{9,11},{10,... | collective-permute-start | bytes 786440 | tf_op jit(solution)/shard_map/ppermute | solution.py:29
  45.9 8.6 %collective-permute-start.7 = (bf16[16,8192]{1,0:T(8,128)(2,1)S(1)}, bf16[16,8192]{1,0:T(8,128)(2,1)S(1)}, u32[]{:S(2)}, u32[]{:S(2)}) collective-permute-start(bf16[16,8192]{1,0:T(8,128)(2,1)S(1)} %fusion.14), channel_id=1, source_target_pairs={{0,2},{1,3},{2,4},{3,5},{4,6},{5,7},{6,8},{7,9},{8,10},{9,11},{10,... | collective-permute-start | bytes 786440 | tf_op jit(solution)/shard_map/ppermute | solution.py:29
  46.0 9.7 %collective-permute-start.9 = (bf16[8,8192]{1,0:T(8,128)(2,1)S(1)}, bf16[8,8192]{1,0:T(8,128)(2,1)S(1)}, u32[]{:S(2)}, u32[]{:S(2)}) collective-permute-start(bf16[8,8192]{1,0:T(8,128)(2,1)S(1)} %get-tuple-element.45), channel_id=1, source_target_pairs={{0,14},{1,15},{2,0},{3,1},{4,2},{5,3},{6,4},{7,5},{8,6},{9,7},{10,... | collective-permute-start | bytes 393224 | tf_op jit(solution)/shard_map/ppermute | solution.py:29
  55.7 6.5 %collective-permute-start.10 = (bf16[16,8192]{1,0:T(8,128)(2,1)S(1)}, bf16[16,8192]{1,0:T(8,128)(2,1)S(1)}, u32[]{:S(2)}, u32[]{:S(2)}) collective-permute-start(bf16[16,8192]{1,0:T(8,128)(2,1)S(1)} %pad_maximum_fusion.2), channel_id=1, source_target_pairs={{0,14},{1,15},{2,0},{3,1},{4,2},{5,3},{6,4},{7,5},{8,6},{9,7},{10,... | collective-permute-start | bytes 786440 | tf_op jit(solution)/shard_map/ppermute | solution.py:29
  63.2 9.5 %collective-permute-start.11 = (bf16[16,8192]{1,0:T(8,128)(2,1)S(1)}, bf16[16,8192]{1,0:T(8,128)(2,1)S(1)}, u32[]{:S(2)}, u32[]{:S(2)}) collective-permute-start(bf16[16,8192]{1,0:T(8,128)(2,1)S(1)} %fusion.9), channel_id=1, source_target_pairs={{0,14},{1,15},{2,0},{3,1},{4,2},{5,3},{6,4},{7,5},{8,6},{9,7},{10,... | collective-permute-start | bytes 786440 | tf_op jit(solution)/shard_map/ppermute | solution.py:29
  64.8 6.6 %collective-permute-start.2 = (bf16[2,128,256]{2,1,0:T(8,128)(2,1)S(1)}, bf16[2,128,256]{2,1,0:T(8,128)(2,1)S(1)}, u32[]{:S(2)}, u32[]{:S(2)}) collective-permute-start(bf16[2,128,256]{2,1,0:T(8,128)(2,1)S(1)} %constant_dynamic-update-slice_fusion), channel_id=1, source_target_pairs={{0,16},{1,17},{2,18},{3,19},{4,20},{5,21},{6,22},{7,23},{8,24},{9,... | collective-permute-start | bytes 393224 | tf_op jit(solution)/shard_map/ppermute | solution.py:29
  72.1 7.7 %collective-permute-start.8 = (bf16[16,8192]{1,0:T(8,128)(2,1)S(1)}, bf16[16,8192]{1,0:T(8,128)(2,1)S(1)}, u32[]{:S(2)}, u32[]{:S(2)}) collective-permute-start(bf16[16,8192]{1,0:T(8,128)(2,1)S(1)} %get-tuple-element.30), channel_id=1, source_target_pairs={{0,2},{1,3},{2,4},{3,5},{4,6},{5,7},{6,8},{7,9},{8,10},{9,11},{10,... | collective-permute-start | bytes 786440 | tf_op jit(solution)/shard_map/ppermute | solution.py:29
  73.9 6.8 %collective-permute-start.12 = (bf16[16,8192]{1,0:T(8,128)(2,1)S(1)}, bf16[16,8192]{1,0:T(8,128)(2,1)S(1)}, u32[]{:S(2)}, u32[]{:S(2)}) collective-permute-start(bf16[16,8192]{1,0:T(8,128)(2,1)S(1)} %fusion.11), channel_id=1, source_target_pairs={{0,14},{1,15},{2,0},{3,1},{4,2},{5,3},{6,4},{7,5},{8,6},{9,7},{10,... | collective-permute-start | bytes 786440 | tf_op jit(solution)/shard_map/ppermute | solution.py:29
  81.9 50.4 %collective-permute-start.13 = (bf16[8,8192]{1,0:T(8,128)(2,1)S(1)}, bf16[8,8192]{1,0:T(8,128)(2,1)S(1)}, u32[]{:S(2)}, u32[]{:S(2)}) collective-permute-start(bf16[8,8192]{1,0:T(8,128)(2,1)S(1)} %slice.393), channel_id=1, source_target_pairs={{0,16},{1,17},{2,18},{3,19},{4,20},{5,21},{6,22},{7,23},{8,24},{9,... | collective-permute-start | bytes 393224 | tf_op jit(solution)/shard_map/ppermute | solution.py:29
  85.2 53.8 %collective-permute-start = (bf16[1,1,128,8192]{3,2,1,0:T(8,128)(2,1)}, bf16[1,1,128,8192]{3,2,1,0:T(8,128)(2,1)S(1)}, u32[]{:S(2)}, u32[]{:S(2)}) collective-permute-start(bf16[1,1,128,8192]{3,2,1,0:T(8,128)(2,1)} %param.7), channel_id=1, source_target_pairs={{0,32},{32,64},{64,96},{96,128},{128,160},{160,192},{192,224},{224... | collective-permute-start | bytes 6291464 | tf_op jit(solution)/shard_map/ppermute | solution.py:34
  85.8 53.2 %collective-permute-start.1 = (bf16[1,1,128,8192]{3,2,1,0:T(8,128)(2,1)}, bf16[1,1,128,8192]{3,2,1,0:T(8,128)(2,1)}, u32[]{:S(2)}, u32[]{:S(2)}) collective-permute-start(bf16[1,1,128,8192]{3,2,1,0:T(8,128)(2,1)} %param.8), channel_id=1, source_target_pairs={{0,224},{32,0},{64,32},{96,64},{128,96},{160,128},{192,160},{224,1... | collective-permute-start | bytes 6291464 | tf_op jit(solution)/shard_map/ppermute | solution.py:34
  112.8 26.1 %collective-permute-start.3 = (bf16[8,2,2,128,256]{4,3,2,1,0:T(8,128)(2,1)}, bf16[8,2,2,128,256]{4,3,2,1,0:T(8,128)(2,1)}, u32[]{:S(2)}, u32[]{:S(2)}) collective-permute-start(bf16[8,2,2,128,256]{4,3,2,1,0:T(8,128)(2,1)} %bitcast.211), channel_id=1, source_target_pairs={{0,1},{1,0},{2,3},{3,2},{4,5},{5,4},{6,7},{7,6},{8,9},{9,8},{10,11... | collective-permute-start | bytes 6291464 | tf_op jit(solution)/shard_map/ppermute | solution.py:29
  132.4 6.5 %collective-permute-start.15 = (bf16[4,8192]{1,0:T(4,128)(2,1)S(1)}, bf16[4,8192]{1,0:T(4,128)(2,1)S(1)}, u32[]{:S(2)}, u32[]{:S(2)}) collective-permute-start(bf16[4,8192]{1,0:T(4,128)(2,1)S(1)} %get-tuple-element.50), channel_id=1, source_target_pairs={{0,224},{32,0},{64,32},{96,64},{128,96},{160,128},{192,160},{224,1... | collective-permute-start | bytes 196616 | tf_op jit(solution)/shard_map/ppermute | solution.py:34
  148.5 11.8 %collective-permute-start.26 = (bf16[8,2,128,256]{3,2,1,0:T(8,128)(2,1)S(1)}, bf16[8,2,128,256]{3,2,1,0:T(8,128)(2,1)S(1)}, u32[]{:S(2)}, u32[]{:S(2)}) collective-permute-start(bf16[8,2,128,256]{3,2,1,0:T(8,128)(2,1)S(1)} %get-tuple-element.29), channel_id=1, source_target_pairs={{0,1},{1,0},{2,3},{3,2},{4,5},{5,4},{6,7},{7,6},{8,9},{9,8},{10,11... | collective-permute-start | bytes 3145736 | tf_op jit(solution)/shard_map/ppermute | solution.py:29
  148.6 15.3 %collective-permute-start.16 = (bf16[8,2,128,256]{3,2,1,0:T(8,128)(2,1)S(1)}, bf16[8,2,128,256]{3,2,1,0:T(8,128)(2,1)S(1)}, u32[]{:S(2)}, u32[]{:S(2)}) collective-permute-start(bf16[8,2,128,256]{3,2,1,0:T(8,128)(2,1)S(1)} %get-tuple-element.27), channel_id=1, source_target_pairs={{0,1},{1,0},{2,3},{3,2},{4,5},{5,4},{6,7},{7,6},{8,9},{9,8},{10,11... | collective-permute-start | bytes 3145736 | tf_op jit(solution)/shard_map/ppermute | solution.py:29
  160.4 7.1 %collective-permute-start.31 = (bf16[1,128,256]{2,1,0:T(8,128)(2,1)S(1)}, bf16[1,128,256]{2,1,0:T(8,128)(2,1)S(1)}, u32[]{:S(2)}, u32[]{:S(2)}) collective-permute-start(bf16[1,128,256]{2,1,0:T(8,128)(2,1)S(1)} %get-tuple-element.47), channel_id=1, source_target_pairs={{0,14},{1,15},{2,0},{3,1},{4,2},{5,3},{6,4},{7,5},{8,6},{9,7},{10,... | collective-permute-start | bytes 196616 | tf_op jit(solution)/shard_map/ppermute | solution.py:29
  163.9 6.9 %collective-permute-start.27 = (bf16[1,128,256]{2,1,0:T(8,128)(2,1)S(1)}, bf16[1,128,256]{2,1,0:T(8,128)(2,1)S(1)}, u32[]{:S(2)}, u32[]{:S(2)}) collective-permute-start(bf16[1,128,256]{2,1,0:T(8,128)(2,1)S(1)} %get-tuple-element.46), channel_id=1, source_target_pairs={{0,2},{1,3},{2,4},{3,5},{4,6},{5,7},{6,8},{7,9},{8,10},{9,11},{10,... | collective-permute-start | bytes 196616 | tf_op jit(solution)/shard_map/ppermute | solution.py:29
  164.0 6.9 %collective-permute-start.21 = (bf16[1,128,256]{2,1,0:T(8,128)(2,1)S(1)}, bf16[1,128,256]{2,1,0:T(8,128)(2,1)S(1)}, u32[]{:S(2)}, u32[]{:S(2)}) collective-permute-start(bf16[1,128,256]{2,1,0:T(8,128)(2,1)S(1)} %get-tuple-element.49), channel_id=1, source_target_pairs={{0,14},{1,15},{2,0},{3,1},{4,2},{5,3},{6,4},{7,5},{8,6},{9,7},{10,... | collective-permute-start | bytes 196616 | tf_op jit(solution)/shard_map/ppermute | solution.py:29
  167.3 7.2 %collective-permute-start.17 = (bf16[1,128,256]{2,1,0:T(8,128)(2,1)S(1)}, bf16[1,128,256]{2,1,0:T(8,128)(2,1)S(1)}, u32[]{:S(2)}, u32[]{:S(2)}) collective-permute-start(bf16[1,128,256]{2,1,0:T(8,128)(2,1)S(1)} %get-tuple-element.48), channel_id=1, source_target_pairs={{0,2},{1,3},{2,4},{3,5},{4,6},{5,7},{6,8},{7,9},{8,10},{9,11},{10,... | collective-permute-start | bytes 196616 | tf_op jit(solution)/shard_map/ppermute | solution.py:29
  167.5 14.0 %collective-permute-start.32 = (bf16[2,128,256]{2,1,0:T(8,128)(2,1)S(1)}, bf16[2,128,256]{2,1,0:T(8,128)(2,1)S(1)}, u32[]{:S(2)}, u32[]{:S(2)}) collective-permute-start(bf16[2,128,256]{2,1,0:T(8,128)(2,1)S(1)} %pad_maximum_fusion.6), channel_id=1, source_target_pairs={{0,14},{1,15},{2,0},{3,1},{4,2},{5,3},{6,4},{7,5},{8,6},{9,7},{10,... | collective-permute-start | bytes 393224 | tf_op jit(solution)/shard_map/ppermute | solution.py:29
  170.8 6.8 %collective-permute-start.28 = (bf16[2,128,256]{2,1,0:T(8,128)(2,1)S(1)}, bf16[2,128,256]{2,1,0:T(8,128)(2,1)S(1)}, u32[]{:S(2)}, u32[]{:S(2)}) collective-permute-start(bf16[2,128,256]{2,1,0:T(8,128)(2,1)S(1)} %pad_maximum_fusion.5), channel_id=1, source_target_pairs={{0,2},{1,3},{2,4},{3,5},{4,6},{5,7},{6,8},{7,9},{8,10},{9,11},{10,... | collective-permute-start | bytes 393224 | tf_op jit(solution)/shard_map/ppermute | solution.py:29
  171.0 16.3 %collective-permute-start.22 = (bf16[2,128,256]{2,1,0:T(8,128)(2,1)S(1)}, bf16[2,128,256]{2,1,0:T(8,128)(2,1)S(1)}, u32[]{:S(2)}, u32[]{:S(2)}) collective-permute-start(bf16[2,128,256]{2,1,0:T(8,128)(2,1)S(1)} %pad_maximum_fusion.4), channel_id=1, source_target_pairs={{0,14},{1,15},{2,0},{3,1},{4,2},{5,3},{6,4},{7,5},{8,6},{9,7},{10,... | collective-permute-start | bytes 393224 | tf_op jit(solution)/shard_map/ppermute | solution.py:29
  174.5 6.8 %collective-permute-start.18 = (bf16[2,128,256]{2,1,0:T(8,128)(2,1)S(1)}, bf16[2,128,256]{2,1,0:T(8,128)(2,1)S(1)}, u32[]{:S(2)}, u32[]{:S(2)}) collective-permute-start(bf16[2,128,256]{2,1,0:T(8,128)(2,1)S(1)} %pad_maximum_fusion.3), channel_id=1, source_target_pairs={{0,2},{1,3},{2,4},{3,5},{4,6},{5,7},{6,8},{7,9},{8,10},{9,11},{10,... | collective-permute-start | bytes 393224 | tf_op jit(solution)/shard_map/ppermute | solution.py:29
  177.7 7.4 %collective-permute-start.29 = (bf16[2,128,256]{2,1,0:T(8,128)(2,1)S(1)}, bf16[2,128,256]{2,1,0:T(8,128)(2,1)S(1)}, u32[]{:S(2)}, u32[]{:S(2)}) collective-permute-start(bf16[2,128,256]{2,1,0:T(8,128)(2,1)S(1)} %fusion.24), channel_id=1, source_target_pairs={{0,2},{1,3},{2,4},{3,5},{4,6},{5,7},{6,8},{7,9},{8,10},{9,11},{10,... | collective-permute-start | bytes 393224 | tf_op jit(solution)/shard_map/ppermute | solution.py:29
  181.4 6.5 %collective-permute-start.19 = (bf16[2,128,256]{2,1,0:T(8,128)(2,1)S(1)}, bf16[2,128,256]{2,1,0:T(8,128)(2,1)S(1)}, u32[]{:S(2)}, u32[]{:S(2)}) collective-permute-start(bf16[2,128,256]{2,1,0:T(8,128)(2,1)S(1)} %fusion.29), channel_id=1, source_target_pairs={{0,2},{1,3},{2,4},{3,5},{4,6},{5,7},{6,8},{7,9},{8,10},{9,11},{10,... | collective-permute-start | bytes 393224 | tf_op jit(solution)/shard_map/ppermute | solution.py:29
  185.1 6.5 %collective-permute-start.33 = (bf16[2,128,256]{2,1,0:T(8,128)(2,1)S(1)}, bf16[2,128,256]{2,1,0:T(8,128)(2,1)S(1)}, u32[]{:S(2)}, u32[]{:S(2)}) collective-permute-start(bf16[2,128,256]{2,1,0:T(8,128)(2,1)S(1)} %get-tuple-element.35), channel_id=1, source_target_pairs={{0,14},{1,15},{2,0},{3,1},{4,2},{5,3},{6,4},{7,5},{8,6},{9,7},{10,... | collective-permute-start | bytes 393224 | tf_op jit(solution)/shard_map/ppermute | solution.py:29
  185.2 9.8 %collective-permute-start.30 = (bf16[2,128,256]{2,1,0:T(8,128)(2,1)S(1)}, bf16[2,128,256]{2,1,0:T(8,128)(2,1)S(1)}, u32[]{:S(2)}, u32[]{:S(2)}) collective-permute-start(bf16[2,128,256]{2,1,0:T(8,128)(2,1)S(1)} %get-tuple-element.34), channel_id=1, source_target_pairs={{0,2},{1,3},{2,4},{3,5},{4,6},{5,7},{6,8},{7,9},{8,10},{9,11},{10,... | collective-permute-start | bytes 393224 | tf_op jit(solution)/shard_map/ppermute | solution.py:29
  188.0 6.4 %collective-permute-start.23 = (bf16[2,128,256]{2,1,0:T(8,128)(2,1)S(1)}, bf16[2,128,256]{2,1,0:T(8,128)(2,1)S(1)}, u32[]{:S(2)}, u32[]{:S(2)}) collective-permute-start(bf16[2,128,256]{2,1,0:T(8,128)(2,1)S(1)} %get-tuple-element.40), channel_id=1, source_target_pairs={{0,14},{1,15},{2,0},{3,1},{4,2},{5,3},{6,4},{7,5},{8,6},{9,7},{10,... | collective-permute-start | bytes 393224 | tf_op jit(solution)/shard_map/ppermute | solution.py:29
  188.7 11.6 %collective-permute-start.20 = (bf16[2,128,256]{2,1,0:T(8,128)(2,1)S(1)}, bf16[2,128,256]{2,1,0:T(8,128)(2,1)S(1)}, u32[]{:S(2)}, u32[]{:S(2)}) collective-permute-start(bf16[2,128,256]{2,1,0:T(8,128)(2,1)S(1)} %get-tuple-element.39), channel_id=1, source_target_pairs={{0,2},{1,3},{2,4},{3,5},{4,6},{5,7},{6,8},{7,9},{8,10},{9,11},{10,... | collective-permute-start | bytes 393224 | tf_op jit(solution)/shard_map/ppermute | solution.py:29
  196.8 6.3 %collective-permute-start.35 = (bf16[128,256]{1,0:T(8,128)(2,1)S(1)}, bf16[128,256]{1,0:T(8,128)(2,1)S(1)}, u32[]{:S(2)}, u32[]{:S(2)}) collective-permute-start(bf16[128,256]{1,0:T(8,128)(2,1)S(1)} %fusion.51), channel_id=1, source_target_pairs={{0,16},{1,17},{2,18},{3,19},{4,20},{5,21},{6,22},{7,23},{8,24},{9,... | collective-permute-start | bytes 196616 | tf_op jit(solution)/shard_map/ppermute | solution.py:29
  (11 other events, 175.5 us)
Sparse Core Ops, SparseCore 0:
  72.2 40.5 all-gather.2

commit v2 on v0

v2 whole, which is shorter than its diff:
```python
import jax
import jax.numpy as jnp
from jax import lax
from jax.experimental import pallas as pl
from jax.experimental.pallas import tpu as pltpu
from jax.sharding import PartitionSpec as P

eps = 1e-05
N_Z = 8
N_DP = 32
BLOCK = 256
F32 = jnp.float32
BF16 = jnp.bfloat16


def place(y, z, c):
    return (y * N_Z + z) * 2 + c


PLACES = [(y, z, c) for y in range(2) for z in range(N_Z) for c in range(2)]
TO_CORE = [(place(y, z, c), place(y, z, 1 - c)) for y, z, c in PLACES]
TO_Y = [(place(y, z, c), place(1 - y, z, c)) for y, z, c in PLACES]
TO_UP = [(place(y, z, c), place(y, (z + 1) % N_Z, c)) for y, z, c in PLACES]
TO_DOWN = [(place(y, z, c), place(y, (z - 1) % N_Z, c)) for y, z, c in PLACES]
Z_GROUPS = [[place(y, z, c) for z in range(N_Z)] for y in range(2) for c in range(2)]


def over_dp(block, pairs):
    return lax.ppermute(block, "dp", pairs)


def over_section(block, distance):
    n = lax.axis_size("section")
    return lax.ppermute(block, "section", [(i, (i + distance) % n) for i in range(n)])


def over_both(block, distance, across):
    n = lax.axis_size("section")
    pairs = [
        (i * N_DP + place(y, z, c), (i + distance) % n * N_DP + place(y ^ across, z, c))
        for i in range(n)
        for y, z, c in PLACES
    ]
    return lax.ppermute(block, ("section", "dp"), pairs)


SLOTS = (4, 3, 5, 2, 6, 1, 7, 0)
N_FIRST = 3


def columns_of(refs, at, c, k, y):
    return refs[c].at[lax.rem(at[32] + k, N_Z), y]


def spot_of(c, k, y):
    return (c * N_Z + k) * 2 + y


def wide(ref):
    return ref[...].astype(F32)


def open_kernel(keep, crossed, up, down):
    total = keep[0] + wide(crossed)[0]
    up[...] = total[:1].astype(BF16)
    down[...] = total[1:].astype(BF16)


def fold_kernel(token, keep_up, keep_down, cross_up, cross_down, got_up, got_down, up, down):
    top = keep_up[0] + wide(cross_up)[0]
    low = keep_down[0] + wide(cross_down)[0]
    if got_up.shape[0] == 1:
        up[0] = (top[0] + wide(got_up)[0]).astype(BF16)
        up[1] = top[1].astype(BF16)
        down[0] = low[0].astype(BF16)
        down[1] = (low[1] + wide(got_down)[0]).astype(BF16)
    else:
        up[...] = (top + wide(got_up)).astype(BF16)
        down[...] = (low + wide(got_down)).astype(BF16)


def close_kernel(keep, crossed, got_up, got_down, own, other):
    total = (keep[0] + wide(crossed)[0]) + (wide(got_up) + wide(got_down))
    own[...] = total[0]
    other[...] = total[1].astype(BF16)


def finish_kernel(own, got, grad_down, grad_up):
    total = (own[...] + wide(got)) * (1.0 / N_DP)
    grad_down[0] = total[0]
    grad_up[0] = total[1]


def square_sums(x_ref):
    rows, width = x_ref.shape

    def square(i, total):
        part = x_ref[:, pl.ds(pl.multiple_of(i * 512, 512), 512)].astype(F32)
        part = part * part
        return total + ((part[:, :128] + part[:, 128:256]) + (part[:, 256:384] + part[:, 384:]))

    total = lax.fori_loop(0, width // 512, square, jnp.zeros((rows, 128), F32))
    return lax.rsqrt(jnp.sum(total, axis=1, keepdims=True) * (1.0 / width) + eps)


def scale_kernel(x_ref, g_ref, inv_ref):
    inv_ref[...] = jnp.broadcast_to(square_sums(x_ref), inv_ref.shape)


def add_kernel(token, a_ref, b_ref, out_ref):
    out_ref[...] = a_ref[...] + b_ref[...]


def lows_of(at, x_ref, g_ref, gain_ref, w_refs, inv, normed):
    trans = (((1,), (1,)), ((), ()))
    low = back = None
    for c in range(2):
        for k in range(N_Z):
            for y in range(2):
                spot = spot_of(c, k, y)
                here = pl.ds(pl.multiple_of(at[spot], BLOCK), BLOCK)
                norm = (x_ref[:, here].astype(F32) * inv * gain_ref[:, here]).astype(BF16)
                if normed is not None:
                    normed[spot] = norm
                w = columns_of(w_refs, at, c, k, y)
                one = lax.dot_general(norm, w[0], trans, preferred_element_type=F32)
                two = lax.dot_general(g_ref[:, here], w[1], trans, preferred_element_type=F32)
                low, back = (one, two) if low is None else (low + one, back + two)
    return low, back


def terms_kernel(at, x_ref, g_ref, gain_ref, *refs):
    w_refs = refs[:2]
    inv_ref, keep_ref, first_ref, second_ref, low_ref, back_ref, dot_ref, normed = refs[2:]
    inv = inv_ref[:, :1]
    low, back = lows_of(at, x_ref, g_ref, gain_ref, w_refs, inv, normed)
    low16, back16 = low.astype(BF16), back.astype(BF16)
    low_ref[...] = low16
    back_ref[...] = back16
    dots = jnp.sum(back16.astype(F32) * low, axis=1, keepdims=True)
    dot_ref[...] = jnp.broadcast_to(dots, dot_ref.shape)
    low_t, back_t = low16.T, back16.T

    def term(spot):
        here = pl.ds(pl.multiple_of(at[spot], BLOCK), BLOCK)
        down = jnp.dot(back_t, normed[spot], preferred_element_type=F32)
        up = jnp.dot(low_t, g_ref[:, here], preferred_element_type=F32)
        return down, up

    for i, k in enumerate(SLOTS):
        out_ref, j = (first_ref, i) if i < N_FIRST else (second_ref, i - N_FIRST)
        for y in range(2):
            for which, value in enumerate(term(spot_of(1, k, y))):
                out_ref[j, y, which] = value.astype(BF16)
            for which, value in enumerate(term(spot_of(0, k, y))):
                keep_ref[i, y, which] = value


def write_outputs(at, x_ref, g_ref, gain_ref, w_refs, low, back, inv, slope, fwd, bwd, keeps=None):
    for c in range(2):
        for k in range(N_Z):
            for y in range(2):
                here = pl.ds(pl.multiple_of(at[spot_of(c, k, y)], BLOCK), BLOCK)
                w = columns_of(w_refs, at, c, k, y)
                lifted = jnp.dot(low, w[1], preferred_element_type=F32)
                pulled = jnp.dot(back, w[0], preferred_element_type=F32)
                part = x_ref[:, here].astype(F32)
                out = (part + lifted).astype(BF16)
                grad = g_ref[:, here].astype(F32) + (pulled * gain_ref[:, here] * inv - part * slope)
                grad = grad.astype(BF16)
                if keeps is not None:
                    out = jnp.where(keeps, out, jnp.zeros_like(out))
                    grad = jnp.where(keeps, grad, jnp.zeros_like(grad))
                fwd[:, here] = out
                bwd[:, here] = grad


def outputs_kernel(token, at, x_ref, g_ref, gain_ref, *refs):
    w_refs = refs[:2]
    low_ref, back_ref, inv_ref, dot_ref, fwd, bwd = refs[2:]
    inv = inv_ref[:, :1]
    slope = inv * inv * dot_ref[:, :1] * (1.0 / x_ref.shape[1])
    write_outputs(
        at, x_ref, g_ref, gain_ref, w_refs, low_ref[...], back_ref[...], inv, slope, fwd, bwd,
        at[33] == 1,
    )


def extras_kernel(token, at, x_ref, g_ref, gain_ref, *refs):
    w_refs = refs[:2]
    fwd, bwd = refs[2:]
    inv = square_sums(x_ref)
    low, back = lows_of(at, x_ref, g_ref, gain_ref, w_refs, inv, None)
    low16, back16 = low.astype(BF16), back.astype(BF16)
    dots = jnp.sum(back16.astype(F32) * low, axis=1, keepdims=True)
    slope = inv * inv * dots * (1.0 / x_ref.shape[1])
    write_outputs(at, x_ref, g_ref, gain_ref, w_refs, low16, back16, inv, slope, fwd, bwd)


def picks_kernel(at, after, before, x_ref, g_ref, keep_ref, send_ref, pick):
    count = x_ref.shape[0]
    share = count // N_DP
    y, c = at[35], at[36]

    @pl.when(pl.program_id(0) == 0)
    def _():
        column = lax.broadcasted_iota(jnp.int32, (8, count), 1)
        line = lax.broadcasted_iota(jnp.int32, (8, count), 0)
        has_x, has_g = at[37].astype(F32), at[38].astype(F32)
        for c_rel in range(2):
            parts_x, parts_g = [], []
            for k in range(N_Z):
                for y_to in (y, 1 - y):
                    to = place(y_to, k, c if c_rel == 0 else 1 - c)
                    hit_x = (column == after[to] * share + line) & (line < share)
                    hit_g = (column == before[to] * share + line - share) & (line >= share)
                    parts_x.append(jnp.where(hit_x, has_x, 0.0))
                    parts_g.append(jnp.where(hit_g, has_g, 0.0))
            pick[c_rel, 0] = jnp.concatenate(parts_x, axis=0).astype(BF16)
            pick[c_rel, 1] = jnp.concatenate(parts_g, axis=0).astype(BF16)

    for c_rel, out_ref in ((0, keep_ref), (1, send_ref)):
        moved = jnp.dot(pick[c_rel, 0], x_ref[...], preferred_element_type=F32)
        moved += jnp.dot(pick[c_rel, 1], g_ref[...], preferred_element_type=F32)
        out_ref[...] = moved.astype(BF16)


def body(arriving, returning, gain, section_down_weight, section_up_weight, failed, route):
    section = lax.axis_index("section")
    sections = lax.axis_size("section")
    rank = lax.axis_index("dp")
    y, z, c = rank // 16, (rank // 2) % N_Z, rank % 2
    count, width = arriving.shape[2], arriving.shape[3]
    depth = section_down_weight.shape[1]
    share = count // N_DP

    inbound = over_section(arriving, 1)[0, 0]
    upstream = over_section(returning, -1)[0, 0]

    here_x, here_g = arriving[0, 0], returning[0, 0]
    after, before = (section + 1) % sections, (section - 1) % sections
    offsets = [
        place(y if yr == 0 else 1 - y, (z + k) % N_Z, c if cr == 0 else 1 - c) * BLOCK
        for cr in range(2)
        for k in range(N_Z)
        for yr in range(2)
    ]
    flags = [z, rank != failed[section], 0, y, c, rank == failed[after], rank == failed[before]]
    at = jnp.stack([jnp.asarray(v, jnp.int32) for v in offsets + flags])
    smem = pl.BlockSpec(memory_space=pltpu.SMEM)
    vmem = pl.BlockSpec(memory_space=pltpu.VMEM)
    whole = jax.ShapeDtypeStruct((count, width), BF16)
    params = pltpu.CompilerParams(vmem_limit_bytes=28 * 2**20)
    step = 1024
    block = pl.BlockSpec((count, step), lambda i: (0, i))
    moved = pl.pallas_call(
        picks_kernel,
        grid=(width // step,),
        out_shape=[whole, whole],
        in_specs=[smem] * 3 + [block] * 2,
        out_specs=[block] * 2,
        scratch_shapes=[pltpu.VMEM((2, 2, count, count), BF16)],
        compiler_params=params,
        cost_estimate=pl.CostEstimate(
            flops=4 * count * width * count, bytes_accessed=8 * 2**20, transcendentals=0
        ),
        name="picks",
    )(at, route[after], route[before], here_x, here_g)
    crossed = over_dp(moved[1], TO_CORE)
    stat = jax.ShapeDtypeStruct((count, 128), F32)
    free = pl.BlockSpec(memory_space=pl.ANY)
    inv = pl.pallas_call(
        scale_kernel,
        out_shape=stat,
        in_specs=[vmem, free],
        out_specs=vmem,
        compiler_params=params,
        cost_estimate=pl.CostEstimate(
            flops=2 * count * width, bytes_accessed=40 * 2**20, transcendentals=0
        ),
        name="scale",
    )(inbound, upstream)
    rows = pl.pallas_call(
        add_kernel,
        grid=(4,),
        out_shape=whole,
        in_specs=[free] + [pl.BlockSpec((count // 4, width), lambda i: (i, 0))] * 2,
        out_specs=pl.BlockSpec((count // 4, width), lambda i: (i, 0)),
        compiler_params=params,
        cost_estimate=pl.CostEstimate(
            flops=count * width, bytes_accessed=6 * 2**20, transcendentals=0
        ),
        name="add",
    )(inv, moved[0], crossed)
    rows = lax.psum_scatter(
        rows, "dp", scatter_dimension=0, axis_index_groups=Z_GROUPS, tiled=True
    )

    shard = jnp.concatenate([section_down_weight, section_up_weight], axis=0)
    chunk = (2, 2, depth, BLOCK)
    both = jnp.stack([shard, over_dp(shard, TO_Y)], axis=0)
    mine = lax.all_gather(both, "dp", axis=0, axis_index_groups=Z_GROUPS, tiled=False)
    weights = [mine, over_dp(mine, TO_CORE)]

    small = jax.ShapeDtypeStruct((count, depth), BF16)
    keep, first, second, low, back, dots = pl.pallas_call(
        terms_kernel,
        out_shape=[
            jax.ShapeDtypeStruct((N_Z, *chunk), F32),
            jax.ShapeDtypeStruct((N_FIRST, *chunk), BF16),
            jax.ShapeDtypeStruct((N_Z - N_FIRST, *chunk), BF16),
            small,
            small,
            stat,
        ],
        in_specs=[smem] + [vmem] * 6,
        out_specs=[vmem] * 6,
        scratch_shapes=[pltpu.VMEM((32, count, BLOCK), BF16)],
        compiler_params=params,
        cost_estimate=pl.CostEstimate(
            flops=8 * count * width * depth, bytes_accessed=16 * 2**20, transcendentals=0
        ),
        name="terms",
    )(at, inbound, upstream, gain, *weights, inv)
    first, second = over_dp(first, TO_CORE), over_dp(second, TO_CORE)

    def slot(i):
        return pl.BlockSpec((1, *chunk), lambda j: (i, 0, 0, 0, 0))

    def all_of(shape):
        return pl.BlockSpec(shape, lambda j: (0,) * len(shape))

    half = jax.ShapeDtypeStruct((1, *chunk[1:]), BF16)
    full = jax.ShapeDtypeStruct(chunk, BF16)
    quick = pl.CostEstimate(flops=2**18, bytes_accessed=2**20, transcendentals=0)
    up, down = pl.pallas_call(
        open_kernel,
        grid=(1,),
        out_shape=[half, half],
        in_specs=[slot(0), slot(0)],
        out_specs=[all_of(half.shape)] * 2,
        compiler_params=params,
        cost_estimate=quick,
        name="open",
    )(keep, first)

    def fold(token, i, crossed, j, up, down):
        return pl.pallas_call(
            fold_kernel,
            grid=(1,),
            out_shape=[full, full],
            in_specs=[free, slot(i), slot(i + 1), slot(j), slot(j + 1)] + [all_of(up.shape)] * 2,
            out_specs=[all_of(full.shape)] * 2,
            compiler_params=params,
        cost_estimate=quick,
            name="fold",
        )(token, keep, keep, crossed, crossed, up, down)

    forward_out, backward_out = pl.pallas_call(
        outputs_kernel,
        out_shape=[whole, whole],
        in_specs=[free, smem] + [vmem] * 9,
        out_specs=[vmem] * 2,
        compiler_params=params,
        cost_estimate=pl.CostEstimate(
            flops=4 * count * width * depth, bytes_accessed=14 * 2**20, transcendentals=0
        ),
        name="outputs",
    )(first, at, inbound, upstream, gain, *weights, low, back, inv, dots)

    up, down = over_dp(up, TO_UP), over_dp(down, TO_DOWN)
    up, down = fold(forward_out, 1, first, 1, up, down)
    up, down = over_dp(up, TO_UP), over_dp(down, TO_DOWN)
    up, down = fold(up, 3, second, 0, up, down)
    up, down = over_dp(up, TO_UP), over_dp(down, TO_DOWN)
    up, down = fold(up, 5, second, 2, up, down)
    rows = rows + up[0, 0, :1, :1] * 0
    extras = []
    for i, distance in ((0, 1), (1, -1)):
        near = over_both(rows[i * share : (i + 1) * share], distance, 0)
        far = over_both(rows[8 + i * share : 8 + (i + 1) * share], distance, 1)
        extras.append(jnp.pad(near + far, ((0, 16 - share), (0, 0))))
    up, down = over_dp(up, TO_UP), over_dp(down, TO_DOWN)
    own, other = pl.pallas_call(
        close_kernel,
        grid=(1,),
        out_shape=[
            jax.ShapeDtypeStruct(chunk[1:], F32),
            jax.ShapeDtypeStruct(chunk[1:], BF16),
        ],
        in_specs=[slot(7), slot(4)] + [all_of(chunk)] * 2,
        out_specs=[all_of(chunk[1:])] * 2,
        compiler_params=params,
        cost_estimate=quick,
        name="close",
    )(keep, second, up, down)
    other = over_dp(other, TO_Y)
    thin = jax.ShapeDtypeStruct((16, width), BF16)
    rerouted_f, rerouted_b = pl.pallas_call(
        extras_kernel,
        out_shape=[thin, thin],
        in_specs=[free, smem] + [vmem] * 5,
        out_specs=[vmem] * 2,
        compiler_params=params,
        cost_estimate=pl.CostEstimate(
            flops=8 * 16 * width * depth, bytes_accessed=6 * 2**20, transcendentals=0
        ),
        name="extras",
    )(own, at, *extras, gain, *weights)
    shard_out = jax.ShapeDtypeStruct((1, depth, BLOCK), F32)
    grad_down, grad_up = pl.pallas_call(
        finish_kernel,
        out_shape=[shard_out, shard_out],
        in_specs=[vmem] * 2,
        out_specs=[vmem] * 2,
        compiler_params=params,
        cost_estimate=quick,
        name="finish",
    )(own, other)
    return (
        forward_out[None, None],
        backward_out[None, None],
        rerouted_f[None, :share],
        rerouted_b[None, :share],
        grad_down,
        grad_up,
    )


def solution(mesh):
    return jax.shard_map(
        body,
        mesh=mesh,
        in_specs=(
            P("section", "dp", None, None),
            P("section", "dp", None, None),
            P("section", None),
            P("section", None, "dp"),
            P("section", None, "dp"),
            P(),
            P(),
        ),
        out_specs=(
            P("section", "dp", None, None),
            P("section", "dp", None, None),
            P("section", "dp", None),
            P("section", "dp", None),
            P("section", None, "dp"),
            P("section", None, "dp"),
        ),
        check_vma=False,
    )
```

time: 952 us -> 162 us (0.17)
  waiting for transfers between devices: 888 us -> 72.8 us
  starting transfers between devices: 4.41 us -> 30.4 us
  Pallas kernels: 0 us -> 20.3 us
  other arithmetic: 20.4 us -> 1.78 us
  matrix products: 12.4 us -> 0 us
  local copies, waits for them, and re-layouts: 9.11 us -> 19.3 us
    psum x2 -> x0, waiting for transfers between devices: 540 us -> none  [from_root(): return lax.psum(block, axis)]
    reduce_scatter x1, waiting for transfers between devices: 154 us -> 0.02 us  [body(): lax.psum_scatter(rows, 'dp', scatter_dimension=0, axis_index_groups=Z_GRO...]
    all_gather x2 -> x1, waiting for transfers between devices: 149 us -> 0.02 us  [body(): lax.all_gather(both, 'dp', axis=0, axis_index_groups=Z_GROUPS, tiled=False)]
    ppermute x2 -> x20, waiting for transfers between devices: 43 us -> 72.8 us  [the longest x2 35.9 us: over_section(): lax.ppermute(block, 'section', [(i, (i + distance) % n) for i in range(n)])]
    ppermute x2 -> x20, starting transfers between devices: 4.21 us -> 30.3 us  [the longest x14 21.6 us: over_dp(): return lax.ppermute(block, 'dp', pairs)]
    pallas_call x0 -> x12, Pallas kernels: none -> 20.3 us  [the longest x1 5.72 us: body(): pl.pallas_call(outputs_kernel, out_shape=[whole, whole], in_specs=[free,...]
    dot_general x6 -> x0, matrix products: 12.4 us -> none  [the longest x1 3.34 us: body(): lax.dot_general(grads, up_weight, (((1,), (1,)), ((), ())), preferred_ele...]
    unnamed x20 -> x31, local copies, waits for them, and re-layouts: 2.5 us -> 14.7 us
  transfers between devices with their start and end apart: 7 -> 22, of which waited for: 6 -> 12; matrix products, arithmetic and copies ran while one was open for 3% -> 3% of each run, Pallas kernels for 0% -> 12%
where the time goes in v2:
time: 162 us; the launch traced here: 161 us
  waiting for transfers between devices  72.8 us (45%)
  starting transfers between devices  30.4 us (19%)
  Pallas kernels  20.3 us (13%)
  local copies, waits for them, and re-layouts  19.3 us (12%)
  between operations  16.7 us (10%)
  other arithmetic  1.78 us (1%)
    ppermute x2, waiting for transfers between devices, over_section(): lax.ppermute(block, 'section', [(i, (i + distance) % n) for i in range(n)])  35.9 us
    ppermute x14, waiting for transfers between devices, over_dp(): return lax.ppermute(block, 'dp', pairs)  31.1 us
    ppermute x14, starting transfers between devices, over_dp(): return lax.ppermute(block, 'dp', pairs)  21.6 us
    unnamed x31, local copies, waits for them, and re-layouts  14.7 us
    ppermute x4, starting transfers between devices, over_both(): return lax.ppermute(block, ('section', 'dp'), pairs)  6.62 us
    ppermute x4, waiting for transfers between devices, over_both(): return lax.ppermute(block, ('section', 'dp'), pairs)  5.78 us
    pallas_call x1, Pallas kernels, body(): pl.pallas_call(outputs_kernel, out_shape=[whole, whole], in_specs=[free,...  5.72 us
    pallas_call x1, Pallas kernels, body(): pl.pallas_call(terms_kernel, out_shape=[jax.ShapeDtypeStruct((N_Z, *chunk...  4.99 us
  transfers between devices with their start and end apart: 22, of which 12 were waited for; matrix products, arithmetic and copies ran while one was open for 3% of the time, Pallas kernels for 12%

profile of v2, /device:TPU:6, one launch (start us, length us, event | category | flops | bytes accessed | tf_op | source)
XLA Modules:
  0.0 161.3 jit_solution(9632452655903398748)
XLA Ops:
  8.9 3.2 %collective-permute-start.2 = (bf16[2,128,256]{2,1,0:T(8,128)(2,1)S(1)}, bf16[2,128,256]{2,1,0:T(8,128)(2,1)S(1)}, u32[]{:S(2)}, u32[]{:S(2)}) collective-permute-start(bf16[2,128,256]{2,1,0:T(8,128)(2,1)S(1)} %constant_dynamic-update-slice_fusion), channel_id=1, source_target_pairs={{0,16},{1,17},{2,18},{3,19},{4,20},{5,21},{6,22},{7,23},{8,24},{9,... | collective-permute-start | bytes 393224 | tf_op jit(solution)/shard_map/ppermute | solution.py:29
  12.1 3.5 %collective-permute-done.2 = bf16[2,128,256]{2,1,0:T(8,128)(2,1)S(1)} collective-permute-done((bf16[2,128,256]{2,1,0:T(8,128)(2,1)S(1)}, bf16[2,128,256]{2,1,0:T(8,128)(2,1)S(1)}, u32[]{:S(2)}, u32[]{:S(2)}) %collective-permute-start.2) | collective-permute-done | bytes 131104 | tf_op jit(solution)/shard_map/ppermute | solution.py:29
  16.4 1.6 collective-permute-start
  18.5 1.4 fusion.1
  22.7 1.6 copy-done.7
  24.3 1.6 copy-done.8
  25.9 4.8 %picks.1 = (bf16[128,8192]{1,0:T(8,128)(2,1)S(1)}, bf16[128,8192]{1,0:T(8,128)(2,1)S(1)}) custom-call(s32[39]{0:T(128)S(1)} %stack.176.at, s32[32]{0:T(128)S(1)} %get-tuple-element.59.after, s32[32]{0:T(128)S(1)} %get-tuple-element.58.before, bf16[128,8192]{1,0:T(8,128)(2,1)S(1)} %bitcast.66, bf16[128,8192]{1,0:T(8,128)(2,1)S(1)} %bitcast.67), custom_call_target="tpu_custom_call" | custom-call | flops 536870912 | bytes 8388608 | tf_op jit(solution)/shard_map/picks/pallas_call | solution.py:256
  30.8 32.4 %collective-permute-done = bf16[1,1,128,8192]{3,2,1,0:T(8,128)(2,1)S(1)} collective-permute-done((bf16[1,1,128,8192]{3,2,1,0:T(8,128)(2,1)}, bf16[1,1,128,8192]{3,2,1,0:T(8,128)(2,1)S(1)}, u32[]{:S(2)}, u32[]{:S(2)}) %collective-permute-start) | collective-permute-done | bytes 2097184 | tf_op jit(solution)/shard_map/ppermute | solution.py:34
  63.2 3.4 %collective-permute-done.1 = bf16[1,1,128,8192]{3,2,1,0:T(8,128)(2,1)} collective-permute-done((bf16[1,1,128,8192]{3,2,1,0:T(8,128)(2,1)}, bf16[1,1,128,8192]{3,2,1,0:T(8,128)(2,1)}, u32[]{:S(2)}, u32[]{:S(2)}) %collective-permute-start.1) | collective-permute-done | bytes 2097184 | tf_op jit(solution)/shard_map/ppermute | solution.py:34
  69.1 4.4 %collective-permute-done.3.refs_1_ = bf16[8,2,2,128,256]{4,3,2,1,0:T(8,128)(2,1)S(1)} collective-permute-done((bf16[8,2,2,128,256]{4,3,2,1,0:T(8,128)(2,1)}, bf16[8,2,2,128,256]{4,3,2,1,0:T(8,128)(2,1)S(1)}, u32[]{:S(2)}, u32[]{:S(2)}) %collective-permute-start.3) | collective-permute-done | bytes 2097184 | tf_op jit(solution)/shard_map/ppermute | solution.py:29
  73.5 1.6 copy-done.2
  75.1 5.0 %terms.1 = (f32[8,2,2,128,256]{4,3,2,1,0:T(8,128)S(1)}, bf16[3,2,2,128,256]{4,3,2,1,0:T(8,128)(2,1)S(1)}, bf16[5,2,2,128,256]{4,3,2,1,0:T(8,128)(2,1)S(1)}, bf16...) custom-call(s32[39]{0:T(128)S(1)} %stack.176.at, bf16[128,8192]{1,0:T(8,128)(2,1)S(1)} %bitcast.60, ...), custom_call_target="tpu_custom_call" | custom-call | flops 1073741824 | bytes 16777216 | tf_op jit(solution)/shard_map/terms/pallas_call | solution.py:306
  80.7 3.6 %collective-permute-done.4.token.crossed.cross_up.cross_down = bf16[3,2,2,128,256]{4,3,2,1,0:T(8,128)(2,1)S(1)} collective-permute-done((bf16[3,2,2,128,256]{4,3,2,1,0:T(8,128)(2,1)S(1)}, bf16[3,2,2,128,256]{4,3,2,1,0:T(8,128)(2,1)S(1)}, u32[]{:S(2)}, u32[]{:S(2)}) %collective-permute-start.4) | collective-permute-done | bytes 786464 | tf_op jit(solution)/shard_map/ppermute | solution.py:29
  84.4 2.0 %collective-permute-start.6 = (bf16[1,2,128,256]{3,2,1,0:T(8,128)(2,1)S(1)}, bf16[1,2,128,256]{3,2,1,0:T(8,128)(2,1)S(1)}, u32[]{:S(2)}, u32[]{:S(2)}) collective-permute-start(bf16[1,2,128,256]{3,2,1,0:T(8,128)(2,1)S(1)} %get-tuple-element.38), channel_id=1, source_target_pairs={{0,2},{1,3},{2,4},{3,5},{4,6},{5,7},{6,8},{7,9},{8,10},{9,11},{10,... | collective-permute-start | bytes 393224 | tf_op jit(solution)/shard_map/ppermute | solution.py:29
  86.4 4.0 %collective-permute-start.7 = (bf16[1,2,128,256]{3,2,1,0:T(8,128)(2,1)S(1)}, bf16[1,2,128,256]{3,2,1,0:T(8,128)(2,1)S(1)}, u32[]{:S(2)}, u32[]{:S(2)}) collective-permute-start(bf16[1,2,128,256]{3,2,1,0:T(8,128)(2,1)S(1)} %get-tuple-element.39), channel_id=1, source_target_pairs={{0,14},{1,15},{2,0},{3,1},{4,2},{5,3},{6,4},{7,5},{8,6},{9,7},{10,... | collective-permute-start | bytes 393224 | tf_op jit(solution)/shard_map/ppermute | solution.py:29
  90.4 5.7 %outputs.1 = (bf16[128,8192]{1,0:T(8,128)(2,1)}, bf16[128,8192]{1,0:T(8,128)(2,1)}) custom-call(bf16[3,2,2,128,256]{4,3,2,1,0:T(8,128)(2,1)S(1)} %collective-permute-done.4.token.crossed.cross_up.cross_down, s32[39]{0:T(128)S(1)} %stack.176.at, bf16[128,8192]{1,0:T(8,128)(2,1)S(1)} %bitcast.61, bf16[128,8192]{1,0:T(8,128)(2,1)} %bitcast.42.g_ref, ...), custom_call_target="tpu_custom_call" | custom-call | flops 536870912 | bytes 14680064 | tf_op jit(solution)/shard_map/outputs/pallas_call | solution.py:359
  97.0 1.6 copy-done.9
  99.1 3.2 %collective-permute-start.9 = (bf16[2,2,128,256]{3,2,1,0:T(8,128)(2,1)S(1)}, bf16[2,2,128,256]{3,2,1,0:T(8,128)(2,1)S(1)}, u32[]{:S(2)}, u32[]{:S(2)}) collective-permute-start(bf16[2,2,128,256]{3,2,1,0:T(8,128)(2,1)S(1)} %get-tuple-element.41), channel_id=1, source_target_pairs={{0,14},{1,15},{2,0},{3,1},{4,2},{5,3},{6,4},{7,5},{8,6},{9,7},{10,... | collective-permute-start | bytes 786440 | tf_op jit(solution)/shard_map/ppermute | solution.py:29
  102.3 12.1 %collective-permute-done.8.token.got_up = bf16[2,2,128,256]{3,2,1,0:T(8,128)(2,1)S(1)} collective-permute-done((bf16[2,2,128,256]{3,2,1,0:T(8,128)(2,1)S(1)}, bf16[2,2,128,256]{3,2,1,0:T(8,128)(2,1)S(1)}, u32[]{:S(2)}, u32[]{:S(2)}) %collective-permute-start.8) | collective-permute-done | bytes 262176 | tf_op jit(solution)/shard_map/ppermute | solution.py:29
  114.6 1.8 %collective-permute-start.10 = (bf16[2,2,128,256]{3,2,1,0:T(8,128)(2,1)S(1)}, bf16[2,2,128,256]{3,2,1,0:T(8,128)(2,1)S(1)}, u32[]{:S(2)}, u32[]{:S(2)}) collective-permute-start(bf16[2,2,128,256]{3,2,1,0:T(8,128)(2,1)S(1)} %get-tuple-element.42), channel_id=1, source_target_pairs={{0,2},{1,3},{2,4},{3,5},{4,6},{5,7},{6,8},{7,9},{8,10},{9,11},{10,... | collective-permute-start | bytes 786440 | tf_op jit(solution)/shard_map/ppermute | solution.py:29
  116.4 1.5 collective-permute-start.11
  117.9 5.3 %collective-permute-done.10.token.got_up = bf16[2,2,128,256]{3,2,1,0:T(8,128)(2,1)S(1)} collective-permute-done((bf16[2,2,128,256]{3,2,1,0:T(8,128)(2,1)S(1)}, bf16[2,2,128,256]{3,2,1,0:T(8,128)(2,1)S(1)}, u32[]{:S(2)}, u32[]{:S(2)}) %collective-permute-start.10) | collective-permute-done | bytes 262176 | tf_op jit(solution)/shard_map/ppermute | solution.py:29
  123.4 1.5 collective-permute-start.12
  125.4 1.8 %collective-permute-start.13 = (bf16[2,2,128,256]{3,2,1,0:T(8,128)(2,1)S(1)}, bf16[2,2,128,256]{3,2,1,0:T(8,128)(2,1)S(1)}, u32[]{:S(2)}, u32[]{:S(2)}) collective-permute-start(bf16[2,2,128,256]{3,2,1,0:T(8,128)(2,1)S(1)} %get-tuple-element.45), channel_id=1, source_target_pairs={{0,14},{1,15},{2,0},{3,1},{4,2},{5,3},{6,4},{7,5},{8,6},{9,7},{10,... | collective-permute-start | bytes 786440 | tf_op jit(solution)/shard_map/ppermute | solution.py:29
  129.7 2.5 %collective-permute-start.16 = (bf16[4,8192]{1,0:T(4,128)(2,1)S(1)}, bf16[4,8192]{1,0:T(4,128)(2,1)S(1)}, u32[]{:S(2)}, u32[]{:S(2)}) collective-permute-start(bf16[4,8192]{1,0:T(4,128)(2,1)S(1)} %get-tuple-element.56), channel_id=1, source_target_pairs={{0,48},{1,49},{2,50},{3,51},{4,52},{5,53},{6,54},{7,55},{8,56},{9,... | collective-permute-start | bytes 196616 | tf_op jit(solution)/shard_map/ppermute | solution.py:44
  132.2 1.7 %collective-permute-start.17 = (bf16[4,8192]{1,0:T(4,128)(2,1)S(1)}, bf16[4,8192]{1,0:T(4,128)(2,1)S(1)}, u32[]{:S(2)}, u32[]{:S(2)}) collective-permute-start(bf16[4,8192]{1,0:T(4,128)(2,1)S(1)} %get-tuple-element.55), channel_id=1, source_target_pairs={{0,224},{1,225},{2,226},{3,227},{4,228},{5,229},{6,230},{7,231},{8... | collective-permute-start | bytes 196616 | tf_op jit(solution)/shard_map/ppermute | solution.py:44
  133.9 1.7 %collective-permute-start.18 = (bf16[4,8192]{1,0:T(4,128)(2,1)S(1)}, bf16[4,8192]{1,0:T(4,128)(2,1)S(1)}, u32[]{:S(2)}, u32[]{:S(2)}) collective-permute-start(bf16[4,8192]{1,0:T(4,128)(2,1)S(1)} %get-tuple-element.54), channel_id=1, source_target_pairs={{0,240},{1,241},{2,242},{3,243},{4,244},{5,245},{6,246},{7,247},{8... | collective-permute-start | bytes 196616 | tf_op jit(solution)/shard_map/ppermute | solution.py:44
  136.7 1.9 %collective-permute-done.17 = bf16[4,8192]{1,0:T(4,128)(2,1)S(1)} collective-permute-done((bf16[4,8192]{1,0:T(4,128)(2,1)S(1)}, bf16[4,8192]{1,0:T(4,128)(2,1)S(1)}, u32[]{:S(2)}, u32[]{:S(2)}) %collective-permute-start.17) | collective-permute-done | bytes 65568 | tf_op jit(solution)/shard_map/ppermute | solution.py:44
  138.6 2.9 %collective-permute-done.18 = bf16[4,8192]{1,0:T(4,128)(2,1)S(1)} collective-permute-done((bf16[4,8192]{1,0:T(4,128)(2,1)S(1)}, bf16[4,8192]{1,0:T(4,128)(2,1)S(1)}, u32[]{:S(2)}, u32[]{:S(2)}) %collective-permute-start.18) | collective-permute-done | bytes 65568 | tf_op jit(solution)/shard_map/ppermute | solution.py:44
  143.0 2.2 %copy-done.1 = f32[8,2,2,128,256]{4,3,2,1,0:T(8,128)S(1)} copy-done((f32[8,2,2,128,256]{4,3,2,1,0:T(8,128)S(1)}, f32[8,2,2,128,256]{4,3,2,1,0:T(8,128)}, u32[]{:S(2)}) %copy-start.1) | copy-done | bytes 4194328
  147.2 1.5 collective-permute-start.19
  149.3 2.6 %extras.1 = (bf16[16,8192]{1,0:T(8,128)(2,1)S(1)}, bf16[16,8192]{1,0:T(8,128)(2,1)S(1)}) custom-call(f32[2,128,256]{2,1,0:T(8,128)S(1)} %get-tuple-element.46.token.own, s32[39]{0:T(128)S(1)} %stack.176.at, bf16[16,8192]{1,0:T(8,128)(2,1)S(1)} %pad.7.x_ref, bf16[16,8192]{1,0:T(8,128)(2,1)S(1)} %pad.8.g_ref, f32[1,8192]{1,0:T(1,128)S(1)} %copy-done.10, ...), custom_call_target="tpu_custom_call" | custom-call | flops 134217728 | bytes 6291456 | tf_op jit(solution)/shard_map/extras/pallas_call | solution.py:399
  (70 shorter events, 18.8 us)
Async XLA Ops:
  7.2 61.8 %all-gather.3.cloned.1.call-start = ((), (), s32[]{:S(2)}) async-start(), calls=%async_computation.2 | async-start | bytes 2359296 | tf_op jit(solution)/shard_map/all_gather | solution.py:302
  8.9 6.7 %collective-permute-start.2 = (bf16[2,128,256]{2,1,0:T(8,128)(2,1)S(1)}, bf16[2,128,256]{2,1,0:T(8,128)(2,1)S(1)}, u32[]{:S(2)}, u32[]{:S(2)}) collective-permute-start(bf16[2,128,256]{2,1,0:T(8,128)(2,1)S(1)} %constant_dynamic-update-slice_fusion), channel_id=1, source_target_pairs={{0,16},{1,17},{2,18},{3,19},{4,20},{5,21},{6,22},{7,23},{8,24},{9,... | collective-permute-start | bytes 393224 | tf_op jit(solution)/shard_map/ppermute | solution.py:29
  16.4 111.5 %reduce-scatter.2.cloned.1.call-start = ((), (), s32[]{:S(2)}) async-start(), calls=%async_computation.1 | async-start | bytes 2359296 | tf_op jit(solution)/shard_map/reduce_scatter | solution.py:295
  16.4 46.8 %collective-permute-start = (bf16[1,1,128,8192]{3,2,1,0:T(8,128)(2,1)}, bf16[1,1,128,8192]{3,2,1,0:T(8,128)(2,1)S(1)}, u32[]{:S(2)}, u32[]{:S(2)}) collective-permute-start(bf16[1,1,128,8192]{3,2,1,0:T(8,128)(2,1)} %param.7), channel_id=1, source_target_pairs={{0,32},{32,64},{64,96},{96,128},{128,160},{160,192},{192,224},{224... | collective-permute-start | bytes 6291464 | tf_op jit(solution)/shard_map/ppermute | solution.py:34
  18.0 48.6 %collective-permute-start.1 = (bf16[1,1,128,8192]{3,2,1,0:T(8,128)(2,1)}, bf16[1,1,128,8192]{3,2,1,0:T(8,128)(2,1)}, u32[]{:S(2)}, u32[]{:S(2)}) collective-permute-start(bf16[1,1,128,8192]{3,2,1,0:T(8,128)(2,1)} %param.8), channel_id=1, source_target_pairs={{0,224},{32,0},{64,32},{96,64},{128,96},{160,128},{192,160},{224,1... | collective-permute-start | bytes 6291464 | tf_op jit(solution)/shard_map/ppermute | solution.py:34
  22.7 1.6 copy-start.7
  24.3 1.6 copy-start.8
  30.7 36.6 %collective-permute-start.14 = (bf16[128,8192]{1,0:T(8,128)(2,1)S(1)}, bf16[128,8192]{1,0:T(8,128)(2,1)S(1)}, u32[]{:S(2)}, u32[]{:S(2)}) collective-permute-start(bf16[128,8192]{1,0:T(8,128)(2,1)S(1)} %get-tuple-element.48), channel_id=1, source_target_pairs={{0,1},{1,0},{2,3},{3,2},{4,5},{5,4},{6,7},{7,6},{8,9},{9,8},{10,11... | collective-permute-start | bytes 6291464 | tf_op jit(solution)/shard_map/ppermute | solution.py:29
  69.0 4.5 %copy-start.10 = (f32[1,8192]{1,0:T(1,128)S(1)}, f32[1,8192]{1,0:T(1,128)}, u32[]{:S(2)}) copy-start(f32[1,8192]{1,0:T(1,128)} %gain_ref.5) | copy-start | bytes 98308
  69.0 4.5 %collective-permute-start.3 = (bf16[8,2,2,128,256]{4,3,2,1,0:T(8,128)(2,1)}, bf16[8,2,2,128,256]{4,3,2,1,0:T(8,128)(2,1)S(1)}, u32[]{:S(2)}, u32[]{:S(2)}) collective-permute-start(bf16[8,2,2,128,256]{4,3,2,1,0:T(8,128)(2,1)} %bitcast.62), channel_id=1, source_target_pairs={{0,1},{1,0},{2,3},{3,2},{4,5},{5,4},{6,7},{7,6},{8,9},{9,8},{10,11... | collective-permute-start | bytes 6291464 | tf_op jit(solution)/shard_map/ppermute | solution.py:29
  73.5 1.6 copy-start.2
  75.1 15.3 %copy-start.4 = (bf16[8,2,2,128,256]{4,3,2,1,0:T(8,128)(2,1)}, bf16[8,2,2,128,256]{4,3,2,1,0:T(8,128)(2,1)S(1)}, u32[]{:S(2)}) copy-start(bf16[8,2,2,128,256]{4,3,2,1,0:T(8,128)(2,1)S(1)} %collective-permute-done.3.refs_1_) | copy-start | bytes 6291460
  80.1 43.2 %copy-start = (f32[8,2,2,128,256]{4,3,2,1,0:T(8,128)}, f32[8,2,2,128,256]{4,3,2,1,0:T(8,128)S(1)}, u32[]{:S(2)}) copy-start(f32[8,2,2,128,256]{4,3,2,1,0:T(8,128)S(1)} %get-tuple-element.36.keep.keep_up.keep_down) | copy-start | bytes 12582916
  80.1 34.3 %collective-permute-start.5 = (bf16[5,2,2,128,256]{4,3,2,1,0:T(8,128)(2,1)S(1)}, bf16[5,2,2,128,256]{4,3,2,1,0:T(8,128)(2,1)S(1)}, u32[]{:S(2)}, u32[]{:S(2)}) collective-permute-start(bf16[5,2,2,128,256]{4,3,2,1,0:T(8,128)(2,1)S(1)} %get-tuple-element.37), channel_id=1, source_target_pairs={{0,1},{1,0},{2,3},{3,2},{4,5},{5,4},{6,7},{7,6},{8,9},{9,8},{10,11... | collective-permute-start | bytes 3932168 | tf_op jit(solution)/shard_map/ppermute | solution.py:29
  80.3 4.0 %collective-permute-start.4 = (bf16[3,2,2,128,256]{4,3,2,1,0:T(8,128)(2,1)S(1)}, bf16[3,2,2,128,256]{4,3,2,1,0:T(8,128)(2,1)S(1)}, u32[]{:S(2)}, u32[]{:S(2)}) collective-permute-start(bf16[3,2,2,128,256]{4,3,2,1,0:T(8,128)(2,1)S(1)} %get-tuple-element.30), channel_id=1, source_target_pairs={{0,1},{1,0},{2,3},{3,2},{4,5},{5,4},{6,7},{7,6},{8,9},{9,8},{10,11... | collective-permute-start | bytes 2359304 | tf_op jit(solution)/shard_map/ppermute | solution.py:29
  84.4 12.7 %collective-permute-start.6 = (bf16[1,2,128,256]{3,2,1,0:T(8,128)(2,1)S(1)}, bf16[1,2,128,256]{3,2,1,0:T(8,128)(2,1)S(1)}, u32[]{:S(2)}, u32[]{:S(2)}) collective-permute-start(bf16[1,2,128,256]{3,2,1,0:T(8,128)(2,1)S(1)} %get-tuple-element.38), channel_id=1, source_target_pairs={{0,2},{1,3},{2,4},{3,5},{4,6},{5,7},{6,8},{7,9},{8,10},{9,11},{10,... | collective-permute-start | bytes 393224 | tf_op jit(solution)/shard_map/ppermute | solution.py:29
  86.4 10.7 %collective-permute-start.7 = (bf16[1,2,128,256]{3,2,1,0:T(8,128)(2,1)S(1)}, bf16[1,2,128,256]{3,2,1,0:T(8,128)(2,1)S(1)}, u32[]{:S(2)}, u32[]{:S(2)}) collective-permute-start(bf16[1,2,128,256]{3,2,1,0:T(8,128)(2,1)S(1)} %get-tuple-element.39), channel_id=1, source_target_pairs={{0,14},{1,15},{2,0},{3,1},{4,2},{5,3},{6,4},{7,5},{8,6},{9,7},{10,... | collective-permute-start | bytes 393224 | tf_op jit(solution)/shard_map/ppermute | solution.py:29
  97.0 1.6 %copy-start.9 = (bf16[128,8192]{1,0:T(8,128)(2,1)S(1)}, bf16[128,8192]{1,0:T(8,128)(2,1)}, u32[]{:S(2)}) copy-start(bf16[128,8192]{1,0:T(8,128)(2,1)} %get-tuple-element.34.token) | copy-start | bytes 6291460
  98.8 15.6 %collective-permute-start.8 = (bf16[2,2,128,256]{3,2,1,0:T(8,128)(2,1)S(1)}, bf16[2,2,128,256]{3,2,1,0:T(8,128)(2,1)S(1)}, u32[]{:S(2)}, u32[]{:S(2)}) collective-permute-start(bf16[2,2,128,256]{3,2,1,0:T(8,128)(2,1)S(1)} %get-tuple-element.40), channel_id=1, source_target_pairs={{0,2},{1,3},{2,4},{3,5},{4,6},{5,7},{6,8},{7,9},{8,10},{9,11},{10,... | collective-permute-start | bytes 786440 | tf_op jit(solution)/shard_map/ppermute | solution.py:29
  99.1 15.3 %collective-permute-start.9 = (bf16[2,2,128,256]{3,2,1,0:T(8,128)(2,1)S(1)}, bf16[2,2,128,256]{3,2,1,0:T(8,128)(2,1)S(1)}, u32[]{:S(2)}, u32[]{:S(2)}) collective-permute-start(bf16[2,2,128,256]{3,2,1,0:T(8,128)(2,1)S(1)} %get-tuple-element.41), channel_id=1, source_target_pairs={{0,14},{1,15},{2,0},{3,1},{4,2},{5,3},{6,4},{7,5},{8,6},{9,7},{10,... | collective-permute-start | bytes 786440 | tf_op jit(solution)/shard_map/ppermute | solution.py:29
  114.6 8.7 %collective-permute-start.10 = (bf16[2,2,128,256]{3,2,1,0:T(8,128)(2,1)S(1)}, bf16[2,2,128,256]{3,2,1,0:T(8,128)(2,1)S(1)}, u32[]{:S(2)}, u32[]{:S(2)}) collective-permute-start(bf16[2,2,128,256]{3,2,1,0:T(8,128)(2,1)S(1)} %get-tuple-element.42), channel_id=1, source_target_pairs={{0,2},{1,3},{2,4},{3,5},{4,6},{5,7},{6,8},{7,9},{8,10},{9,11},{10,... | collective-permute-start | bytes 786440 | tf_op jit(solution)/shard_map/ppermute | solution.py:29
  116.4 6.8 %collective-permute-start.11 = (bf16[2,2,128,256]{3,2,1,0:T(8,128)(2,1)S(1)}, bf16[2,2,128,256]{3,2,1,0:T(8,128)(2,1)S(1)}, u32[]{:S(2)}, u32[]{:S(2)}) collective-permute-start(bf16[2,2,128,256]{3,2,1,0:T(8,128)(2,1)S(1)} %get-tuple-element.43), channel_id=1, source_target_pairs={{0,14},{1,15},{2,0},{3,1},{4,2},{5,3},{6,4},{7,5},{8,6},{9,7},{10,... | collective-permute-start | bytes 786440 | tf_op jit(solution)/shard_map/ppermute | solution.py:29
  123.4 18.1 %collective-permute-start.12 = (bf16[2,2,128,256]{3,2,1,0:T(8,128)(2,1)S(1)}, bf16[2,2,128,256]{3,2,1,0:T(8,128)(2,1)S(1)}, u32[]{:S(2)}, u32[]{:S(2)}) collective-permute-start(bf16[2,2,128,256]{3,2,1,0:T(8,128)(2,1)S(1)} %get-tuple-element.44), channel_id=1, source_target_pairs={{0,2},{1,3},{2,4},{3,5},{4,6},{5,7},{6,8},{7,9},{8,10},{9,11},{10,... | collective-permute-start | bytes 786440 | tf_op jit(solution)/shard_map/ppermute | solution.py:29
  125.4 16.9 %collective-permute-start.13 = (bf16[2,2,128,256]{3,2,1,0:T(8,128)(2,1)S(1)}, bf16[2,2,128,256]{3,2,1,0:T(8,128)(2,1)S(1)}, u32[]{:S(2)}, u32[]{:S(2)}) collective-permute-start(bf16[2,2,128,256]{3,2,1,0:T(8,128)(2,1)S(1)} %get-tuple-element.45), channel_id=1, source_target_pairs={{0,14},{1,15},{2,0},{3,1},{4,2},{5,3},{6,4},{7,5},{8,6},{9,7},{10,... | collective-permute-start | bytes 786440 | tf_op jit(solution)/shard_map/ppermute | solution.py:29
  129.0 4.9 %collective-permute-start.15 = (bf16[4,8192]{1,0:T(4,128)(2,1)S(1)}, bf16[4,8192]{1,0:T(4,128)(2,1)S(1)}, u32[]{:S(2)}, u32[]{:S(2)}) collective-permute-start(bf16[4,8192]{1,0:T(4,128)(2,1)S(1)} %get-tuple-element.57), channel_id=1, source_target_pairs={{0,32},{1,33},{2,34},{3,35},{4,36},{5,37},{6,38},{7,39},{8,40},{9,... | collective-permute-start | bytes 196616 | tf_op jit(solution)/shard_map/ppermute | solution.py:44
  129.7 6.9 %collective-permute-start.16 = (bf16[4,8192]{1,0:T(4,128)(2,1)S(1)}, bf16[4,8192]{1,0:T(4,128)(2,1)S(1)}, u32[]{:S(2)}, u32[]{:S(2)}) collective-permute-start(bf16[4,8192]{1,0:T(4,128)(2,1)S(1)} %get-tuple-element.56), channel_id=1, source_target_pairs={{0,48},{1,49},{2,50},{3,51},{4,52},{5,53},{6,54},{7,55},{8,56},{9,... | collective-permute-start | bytes 196616 | tf_op jit(solution)/shard_map/ppermute | solution.py:44
  132.2 6.4 %collective-permute-start.17 = (bf16[4,8192]{1,0:T(4,128)(2,1)S(1)}, bf16[4,8192]{1,0:T(4,128)(2,1)S(1)}, u32[]{:S(2)}, u32[]{:S(2)}) collective-permute-start(bf16[4,8192]{1,0:T(4,128)(2,1)S(1)} %get-tuple-element.55), channel_id=1, source_target_pairs={{0,224},{1,225},{2,226},{3,227},{4,228},{5,229},{6,230},{7,231},{8... | collective-permute-start | bytes 196616 | tf_op jit(solution)/shard_map/ppermute | solution.py:44
  133.9 7.6 %collective-permute-start.18 = (bf16[4,8192]{1,0:T(4,128)(2,1)S(1)}, bf16[4,8192]{1,0:T(4,128)(2,1)S(1)}, u32[]{:S(2)}, u32[]{:S(2)}) collective-permute-start(bf16[4,8192]{1,0:T(4,128)(2,1)S(1)} %get-tuple-element.54), channel_id=1, source_target_pairs={{0,240},{1,241},{2,242},{3,243},{4,244},{5,245},{6,246},{7,247},{8... | collective-permute-start | bytes 196616 | tf_op jit(solution)/shard_map/ppermute | solution.py:44
  143.0 2.2 %copy-start.1 = (f32[8,2,2,128,256]{4,3,2,1,0:T(8,128)S(1)}, f32[8,2,2,128,256]{4,3,2,1,0:T(8,128)}, u32[]{:S(2)}) copy-start(f32[8,2,2,128,256]{4,3,2,1,0:T(8,128)} %copy-done) | copy-start | bytes 12582916
  147.1 1.6 %copy-start.3 = (bf16[16,2,128,256]{3,2,1,0:T(8,128)(2,1)S(1)}, bf16[16,2,128,256]{3,2,1,0:T(8,128)(2,1)}, u32[]{:S(2)}) copy-start(bf16[16,2,128,256]{3,2,1,0:T(8,128)(2,1)} %all-gather.3.cloned.1.call-done) | copy-start | bytes 6291460
  147.1 2.2 %copy-start.5 = (bf16[8,2,2,128,256]{4,3,2,1,0:T(8,128)(2,1)S(1)}, bf16[8,2,2,128,256]{4,3,2,1,0:T(8,128)(2,1)}, u32[]{:S(2)}) copy-start(bf16[8,2,2,128,256]{4,3,2,1,0:T(8,128)(2,1)} %copy-done.4) | copy-start | bytes 6291460
  147.2 6.6 %collective-permute-start.19 = (bf16[2,128,256]{2,1,0:T(8,128)(2,1)S(1)}, bf16[2,128,256]{2,1,0:T(8,128)(2,1)S(1)}, u32[]{:S(2)}, u32[]{:S(2)}) collective-permute-start(bf16[2,128,256]{2,1,0:T(8,128)(2,1)S(1)} %get-tuple-element.51), channel_id=1, source_target_pairs={{0,16},{1,17},{2,18},{3,19},{4,20},{5,21},{6,22},{7,23},{8,24},{9,... | collective-permute-start | bytes 393224 | tf_op jit(solution)/shard_map/ppermute | solution.py:29
  (5 other events, 4.7 us)
Sparse Core Ops, SparseCore 0:
  16.5 43.8 all-gather.2
  69.1 49.6 reduce-scatter.1

commit v3 on v2

--- a/solution.py
+++ b/solution.py
@@ -48,6 +48,11 @@
 N_FIRST = 3
 
 
+def both_kernel(token, mine, other, out):
+    out[0] = mine[...]
+    out[1] = other[...]
+
+
 def columns_of(refs, at, c, k, y):
     return refs[c].at[lax.rem(at[32] + k, N_Z), y]
 
@@ -58,6 +63,10 @@
 
 def wide(ref):
     return ref[...].astype(F32)
+
+
+def later_kernel(token, a_ref, out_ref):
+    out_ref[...] = a_ref[...]
 
 
 def open_kernel(keep, crossed, up, down):
@@ -79,7 +88,7 @@
         down[...] = (low + wide(got_down)).astype(BF16)
 
 
-def close_kernel(keep, crossed, got_up, got_down, own, other):
+def close_kernel(token_1, token_2, keep, crossed, got_up, got_down, own, other):
     total = (keep[0] + wide(crossed)[0]) + (wide(got_up) + wide(got_down))
     own[...] = total[0]
     other[...] = total[1].astype(BF16)
@@ -107,7 +116,7 @@
     inv_ref[...] = jnp.broadcast_to(square_sums(x_ref), inv_ref.shape)
 
 
-def add_kernel(token, a_ref, b_ref, out_ref):
+def add_kernel(a_ref, b_ref, out_ref):
     out_ref[...] = a_ref[...] + b_ref[...]
 
 
@@ -129,7 +138,7 @@
     return low, back
 
 
-def terms_kernel(at, x_ref, g_ref, gain_ref, *refs):
+def terms_kernel(token, at, x_ref, g_ref, gain_ref, *refs):
     w_refs = refs[:2]
     inv_ref, keep_ref, first_ref, second_ref, low_ref, back_ref, dot_ref, normed = refs[2:]
     inv = inv_ref[:, :1]
@@ -177,7 +186,8 @@
 
 def outputs_kernel(token, at, x_ref, g_ref, gain_ref, *refs):
     w_refs = refs[:2]
-    low_ref, back_ref, inv_ref, dot_ref, fwd, bwd = refs[2:]
+    low_ref, back_ref, inv_ref, dot_ref, fwd, bwd, mark = refs[2:]
+    mark[...] = jnp.zeros_like(mark)
     inv = inv_ref[:, :1]
     slope = inv * inv * dot_ref[:, :1] * (1.0 / x_ref.shape[1])
     write_outputs(
@@ -197,23 +207,26 @@
     write_outputs(at, x_ref, g_ref, gain_ref, w_refs, low16, back16, inv, slope, fwd, bwd)
 
 
-def picks_kernel(at, after, before, x_ref, g_ref, keep_ref, send_ref, pick):
+def picks_kernel(who, failed, route, x_ref, g_ref, keep_ref, send_ref, pick):
     count = x_ref.shape[0]
     share = count // N_DP
-    y, c = at[35], at[36]
+    rank, section = who[0], who[1]
+    y, c = rank // 16, rank % 2
+    after, before = lax.rem(section + 1, 8), lax.rem(section + 7, 8)
 
     @pl.when(pl.program_id(0) == 0)
     def _():
         column = lax.broadcasted_iota(jnp.int32, (8, count), 1)
         line = lax.broadcasted_iota(jnp.int32, (8, count), 0)
-        has_x, has_g = at[37].astype(F32), at[38].astype(F32)
+        has_x = jnp.where(failed[after] == rank, 1.0, 0.0)
+        has_g = jnp.where(failed[before] == rank, 1.0, 0.0)
         for c_rel in range(2):
             parts_x, parts_g = [], []
             for k in range(N_Z):
                 for y_to in (y, 1 - y):
                     to = place(y_to, k, c if c_rel == 0 else 1 - c)
-                    hit_x = (column == after[to] * share + line) & (line < share)
-                    hit_g = (column == before[to] * share + line - share) & (line >= share)
+                    hit_x = (column == route[after, to] * share + line) & (line < share)
+                    hit_g = (column == route[before, to] * share + line - share) & (line >= share)
                     parts_x.append(jnp.where(hit_x, has_x, 0.0))
                     parts_g.append(jnp.where(hit_g, has_g, 0.0))
             pick[c_rel, 0] = jnp.concatenate(parts_x, axis=0).astype(BF16)
@@ -227,7 +240,6 @@
 
 def body(arriving, returning, gain, section_down_weight, section_up_weight, failed, route):
     section = lax.axis_index("section")
-    sections = lax.axis_size("section")
     rank = lax.axis_index("dp")
     y, z, c = rank // 16, (rank // 2) % N_Z, rank % 2
     count, width = arriving.shape[2], arriving.shape[3]
@@ -238,18 +250,16 @@
     upstream = over_section(returning, -1)[0, 0]
 
     here_x, here_g = arriving[0, 0], returning[0, 0]
-    after, before = (section + 1) % sections, (section - 1) % sections
-    offsets = [
-        place(y if yr == 0 else 1 - y, (z + k) % N_Z, c if cr == 0 else 1 - c) * BLOCK
-        for cr in range(2)
-        for k in range(N_Z)
-        for yr in range(2)
-    ]
-    flags = [z, rank != failed[section], 0, y, c, rank == failed[after], rank == failed[before]]
-    at = jnp.stack([jnp.asarray(v, jnp.int32) for v in offsets + flags])
+    who = jnp.where(jnp.arange(2) == 0, rank, section).astype(jnp.int32)
+    i = jnp.arange(34)
+    i_y, i_z, i_c = i % 2, i // 2 % N_Z, i // 16
+    spots = place(y ^ i_y, (z + i_z) % N_Z, c ^ i_c) * BLOCK
+    kept = (rank != failed[section]).astype(jnp.int32)
+    at = jnp.where(i < 32, spots, jnp.where(i == 32, z, kept)).astype(jnp.int32)
     smem = pl.BlockSpec(memory_space=pltpu.SMEM)
     vmem = pl.BlockSpec(memory_space=pltpu.VMEM)
     whole = jax.ShapeDtypeStruct((count, width), BF16)
+    quick = pl.CostEstimate(flops=2**18, bytes_accessed=2**20, transcendentals=0)
     params = pltpu.CompilerParams(vmem_limit_bytes=28 * 2**20)
     step = 1024
     block = pl.BlockSpec((count, step), lambda i: (0, i))
@@ -260,12 +270,10 @@
         in_specs=[smem] * 3 + [block] * 2,
         out_specs=[block] * 2,
         scratch_shapes=[pltpu.VMEM((2, 2, count, count), BF16)],
-        compiler_params=params,
-        cost_estimate=pl.CostEstimate(
-            flops=4 * count * width * count, bytes_accessed=8 * 2**20, transcendentals=0
-        ),
+        compiler_params=pltpu.CompilerParams(vmem_limit_bytes=60 * 2**20),
+        cost_estimate=pl.CostEstimate(flops=0, bytes_accessed=1024, transcendentals=0),
         name="picks",
-    )(at, route[after], route[before], here_x, here_g)
+    )(who, failed, route, here_x, here_g)
     crossed = over_dp(moved[1], TO_CORE)
     stat = jax.ShapeDtypeStruct((count, 128), F32)
     free = pl.BlockSpec(memory_space=pl.ANY)
@@ -276,31 +284,40 @@
         out_specs=vmem,
         compiler_params=params,
         cost_estimate=pl.CostEstimate(
-            flops=2 * count * width, bytes_accessed=40 * 2**20, transcendentals=0
+            flops=2 * count * width, bytes_accessed=50331648, transcendentals=0
         ),
         name="scale",
     )(inbound, upstream)
-    rows = pl.pallas_call(
+    shard = jnp.concatenate([section_down_weight, section_up_weight], axis=0)
+    chunk = (2, 2, depth, BLOCK)
+    both = pl.pallas_call(
+        both_kernel,
+        out_shape=jax.ShapeDtypeStruct(chunk, BF16),
+        in_specs=[free, vmem, vmem],
+        out_specs=vmem,
+        compiler_params=params,
+        cost_estimate=quick,
+        name="both",
+    )(moved[0], shard, over_dp(shard, TO_Y))
+    mine = lax.all_gather(both, "dp", axis=0, axis_index_groups=Z_GROUPS, tiled=False)
+    weights = [mine, over_dp(mine, TO_CORE)]
+
+    added = pl.pallas_call(
         add_kernel,
         grid=(4,),
         out_shape=whole,
-        in_specs=[free] + [pl.BlockSpec((count // 4, width), lambda i: (i, 0))] * 2,
+        in_specs=[pl.BlockSpec((count // 4, width), lambda i: (i, 0))] * 2,
         out_specs=pl.BlockSpec((count // 4, width), lambda i: (i, 0)),
         compiler_params=params,
         cost_estimate=pl.CostEstimate(
-            flops=count * width, bytes_accessed=6 * 2**20, transcendentals=0
+            flops=count * width, bytes_accessed=1024, transcendentals=0
         ),
         name="add",
-    )(inv, moved[0], crossed)
+    )(moved[0], crossed)
     rows = lax.psum_scatter(
-        rows, "dp", scatter_dimension=0, axis_index_groups=Z_GROUPS, tiled=True
+        added, "dp", scatter_dimension=0, axis_index_groups=Z_GROUPS, tiled=True
     )
 
-    shard = jnp.concatenate([section_down_weight, section_up_weight], axis=0)
-    chunk = (2, 2, depth, BLOCK)
-    both = jnp.stack([shard, over_dp(shard, TO_Y)], axis=0)
-    mine = lax.all_gather(both, "dp", axis=0, axis_index_groups=Z_GROUPS, tiled=False)
-    weights = [mine, over_dp(mine, TO_CORE)]
 
     small = jax.ShapeDtypeStruct((count, depth), BF16)
     keep, first, second, low, back, dots = pl.pallas_call(
@@ -313,7 +330,7 @@
             small,
             stat,
         ],
-        in_specs=[smem] + [vmem] * 6,
+        in_specs=[free, smem] + [vmem] * 6,
         out_specs=[vmem] * 6,
         scratch_shapes=[pltpu.VMEM((32, count, BLOCK), BF16)],
         compiler_params=params,
@@ -321,8 +338,8 @@
             flops=8 * count * width * depth, bytes_accessed=16 * 2**20, transcendentals=0
         ),
         name="terms",
-    )(at, inbound, upstream, gain, *weights, inv)
-    first, second = over_dp(first, TO_CORE), over_dp(second, TO_CORE)
+    )(added, at, inbound, upstream, gain, *weights, inv)
+    first = over_dp(first, TO_CORE)
 
     def slot(i):
         return pl.BlockSpec((1, *chunk), lambda j: (i, 0, 0, 0, 0))
@@ -332,7 +349,6 @@
 
     half = jax.ShapeDtypeStruct((1, *chunk[1:]), BF16)
     full = jax.ShapeDtypeStruct(chunk, BF16)
-    quick = pl.CostEstimate(flops=2**18, bytes_accessed=2**20, transcendentals=0)
     up, down = pl.pallas_call(
         open_kernel,
         grid=(1,),
@@ -343,6 +359,17 @@
         cost_estimate=quick,
         name="open",
     )(keep, first)
+
+    second = pl.pallas_call(
+        later_kernel,
+        out_shape=jax.ShapeDtypeStruct(second.shape, BF16),
+        in_specs=[free, vmem],
+        out_specs=vmem,
+        compiler_params=params,
+        cost_estimate=quick,
+        name="later",
+    )(up, second)
+    second = over_dp(second, TO_CORE)
 
     def fold(token, i, crossed, j, up, down):
         return pl.pallas_call(
@@ -356,25 +383,33 @@
             name="fold",
         )(token, keep, keep, crossed, crossed, up, down)
 
-    forward_out, backward_out = pl.pallas_call(
+    up, down = over_dp(up, TO_UP), over_dp(down, TO_DOWN)
+    up, down = fold(inv, 1, first, 1, up, down)
+    forward_out, backward_out, mark = pl.pallas_call(
         outputs_kernel,
-        out_shape=[whole, whole],
+        out_shape=[whole, whole, jax.ShapeDtypeStruct((8, 128), F32)],
         in_specs=[free, smem] + [vmem] * 9,
-        out_specs=[vmem] * 2,
+        out_specs=[vmem] * 3,
         compiler_params=params,
         cost_estimate=pl.CostEstimate(
             flops=4 * count * width * depth, bytes_accessed=14 * 2**20, transcendentals=0
         ),
         name="outputs",
-    )(first, at, inbound, upstream, gain, *weights, low, back, inv, dots)
+    )(up, at, inbound, upstream, gain, *weights, low, back, inv, dots)
 
     up, down = over_dp(up, TO_UP), over_dp(down, TO_DOWN)
-    up, down = fold(forward_out, 1, first, 1, up, down)
+    up, down = fold(mark, 3, second, 0, up, down)
     up, down = over_dp(up, TO_UP), over_dp(down, TO_DOWN)
-    up, down = fold(up, 3, second, 0, up, down)
-    up, down = over_dp(up, TO_UP), over_dp(down, TO_DOWN)
-    up, down = fold(up, 5, second, 2, up, down)
-    rows = rows + up[0, 0, :1, :1] * 0
+    up, down = fold(inv, 5, second, 2, up, down)
+    rows = pl.pallas_call(
+        later_kernel,
+        out_shape=jax.ShapeDtypeStruct(rows.shape, BF16),
+        in_specs=[free, vmem],
+        out_specs=vmem,
+        compiler_params=params,
+        cost_estimate=quick,
+        name="wait",
+    )(up, rows)
     extras = []
     for i, distance in ((0, 1), (1, -1)):
         near = over_both(rows[i * share : (i + 1) * share], distance, 0)
@@ -388,12 +423,12 @@
             jax.ShapeDtypeStruct(chunk[1:], F32),
             jax.ShapeDtypeStruct(chunk[1:], BF16),
         ],
-        in_specs=[slot(7), slot(4)] + [all_of(chunk)] * 2,
+        in_specs=[free, free, slot(7), slot(4)] + [all_of(chunk)] * 2,
         out_specs=[all_of(chunk[1:])] * 2,
         compiler_params=params,
         cost_estimate=quick,
         name="close",
-    )(keep, second, up, down)
+    )(extras[0], extras[1], keep, second, up, down)
     other = over_dp(other, TO_Y)
     thin = jax.ShapeDtypeStruct((16, width), BF16)
     rerouted_f, rerouted_b = pl.pallas_call(

time: 162 us -> 157 us (0.969)
  Pallas kernels: 20.3 us -> 29.3 us
  local copies, waits for them, and re-layouts: 19.3 us -> 11 us
  starting transfers between devices: 30.4 us -> 26.1 us
  between operations: 16.7 us -> 14.9 us
    all_gather x1, waiting for transfers between devices: 0.02 us -> 39.9 us  [body(): lax.all_gather(both, 'dp', axis=0, axis_index_groups=Z_GROUPS, tiled=False)]
    ppermute x2, waiting for transfers between devices: 35.9 us -> 1.38 us  [over_section(): lax.ppermute(block, 'section', [(i, (i + distance) % n) for i in range(n)])]
    ppermute x14, waiting for transfers between devices: 31.1 us -> 24.3 us  [over_dp(): return lax.ppermute(block, 'dp', pairs)]
    unnamed x31 -> x19, local copies, waits for them, and re-layouts: 14.7 us -> 8.75 us
    pallas_call x2 -> x5, Pallas kernels: 6 us -> 11 us  [the longest x1 6.36 us: body(): pl.pallas_call(outputs_kernel, out_shape=[whole, whole, jax.ShapeDtypeStr...]
    pallas_call x1, Pallas kernels: 4.77 us -> 7.8 us  [body(): pl.pallas_call(picks_kernel, grid=(width // step,), out_shape=[whole, who...]
    ppermute x4, waiting for transfers between devices: 5.78 us -> 8.53 us  [over_both(): return lax.ppermute(block, ('section', 'dp'), pairs)]
    ppermute x14, starting transfers between devices: 21.6 us -> 19.4 us  [over_dp(): return lax.ppermute(block, 'dp', pairs)]
  transfers between devices with their start and end apart: 22 -> 22, of which waited for: 12 -> 12; matrix products, arithmetic and copies ran while one was open for 3% -> 1% of each run, Pallas kernels for 12% -> 18%
where the time goes in v3:
time: 157 us; the launch traced here: 156 us
  waiting for transfers between devices  74.2 us (47%)
  Pallas kernels  29.3 us (19%)
  starting transfers between devices  26.1 us (17%)
  between operations  14.9 us (9%)
  local copies, waits for them, and re-layouts  11 us (7%)
    all_gather x1, waiting for transfers between devices, body(): lax.all_gather(both, 'dp', axis=0, axis_index_groups=Z_GROUPS, tiled=False)  39.9 us
    ppermute x14, waiting for transfers between devices, over_dp(): return lax.ppermute(block, 'dp', pairs)  24.3 us
    ppermute x14, starting transfers between devices, over_dp(): return lax.ppermute(block, 'dp', pairs)  19.4 us
    unnamed x19, local copies, waits for them, and re-layouts  8.75 us
    ppermute x4, waiting for transfers between devices, over_both(): return lax.ppermute(block, ('section', 'dp'), pairs)  8.53 us
    pallas_call x1, Pallas kernels, body(): pl.pallas_call(picks_kernel, grid=(width // step,), out_shape=[whole, who...  7.8 us
    pallas_call x1, Pallas kernels, body(): pl.pallas_call(outputs_kernel, out_shape=[whole, whole, jax.ShapeDtypeStr...  6.36 us
    pallas_call x1, Pallas kernels, body(): pl.pallas_call(terms_kernel, out_shape=[jax.ShapeDtypeStruct((N_Z, *chunk...  4.86 us
  transfers between devices with their start and end apart: 22, of which 12 were waited for; matrix products, arithmetic and copies ran while one was open for 1% of the time, Pallas kernels for 18%

profile of v3, /device:TPU:6, one launch (start us, length us, event | category | flops | bytes accessed | tf_op | source)
XLA Modules:
  0.0 156.1 jit_solution(18361112477139160910)
XLA Ops:
  7.2 0.8 constant_dynamic-update-slice_fusion.1
  8.9 3.2 %collective-permute-start.3 = (bf16[2,128,256]{2,1,0:T(8,128)(2,1)S(1)}, bf16[2,128,256]{2,1,0:T(8,128)(2,1)S(1)}, u32[]{:S(2)}, u32[]{:S(2)}) collective-permute-start(bf16[2,128,256]{2,1,0:T(8,128)(2,1)S(1)} %constant_dynamic-update-slice_fusion.mine), channel_id=1, source_target_pairs={{0,16},{1,17},{2,18},{3,19},{4,20},{5,21},{6,22},{7,23},{8,24},{9,... | collective-permute-start | bytes 393224 | tf_op jit(solution)/shard_map/ppermute | solution.py:29
  12.6 7.8 %picks.1 = (bf16[128,8192]{1,0:T(8,128)(2,1)}, bf16[128,8192]{1,0:T(8,128)(2,1)}) custom-call(s32[2]{0:T(128)} %compare_select_fusion.6.who, s32[8]{0:T(128)} %failed.1, s32[8,32]{1,0:T(8,128)} %route.1, bf16[128,8192]{1,0:T(8,128)(2,1)} %bitcast.19, bf16[128,8192]{1,0:T(8,128)(2,1)} %bitcast.20), custom_call_target="tpu_custom_call" | custom-call | bytes 1024 | tf_op jit(solution)/shard_map/picks/pallas_call | solution.py:266
  20.4 1.6 %copy-done.4 = bf16[128,8192]{1,0:T(8,128)(2,1)S(1)} copy-done((bf16[128,8192]{1,0:T(8,128)(2,1)S(1)}, bf16[128,8192]{1,0:T(8,128)(2,1)}, u32[]{:S(2)}) %copy-start.4) | copy-done | bytes 2097176
  23.6 1.4 collective-permute-start.1
  25.0 39.9 %all-gather.3.cloned.1.call-done = bf16[16,2,128,256]{3,2,1,0:T(8,128)(2,1)} async-done(((bf16[2,2,128,256]{3,2,1,0:T(8,128)(2,1)}), bf16[16,2,128,256]{3,2,1,0:T(8,128)(2,1)}) %all-gather.3.cloned.1.call-update) | async-done | bytes 2097168 | tf_op jit(solution)/shard_map/all_gather | solution.py:302
  64.9 1.6 %copy-done.5 = bf16[128,8192]{1,0:T(8,128)(2,1)S(1)} copy-done((bf16[128,8192]{1,0:T(8,128)(2,1)S(1)}, bf16[128,8192]{1,0:T(8,128)(2,1)}, u32[]{:S(2)}) %copy-start.5) | copy-done | bytes 2097176
  66.5 3.8 %add.111.token = bf16[128,8192]{1,0:T(8,128)(2,1)} custom-call(bf16[128,8192]{1,0:T(8,128)(2,1)S(1)} %copy-done.5, bf16[128,8192]{1,0:T(8,128)(2,1)} %collective-permute-done.2.b_ref), custom_call_target="tpu_custom_call" | custom-call | flops 1048576 | bytes 1024 | tf_op jit(solution)/shard_map/add/pallas_call | solution.py:305
  72.3 1.4 collective-permute-done.1
  74.3 1.0 copy-done.2
  75.3 4.9 %terms.1 = (f32[8,2,2,128,256]{4,3,2,1,0:T(8,128)S(1)}, bf16[3,2,2,128,256]{4,3,2,1,0:T(8,128)(2,1)S(1)}, bf16[5,2,2,128,256]{4,3,2,1,0:T(8,128)(2,1)S(1)}, bf16...) custom-call(bf16[128,8192]{1,0:T(8,128)(2,1)} %add.111.token, ...), custom_call_target="tpu_custom_call" | custom-call | flops 1073741824 | bytes 16777216 | tf_op jit(solution)/shard_map/terms/pallas_call | solution.py:323
  80.3 2.3 %collective-permute-done.5.crossed.cross_up.cross_down = bf16[3,2,2,128,256]{4,3,2,1,0:T(8,128)(2,1)S(1)} collective-permute-done((bf16[3,2,2,128,256]{4,3,2,1,0:T(8,128)(2,1)S(1)}, bf16[3,2,2,128,256]{4,3,2,1,0:T(8,128)(2,1)S(1)}, u32[]{:S(2)}, u32[]{:S(2)}) %collective-permute-start.5) | collective-permute-done | bytes 786464 | tf_op jit(solution)/shard_map/ppermute | solution.py:29
  82.9 5.9 %collective-permute-start.7 = (bf16[1,2,128,256]{3,2,1,0:T(8,128)(2,1)S(1)}, bf16[1,2,128,256]{3,2,1,0:T(8,128)(2,1)S(1)}, u32[]{:S(2)}, u32[]{:S(2)}) collective-permute-start(bf16[1,2,128,256]{3,2,1,0:T(8,128)(2,1)S(1)} %get-tuple-element.36), channel_id=1, source_target_pairs={{0,14},{1,15},{2,0},{3,1},{4,2},{5,3},{6,4},{7,5},{8,6},{9,7},{10,... | collective-permute-start | bytes 393224 | tf_op jit(solution)/shard_map/ppermute | solution.py:29
  88.8 6.2 %collective-permute-done.7.got_down = bf16[1,2,128,256]{3,2,1,0:T(8,128)(2,1)S(1)} collective-permute-done((bf16[1,2,128,256]{3,2,1,0:T(8,128)(2,1)S(1)}, bf16[1,2,128,256]{3,2,1,0:T(8,128)(2,1)S(1)}, u32[]{:S(2)}, u32[]{:S(2)}) %collective-permute-start.7) | collective-permute-done | bytes 131104 | tf_op jit(solution)/shard_map/ppermute | solution.py:29
  95.0 3.5 %collective-permute-done.6.got_up = bf16[1,2,128,256]{3,2,1,0:T(8,128)(2,1)S(1)} collective-permute-done((bf16[1,2,128,256]{3,2,1,0:T(8,128)(2,1)S(1)}, bf16[1,2,128,256]{3,2,1,0:T(8,128)(2,1)S(1)}, u32[]{:S(2)}, u32[]{:S(2)}) %collective-permute-start.6) | collective-permute-done | bytes 131104 | tf_op jit(solution)/shard_map/ppermute | solution.py:29
  98.9 1.9 %collective-permute-start.9 = (bf16[2,2,128,256]{3,2,1,0:T(8,128)(2,1)S(1)}, bf16[2,2,128,256]{3,2,1,0:T(8,128)(2,1)S(1)}, u32[]{:S(2)}, u32[]{:S(2)}) collective-permute-start(bf16[2,2,128,256]{3,2,1,0:T(8,128)(2,1)S(1)} %get-tuple-element.37.token), channel_id=1, source_target_pairs={{0,2},{1,3},{2,4},{3,5},{4,6},{5,7},{6,8},{7,9},{8,10},{9,11},{10,... | collective-permute-start | bytes 786440 | tf_op jit(solution)/shard_map/ppermute | solution.py:29
  100.7 6.4 %outputs.1 = (bf16[128,8192]{1,0:T(8,128)(2,1)}, bf16[128,8192]{1,0:T(8,128)(2,1)}, f32[8,128]{1,0:T(8,128)S(1)}) custom-call(bf16[2,2,128,256]{3,2,1,0:T(8,128)(2,1)S(1)} %get-tuple-element.37.token, s32[34]{0:T(128)S(1)} %compare_select_fusion.5.at, bf16[128,8192]{1,0:T(8,128)(2,1)S(1)} %bitcast.14, bf16[128,8192]{1,0:T(8,128)(2,1)} %bitcast.1.g_ref, ...), custom_call_target="tpu_custom_call" | custom-call | flops 536870912 | bytes 14680064 | tf_op jit(solution)/shard_map/outputs/pallas_call | solution.py:388
  107.1 5.3 %collective-permute-done.10.got_down = bf16[2,2,128,256]{3,2,1,0:T(8,128)(2,1)S(1)} collective-permute-done((bf16[2,2,128,256]{3,2,1,0:T(8,128)(2,1)S(1)}, bf16[2,2,128,256]{3,2,1,0:T(8,128)(2,1)S(1)}, u32[]{:S(2)}, u32[]{:S(2)}) %collective-permute-start.10) | collective-permute-done | bytes 262176 | tf_op jit(solution)/shard_map/ppermute | solution.py:29
  112.3 1.0 collective-permute-done.9.got_up
  114.2 2.6 %collective-permute-start.12 = (bf16[2,2,128,256]{3,2,1,0:T(8,128)(2,1)S(1)}, bf16[2,2,128,256]{3,2,1,0:T(8,128)(2,1)S(1)}, u32[]{:S(2)}, u32[]{:S(2)}) collective-permute-start(bf16[2,2,128,256]{3,2,1,0:T(8,128)(2,1)S(1)} %get-tuple-element.47), channel_id=1, source_target_pairs={{0,14},{1,15},{2,0},{3,1},{4,2},{5,3},{6,4},{7,5},{8,6},{9,7},{10,... | collective-permute-start | bytes 786440 | tf_op jit(solution)/shard_map/ppermute | solution.py:29
  116.8 5.4 %collective-permute-done.11.got_up = bf16[2,2,128,256]{3,2,1,0:T(8,128)(2,1)S(1)} collective-permute-done((bf16[2,2,128,256]{3,2,1,0:T(8,128)(2,1)S(1)}, bf16[2,2,128,256]{3,2,1,0:T(8,128)(2,1)S(1)}, u32[]{:S(2)}, u32[]{:S(2)}) %collective-permute-start.11) | collective-permute-done | bytes 262176 | tf_op jit(solution)/shard_map/ppermute | solution.py:29
  122.4 3.0 %collective-permute-start.18 = (bf16[2,2,128,256]{3,2,1,0:T(8,128)(2,1)S(1)}, bf16[2,2,128,256]{3,2,1,0:T(8,128)(2,1)S(1)}, u32[]{:S(2)}, u32[]{:S(2)}) collective-permute-start(bf16[2,2,128,256]{3,2,1,0:T(8,128)(2,1)S(1)} %get-tuple-element.49), channel_id=1, source_target_pairs={{0,14},{1,15},{2,0},{3,1},{4,2},{5,3},{6,4},{7,5},{8,6},{9,7},{10,... | collective-permute-start | bytes 786440 | tf_op jit(solution)/shard_map/ppermute | solution.py:29
  125.4 0.9 copy-done.7
  126.5 0.8 collective-permute-start.14
  127.3 1.3 collective-permute-start.13
  128.6 2.4 %collective-permute-start.16 = (bf16[4,8192]{1,0:T(4,128)(2,1)S(1)}, bf16[4,8192]{1,0:T(4,128)(2,1)S(1)}, u32[]{:S(2)}, u32[]{:S(2)}) collective-permute-start(bf16[4,8192]{1,0:T(4,128)(2,1)S(1)} %get-tuple-element.56), channel_id=1, source_target_pairs={{0,240},{1,241},{2,242},{3,243},{4,244},{5,245},{6,246},{7,247},{8... | collective-permute-start | bytes 196616 | tf_op jit(solution)/shard_map/ppermute | solution.py:44
  131.0 2.2 %collective-permute-done.14 = bf16[4,8192]{1,0:T(4,128)(2,1)S(1)} collective-permute-done((bf16[4,8192]{1,0:T(4,128)(2,1)S(1)}, bf16[4,8192]{1,0:T(4,128)(2,1)S(1)}, u32[]{:S(2)}, u32[]{:S(2)}) %collective-permute-start.14) | collective-permute-done | bytes 65568 | tf_op jit(solution)/shard_map/ppermute | solution.py:44
  133.3 2.9 %collective-permute-done.16 = bf16[4,8192]{1,0:T(4,128)(2,1)S(1)} collective-permute-done((bf16[4,8192]{1,0:T(4,128)(2,1)S(1)}, bf16[4,8192]{1,0:T(4,128)(2,1)S(1)}, u32[]{:S(2)}, u32[]{:S(2)}) %collective-permute-start.16) | collective-permute-done | bytes 65568 | tf_op jit(solution)/shard_map/ppermute | solution.py:44
  136.2 3.4 %collective-permute-done.15 = bf16[4,8192]{1,0:T(4,128)(2,1)S(1)} collective-permute-done((bf16[4,8192]{1,0:T(4,128)(2,1)S(1)}, bf16[4,8192]{1,0:T(4,128)(2,1)S(1)}, u32[]{:S(2)}, u32[]{:S(2)}) %collective-permute-start.15) | collective-permute-done | bytes 65568 | tf_op jit(solution)/shard_map/ppermute | solution.py:44
  139.7 2.2 %copy-done.1 = f32[8,2,2,128,256]{4,3,2,1,0:T(8,128)S(1)} copy-done((f32[8,2,2,128,256]{4,3,2,1,0:T(8,128)S(1)}, f32[8,2,2,128,256]{4,3,2,1,0:T(8,128)}, u32[]{:S(2)}) %copy-start.1) | copy-done | bytes 4194328
  142.0 1.5 collective-permute-start.19
  143.5 3.7 %extras.1 = (bf16[16,8192]{1,0:T(8,128)(2,1)S(1)}, bf16[16,8192]{1,0:T(8,128)(2,1)S(1)}) custom-call(f32[2,128,256]{2,1,0:T(8,128)S(1)} %get-tuple-element.50.token.own, s32[34]{0:T(128)S(1)} %compare_select_fusion.5.at, bf16[16,8192]{1,0:T(8,128)(2,1)S(1)} %pad.7.token_1.x_ref, bf16[16,8192]{1,0:T(8,128)(2,1)S(1)} %pad.8.token_2.g_ref, ...), custom_call_target="tpu_custom_call" | custom-call | flops 134217728 | bytes 6291456 | tf_op jit(solution)/shard_map/extras/pallas_call | solution.py:434
  (58 shorter events, 9.1 us)
Async XLA Ops:
  7.2 57.8 %all-gather.3.cloned.1.call-start = ((), (), s32[]{:S(2)}) async-start(), calls=%async_computation.2 | async-start | bytes 2359296 | tf_op jit(solution)/shard_map/all_gather | solution.py:302
  8.9 11.5 %collective-permute-start.3 = (bf16[2,128,256]{2,1,0:T(8,128)(2,1)S(1)}, bf16[2,128,256]{2,1,0:T(8,128)(2,1)S(1)}, u32[]{:S(2)}, u32[]{:S(2)}) collective-permute-start(bf16[2,128,256]{2,1,0:T(8,128)(2,1)S(1)} %constant_dynamic-update-slice_fusion.mine), channel_id=1, source_target_pairs={{0,16},{1,17},{2,18},{3,19},{4,20},{5,21},{6,22},{7,23},{8,24},{9,... | collective-permute-start | bytes 393224 | tf_op jit(solution)/shard_map/ppermute | solution.py:29
  20.4 1.6 %copy-start.4 = (bf16[128,8192]{1,0:T(8,128)(2,1)S(1)}, bf16[128,8192]{1,0:T(8,128)(2,1)}, u32[]{:S(2)}) copy-start(bf16[128,8192]{1,0:T(8,128)(2,1)} %get-tuple-element.31.a_ref.token) | copy-start | bytes 6291460
  22.8 102.6 %reduce-scatter.2.cloned.1.call-start = ((), (), s32[]{:S(2)}) async-start(), calls=%async_computation.1 | async-start | bytes 2359296 | tf_op jit(solution)/shard_map/reduce_scatter | solution.py:317
  22.8 42.1 %collective-permute-start.2 = (bf16[128,8192]{1,0:T(8,128)(2,1)}, bf16[128,8192]{1,0:T(8,128)(2,1)}, u32[]{:S(2)}, u32[]{:S(2)}) collective-permute-start(bf16[128,8192]{1,0:T(8,128)(2,1)} %get-tuple-element.32), channel_id=1, source_target_pairs={{0,1},{1,0},{2,3},{3,2},{4,5},{5,4},{6,7},{7,6},{8,9},{9,8},{10,11... | collective-permute-start | bytes 6291464 | tf_op jit(solution)/shard_map/ppermute | solution.py:29
  22.9 49.4 %collective-permute-start = (bf16[1,1,128,8192]{3,2,1,0:T(8,128)(2,1)}, bf16[1,1,128,8192]{3,2,1,0:T(8,128)(2,1)S(1)}, u32[]{:S(2)}, u32[]{:S(2)}) collective-permute-start(bf16[1,1,128,8192]{3,2,1,0:T(8,128)(2,1)} %param.7), channel_id=1, source_target_pairs={{0,32},{32,64},{64,96},{96,128},{128,160},{160,192},{192,224},{224... | collective-permute-start | bytes 6291464 | tf_op jit(solution)/shard_map/ppermute | solution.py:34
  23.6 50.1 %collective-permute-start.1 = (bf16[1,1,128,8192]{3,2,1,0:T(8,128)(2,1)}, bf16[1,1,128,8192]{3,2,1,0:T(8,128)(2,1)}, u32[]{:S(2)}, u32[]{:S(2)}) collective-permute-start(bf16[1,1,128,8192]{3,2,1,0:T(8,128)(2,1)} %param.8), channel_id=1, source_target_pairs={{0,224},{32,0},{64,32},{96,64},{128,96},{160,128},{192,160},{224,1... | collective-permute-start | bytes 6291464 | tf_op jit(solution)/shard_map/ppermute | solution.py:34
  64.9 9.4 %collective-permute-start.4 = (bf16[8,2,2,128,256]{4,3,2,1,0:T(8,128)(2,1)}, bf16[8,2,2,128,256]{4,3,2,1,0:T(8,128)(2,1)}, u32[]{:S(2)}, u32[]{:S(2)}) collective-permute-start(bf16[8,2,2,128,256]{4,3,2,1,0:T(8,128)(2,1)} %bitcast.15), channel_id=1, source_target_pairs={{0,1},{1,0},{2,3},{3,2},{4,5},{5,4},{6,7},{7,6},{8,9},{9,8},{10,11... | collective-permute-start | bytes 6291464 | tf_op jit(solution)/shard_map/ppermute | solution.py:29
  64.9 1.6 %copy-start.5 = (bf16[128,8192]{1,0:T(8,128)(2,1)S(1)}, bf16[128,8192]{1,0:T(8,128)(2,1)}, u32[]{:S(2)}) copy-start(bf16[128,8192]{1,0:T(8,128)(2,1)} %get-tuple-element.31.a_ref.token) | copy-start | bytes 6291460
  70.4 0.7 copy-start.8
  73.7 1.6 %copy-start.2 = (bf16[16,2,128,256]{3,2,1,0:T(8,128)(2,1)S(1)}, bf16[16,2,128,256]{3,2,1,0:T(8,128)(2,1)}, u32[]{:S(2)}) copy-start(bf16[16,2,128,256]{3,2,1,0:T(8,128)(2,1)} %all-gather.3.cloned.1.call-done) | copy-start | bytes 6291460
  73.7 1.6 %copy-start.6 = (f32[1,8192]{1,0:T(1,128)S(1)}, f32[1,8192]{1,0:T(1,128)}, u32[]{:S(2)}) copy-start(f32[1,8192]{1,0:T(1,128)} %gain_ref.5) | copy-start | bytes 98308
  80.2 42.0 %copy-start = (f32[8,2,2,128,256]{4,3,2,1,0:T(8,128)}, f32[8,2,2,128,256]{4,3,2,1,0:T(8,128)S(1)}, u32[]{:S(2)}) copy-start(f32[8,2,2,128,256]{4,3,2,1,0:T(8,128)S(1)} %get-tuple-element.33.keep.keep_up.keep_down) | copy-start | bytes 12582916
  80.2 2.4 %collective-permute-start.5 = (bf16[3,2,2,128,256]{4,3,2,1,0:T(8,128)(2,1)S(1)}, bf16[3,2,2,128,256]{4,3,2,1,0:T(8,128)(2,1)S(1)}, u32[]{:S(2)}, u32[]{:S(2)}) collective-permute-start(bf16[3,2,2,128,256]{4,3,2,1,0:T(8,128)(2,1)S(1)} %get-tuple-element.34), channel_id=1, source_target_pairs={{0,1},{1,0},{2,3},{3,2},{4,5},{5,4},{6,7},{7,6},{8,9},{9,8},{10,11... | collective-permute-start | bytes 2359304 | tf_op jit(solution)/shard_map/ppermute | solution.py:29
  82.7 30.6 %collective-permute-start.8 = (bf16[5,2,2,128,256]{4,3,2,1,0:T(8,128)(2,1)S(1)}, bf16[5,2,2,128,256]{4,3,2,1,0:T(8,128)(2,1)S(1)}, u32[]{:S(2)}, u32[]{:S(2)}) collective-permute-start(bf16[5,2,2,128,256]{4,3,2,1,0:T(8,128)(2,1)S(1)} %later.1), channel_id=1, source_target_pairs={{0,1},{1,0},{2,3},{3,2},{4,5},{5,4},{6,7},{7,6},{8,9},{9,8},{10,11... | collective-permute-start | bytes 3932168 | tf_op jit(solution)/shard_map/ppermute | solution.py:29
  82.9 12.1 %collective-permute-start.7 = (bf16[1,2,128,256]{3,2,1,0:T(8,128)(2,1)S(1)}, bf16[1,2,128,256]{3,2,1,0:T(8,128)(2,1)S(1)}, u32[]{:S(2)}, u32[]{:S(2)}) collective-permute-start(bf16[1,2,128,256]{3,2,1,0:T(8,128)(2,1)S(1)} %get-tuple-element.36), channel_id=1, source_target_pairs={{0,14},{1,15},{2,0},{3,1},{4,2},{5,3},{6,4},{7,5},{8,6},{9,7},{10,... | collective-permute-start | bytes 393224 | tf_op jit(solution)/shard_map/ppermute | solution.py:29
  88.8 9.7 %collective-permute-start.6 = (bf16[1,2,128,256]{3,2,1,0:T(8,128)(2,1)S(1)}, bf16[1,2,128,256]{3,2,1,0:T(8,128)(2,1)S(1)}, u32[]{:S(2)}, u32[]{:S(2)}) collective-permute-start(bf16[1,2,128,256]{3,2,1,0:T(8,128)(2,1)S(1)} %get-tuple-element.35.token), channel_id=1, source_target_pairs={{0,2},{1,3},{2,4},{3,5},{4,6},{5,7},{6,8},{7,9},{8,10},{9,11},{10,... | collective-permute-start | bytes 393224 | tf_op jit(solution)/shard_map/ppermute | solution.py:29
  98.6 13.7 %collective-permute-start.10 = (bf16[2,2,128,256]{3,2,1,0:T(8,128)(2,1)S(1)}, bf16[2,2,128,256]{3,2,1,0:T(8,128)(2,1)S(1)}, u32[]{:S(2)}, u32[]{:S(2)}) collective-permute-start(bf16[2,2,128,256]{3,2,1,0:T(8,128)(2,1)S(1)} %get-tuple-element.45), channel_id=1, source_target_pairs={{0,14},{1,15},{2,0},{3,1},{4,2},{5,3},{6,4},{7,5},{8,6},{9,7},{10,... | collective-permute-start | bytes 786440 | tf_op jit(solution)/shard_map/ppermute | solution.py:29
  98.9 14.4 %collective-permute-start.9 = (bf16[2,2,128,256]{3,2,1,0:T(8,128)(2,1)S(1)}, bf16[2,2,128,256]{3,2,1,0:T(8,128)(2,1)S(1)}, u32[]{:S(2)}, u32[]{:S(2)}) collective-permute-start(bf16[2,2,128,256]{3,2,1,0:T(8,128)(2,1)S(1)} %get-tuple-element.37.token), channel_id=1, source_target_pairs={{0,2},{1,3},{2,4},{3,5},{4,6},{5,7},{6,8},{7,9},{8,10},{9,11},{10,... | collective-permute-start | bytes 786440 | tf_op jit(solution)/shard_map/ppermute | solution.py:29
  113.5 8.7 %collective-permute-start.11 = (bf16[2,2,128,256]{3,2,1,0:T(8,128)(2,1)S(1)}, bf16[2,2,128,256]{3,2,1,0:T(8,128)(2,1)S(1)}, u32[]{:S(2)}, u32[]{:S(2)}) collective-permute-start(bf16[2,2,128,256]{3,2,1,0:T(8,128)(2,1)S(1)} %get-tuple-element.46), channel_id=1, source_target_pairs={{0,2},{1,3},{2,4},{3,5},{4,6},{5,7},{6,8},{7,9},{8,10},{9,11},{10,... | collective-permute-start | bytes 786440 | tf_op jit(solution)/shard_map/ppermute | solution.py:29
  114.2 8.0 %collective-permute-start.12 = (bf16[2,2,128,256]{3,2,1,0:T(8,128)(2,1)S(1)}, bf16[2,2,128,256]{3,2,1,0:T(8,128)(2,1)S(1)}, u32[]{:S(2)}, u32[]{:S(2)}) collective-permute-start(bf16[2,2,128,256]{3,2,1,0:T(8,128)(2,1)S(1)} %get-tuple-element.47), channel_id=1, source_target_pairs={{0,14},{1,15},{2,0},{3,1},{4,2},{5,3},{6,4},{7,5},{8,6},{9,7},{10,... | collective-permute-start | bytes 786440 | tf_op jit(solution)/shard_map/ppermute | solution.py:29
  122.4 17.3 %collective-permute-start.18 = (bf16[2,2,128,256]{3,2,1,0:T(8,128)(2,1)S(1)}, bf16[2,2,128,256]{3,2,1,0:T(8,128)(2,1)S(1)}, u32[]{:S(2)}, u32[]{:S(2)}) collective-permute-start(bf16[2,2,128,256]{3,2,1,0:T(8,128)(2,1)S(1)} %get-tuple-element.49), channel_id=1, source_target_pairs={{0,14},{1,15},{2,0},{3,1},{4,2},{5,3},{6,4},{7,5},{8,6},{9,7},{10,... | collective-permute-start | bytes 786440 | tf_op jit(solution)/shard_map/ppermute | solution.py:29
  125.4 14.3 %collective-permute-start.17 = (bf16[2,2,128,256]{3,2,1,0:T(8,128)(2,1)S(1)}, bf16[2,2,128,256]{3,2,1,0:T(8,128)(2,1)S(1)}, u32[]{:S(2)}, u32[]{:S(2)}) collective-permute-start(bf16[2,2,128,256]{3,2,1,0:T(8,128)(2,1)S(1)} %get-tuple-element.48.token), channel_id=1, source_target_pairs={{0,2},{1,3},{2,4},{3,5},{4,6},{5,7},{6,8},{7,9},{8,10},{9,11},{10,... | collective-permute-start | bytes 786440 | tf_op jit(solution)/shard_map/ppermute | solution.py:29
  125.4 1.0 copy-start.7
  126.5 6.7 %collective-permute-start.14 = (bf16[4,8192]{1,0:T(4,128)(2,1)S(1)}, bf16[4,8192]{1,0:T(4,128)(2,1)S(1)}, u32[]{:S(2)}, u32[]{:S(2)}) collective-permute-start(bf16[4,8192]{1,0:T(4,128)(2,1)S(1)} %get-tuple-element.58), channel_id=1, source_target_pairs={{0,48},{1,49},{2,50},{3,51},{4,52},{5,53},{6,54},{7,55},{8,56},{9,... | collective-permute-start | bytes 196616 | tf_op jit(solution)/shard_map/ppermute | solution.py:44
  127.3 5.9 %collective-permute-start.13 = (bf16[4,8192]{1,0:T(4,128)(2,1)S(1)}, bf16[4,8192]{1,0:T(4,128)(2,1)S(1)}, u32[]{:S(2)}, u32[]{:S(2)}) collective-permute-start(bf16[4,8192]{1,0:T(4,128)(2,1)S(1)} %get-tuple-element.59), channel_id=1, source_target_pairs={{0,32},{1,33},{2,34},{3,35},{4,36},{5,37},{6,38},{7,39},{8,40},{9,... | collective-permute-start | bytes 196616 | tf_op jit(solution)/shard_map/ppermute | solution.py:44
  128.6 7.6 %collective-permute-start.16 = (bf16[4,8192]{1,0:T(4,128)(2,1)S(1)}, bf16[4,8192]{1,0:T(4,128)(2,1)S(1)}, u32[]{:S(2)}, u32[]{:S(2)}) collective-permute-start(bf16[4,8192]{1,0:T(4,128)(2,1)S(1)} %get-tuple-element.56), channel_id=1, source_target_pairs={{0,240},{1,241},{2,242},{3,243},{4,244},{5,245},{6,246},{7,247},{8... | collective-permute-start | bytes 196616 | tf_op jit(solution)/shard_map/ppermute | solution.py:44
  133.2 6.4 %collective-permute-start.15 = (bf16[4,8192]{1,0:T(4,128)(2,1)S(1)}, bf16[4,8192]{1,0:T(4,128)(2,1)S(1)}, u32[]{:S(2)}, u32[]{:S(2)}) collective-permute-start(bf16[4,8192]{1,0:T(4,128)(2,1)S(1)} %get-tuple-element.57), channel_id=1, source_target_pairs={{0,224},{1,225},{2,226},{3,227},{4,228},{5,229},{6,230},{7,231},{8... | collective-permute-start | bytes 196616 | tf_op jit(solution)/shard_map/ppermute | solution.py:44
  139.7 2.2 %copy-start.1 = (f32[8,2,2,128,256]{4,3,2,1,0:T(8,128)S(1)}, f32[8,2,2,128,256]{4,3,2,1,0:T(8,128)}, u32[]{:S(2)}) copy-start(f32[8,2,2,128,256]{4,3,2,1,0:T(8,128)} %copy-done) | copy-start | bytes 12582916
  141.9 1.6 %copy-start.3 = (bf16[16,2,128,256]{3,2,1,0:T(8,128)(2,1)S(1)}, bf16[16,2,128,256]{3,2,1,0:T(8,128)(2,1)}, u32[]{:S(2)}) copy-start(bf16[16,2,128,256]{3,2,1,0:T(8,128)(2,1)} %all-gather.3.cloned.1.call-done) | copy-start | bytes 6291460
  142.0 6.6 %collective-permute-start.19 = (bf16[2,128,256]{2,1,0:T(8,128)(2,1)S(1)}, bf16[2,128,256]{2,1,0:T(8,128)(2,1)S(1)}, u32[]{:S(2)}, u32[]{:S(2)}) collective-permute-start(bf16[2,128,256]{2,1,0:T(8,128)(2,1)S(1)} %get-tuple-element.53), channel_id=1, source_target_pairs={{0,16},{1,17},{2,18},{3,19},{4,20},{5,21},{6,22},{7,23},{8,24},{9,... | collective-permute-start | bytes 393224 | tf_op jit(solution)/shard_map/ppermute | solution.py:29
Sparse Core Ops, SparseCore 0:
  22.9 41.9 all-gather.2
  70.5 45.7 reduce-scatter.1

commit v4 on v3

--- a/solution.py
+++ b/solution.py
@@ -46,6 +46,11 @@
 
 SLOTS = (4, 3, 5, 2, 6, 1, 7, 0)
 N_FIRST = 3
+
+
+def pair_kernel(down, up, out):
+    out[0] = down[0]
+    out[1] = up[0]
 
 
 def both_kernel(token, mine, other, out):
@@ -229,13 +234,14 @@
                     hit_g = (column == route[before, to] * share + line - share) & (line >= share)
                     parts_x.append(jnp.where(hit_x, has_x, 0.0))
                     parts_g.append(jnp.where(hit_g, has_g, 0.0))
-            pick[c_rel, 0] = jnp.concatenate(parts_x, axis=0).astype(BF16)
-            pick[c_rel, 1] = jnp.concatenate(parts_g, axis=0).astype(BF16)
-
-    for c_rel, out_ref in ((0, keep_ref), (1, send_ref)):
-        moved = jnp.dot(pick[c_rel, 0], x_ref[...], preferred_element_type=F32)
-        moved += jnp.dot(pick[c_rel, 1], g_ref[...], preferred_element_type=F32)
-        out_ref[...] = moved.astype(BF16)
+            here = pl.ds(c_rel * count, count)
+            pick[here, :count] = jnp.concatenate(parts_x, axis=0).astype(BF16)
+            pick[here, count:] = jnp.concatenate(parts_g, axis=0).astype(BF16)
+
+    both = jnp.concatenate([x_ref[...], g_ref[...]], axis=0)
+    moved = jnp.dot(pick[...], both, preferred_element_type=F32).astype(BF16)
+    keep_ref[...] = moved[:count]
+    send_ref[...] = moved[count:]
 
 
 def body(arriving, returning, gain, section_down_weight, section_up_weight, failed, route):
@@ -269,7 +275,7 @@
         out_shape=[whole, whole],
         in_specs=[smem] * 3 + [block] * 2,
         out_specs=[block] * 2,
-        scratch_shapes=[pltpu.VMEM((2, 2, count, count), BF16)],
+        scratch_shapes=[pltpu.VMEM((2 * count, 2 * count), BF16)],
         compiler_params=pltpu.CompilerParams(vmem_limit_bytes=60 * 2**20),
         cost_estimate=pl.CostEstimate(flops=0, bytes_accessed=1024, transcendentals=0),
         name="picks",
@@ -288,7 +294,15 @@
         ),
         name="scale",
     )(inbound, upstream)
-    shard = jnp.concatenate([section_down_weight, section_up_weight], axis=0)
+    shard = pl.pallas_call(
+        pair_kernel,
+        out_shape=jax.ShapeDtypeStruct((2, depth, BLOCK), BF16),
+        in_specs=[vmem] * 2,
+        out_specs=vmem,
+        compiler_params=params,
+        cost_estimate=quick,
+        name="pair",
+    )(section_down_weight, section_up_weight)
     chunk = (2, 2, depth, BLOCK)
     both = pl.pallas_call(
         both_kernel,

time: 157 us -> 156 us (level)
    unnamed x19 -> x22, local copies, waits for them, and re-layouts: 8.75 us -> 9.57 us
where the time goes in v4:
time: 156 us
  waiting for transfers between devices  74 us (47%)
  Pallas kernels  29 us (19%)
  starting transfers between devices  26.3 us (17%)
  between operations  14.9 us (10%)
  local copies, waits for them, and re-layouts  11 us (7%)
    all_gather x1, waiting for transfers between devices, body(): lax.all_gather(both, 'dp', axis=0, axis_index_groups=Z_GROUPS, tiled=False)  39.9 us
    ppermute x14, waiting for transfers between devices, over_dp(): return lax.ppermute(block, 'dp', pairs)  24.1 us
    ppermute x14, starting transfers between devices, over_dp(): return lax.ppermute(block, 'dp', pairs)  19.6 us
    unnamed x22, local copies, waits for them, and re-layouts  9.57 us
    ppermute x4, waiting for transfers between devices, over_both(): return lax.ppermute(block, ('section', 'dp'), pairs)  8.53 us
    pallas_call x1, Pallas kernels, body(): pl.pallas_call(picks_kernel, grid=(width // step,), out_shape=[whole, who...  7.54 us
    pallas_call x1, Pallas kernels, body(): pl.pallas_call(outputs_kernel, out_shape=[whole, whole, jax.ShapeDtypeStr...  6.36 us
    pallas_call x1, Pallas kernels, body(): pl.pallas_call(terms_kernel, out_shape=[jax.ShapeDtypeStruct((N_Z, *chunk...  4.87 us
  transfers between devices with their start and end apart: 22, of which 12 were waited for; matrix products, arithmetic and copies ran while one was open for 1% of the time, Pallas kernels for 18%

profile of v4, /device:TPU:6, one launch (start us, length us, event | category | flops | bytes accessed | tf_op | source)
XLA Modules:
  0.0 155.8 jit_solution(13859352659404532407)
XLA Ops:
  8.1 0.8 copy-done.9
  8.9 3.3 %collective-permute-start.3 = (bf16[2,128,256]{2,1,0:T(8,128)(2,1)S(1)}, bf16[2,128,256]{2,1,0:T(8,128)(2,1)S(1)}, u32[]{:S(2)}, u32[]{:S(2)}) collective-permute-start(bf16[2,128,256]{2,1,0:T(8,128)(2,1)S(1)} %pair.1.mine), channel_id=1, source_target_pairs={{0,16},{1,17},{2,18},{3,19},{4,20},{5,21},{6,22},{7,23},{8,24},{9,... | collective-permute-start | bytes 393224 | tf_op jit(solution)/shard_map/ppermute | solution.py:29
  12.7 7.5 %picks.1 = (bf16[128,8192]{1,0:T(8,128)(2,1)}, bf16[128,8192]{1,0:T(8,128)(2,1)}) custom-call(s32[2]{0:T(128)} %compare_select_fusion.6.who, s32[8]{0:T(128)} %failed.1, s32[8,32]{1,0:T(8,128)} %route.1, bf16[128,8192]{1,0:T(8,128)(2,1)} %bitcast.19, bf16[128,8192]{1,0:T(8,128)(2,1)} %bitcast.20), custom_call_target="tpu_custom_call" | custom-call | bytes 1024 | tf_op jit(solution)/shard_map/picks/pallas_call | solution.py:272
  20.2 1.6 %copy-done.4 = bf16[128,8192]{1,0:T(8,128)(2,1)S(1)} copy-done((bf16[128,8192]{1,0:T(8,128)(2,1)S(1)}, bf16[128,8192]{1,0:T(8,128)(2,1)}, u32[]{:S(2)}) %copy-start.4) | copy-done | bytes 2097176
  23.4 1.4 collective-permute-start.1
  24.8 39.9 %all-gather.3.cloned.1.call-done = bf16[16,2,128,256]{3,2,1,0:T(8,128)(2,1)} async-done(((bf16[2,2,128,256]{3,2,1,0:T(8,128)(2,1)}), bf16[16,2,128,256]{3,2,1,0:T(8,128)(2,1)}) %all-gather.3.cloned.1.call-update) | async-done | bytes 2097168 | tf_op jit(solution)/shard_map/all_gather | solution.py:316
  64.7 1.6 %copy-done.5 = bf16[128,8192]{1,0:T(8,128)(2,1)S(1)} copy-done((bf16[128,8192]{1,0:T(8,128)(2,1)S(1)}, bf16[128,8192]{1,0:T(8,128)(2,1)}, u32[]{:S(2)}) %copy-start.5) | copy-done | bytes 2097176
  66.3 3.8 %add.111.token = bf16[128,8192]{1,0:T(8,128)(2,1)} custom-call(bf16[128,8192]{1,0:T(8,128)(2,1)S(1)} %copy-done.5, bf16[128,8192]{1,0:T(8,128)(2,1)} %collective-permute-done.2.b_ref), custom_call_target="tpu_custom_call" | custom-call | flops 1048576 | bytes 1024 | tf_op jit(solution)/shard_map/add/pallas_call | solution.py:319
  72.1 1.4 collective-permute-done.1
  74.1 1.0 copy-done.2
  75.1 4.9 %terms.1 = (f32[8,2,2,128,256]{4,3,2,1,0:T(8,128)S(1)}, bf16[3,2,2,128,256]{4,3,2,1,0:T(8,128)(2,1)S(1)}, bf16[5,2,2,128,256]{4,3,2,1,0:T(8,128)(2,1)S(1)}, bf16...) custom-call(bf16[128,8192]{1,0:T(8,128)(2,1)} %add.111.token, ...), custom_call_target="tpu_custom_call" | custom-call | flops 1073741824 | bytes 16777216 | tf_op jit(solution)/shard_map/terms/pallas_call | solution.py:337
  80.1 2.3 %collective-permute-done.5.crossed.cross_up.cross_down = bf16[3,2,2,128,256]{4,3,2,1,0:T(8,128)(2,1)S(1)} collective-permute-done((bf16[3,2,2,128,256]{4,3,2,1,0:T(8,128)(2,1)S(1)}, bf16[3,2,2,128,256]{4,3,2,1,0:T(8,128)(2,1)S(1)}, u32[]{:S(2)}, u32[]{:S(2)}) %collective-permute-start.5) | collective-permute-done | bytes 786464 | tf_op jit(solution)/shard_map/ppermute | solution.py:29
  82.7 5.9 %collective-permute-start.7 = (bf16[1,2,128,256]{3,2,1,0:T(8,128)(2,1)S(1)}, bf16[1,2,128,256]{3,2,1,0:T(8,128)(2,1)S(1)}, u32[]{:S(2)}, u32[]{:S(2)}) collective-permute-start(bf16[1,2,128,256]{3,2,1,0:T(8,128)(2,1)S(1)} %get-tuple-element.36), channel_id=1, source_target_pairs={{0,14},{1,15},{2,0},{3,1},{4,2},{5,3},{6,4},{7,5},{8,6},{9,7},{10,... | collective-permute-start | bytes 393224 | tf_op jit(solution)/shard_map/ppermute | solution.py:29
  88.6 6.2 %collective-permute-done.7.got_down = bf16[1,2,128,256]{3,2,1,0:T(8,128)(2,1)S(1)} collective-permute-done((bf16[1,2,128,256]{3,2,1,0:T(8,128)(2,1)S(1)}, bf16[1,2,128,256]{3,2,1,0:T(8,128)(2,1)S(1)}, u32[]{:S(2)}, u32[]{:S(2)}) %collective-permute-start.7) | collective-permute-done | bytes 131104 | tf_op jit(solution)/shard_map/ppermute | solution.py:29
  94.8 3.5 %collective-permute-done.6.got_up = bf16[1,2,128,256]{3,2,1,0:T(8,128)(2,1)S(1)} collective-permute-done((bf16[1,2,128,256]{3,2,1,0:T(8,128)(2,1)S(1)}, bf16[1,2,128,256]{3,2,1,0:T(8,128)(2,1)S(1)}, u32[]{:S(2)}, u32[]{:S(2)}) %collective-permute-start.6) | collective-permute-done | bytes 131104 | tf_op jit(solution)/shard_map/ppermute | solution.py:29
  98.7 1.9 %collective-permute-start.9 = (bf16[2,2,128,256]{3,2,1,0:T(8,128)(2,1)S(1)}, bf16[2,2,128,256]{3,2,1,0:T(8,128)(2,1)S(1)}, u32[]{:S(2)}, u32[]{:S(2)}) collective-permute-start(bf16[2,2,128,256]{3,2,1,0:T(8,128)(2,1)S(1)} %get-tuple-element.37.token), channel_id=1, source_target_pairs={{0,2},{1,3},{2,4},{3,5},{4,6},{5,7},{6,8},{7,9},{8,10},{9,11},{10,... | collective-permute-start | bytes 786440 | tf_op jit(solution)/shard_map/ppermute | solution.py:29
  100.5 6.4 %outputs.1 = (bf16[128,8192]{1,0:T(8,128)(2,1)}, bf16[128,8192]{1,0:T(8,128)(2,1)}, f32[8,128]{1,0:T(8,128)S(1)}) custom-call(bf16[2,2,128,256]{3,2,1,0:T(8,128)(2,1)S(1)} %get-tuple-element.37.token, s32[34]{0:T(128)S(1)} %compare_select_fusion.5.at, bf16[128,8192]{1,0:T(8,128)(2,1)S(1)} %bitcast.14, bf16[128,8192]{1,0:T(8,128)(2,1)} %bitcast.1.g_ref, ...), custom_call_target="tpu_custom_call" | custom-call | flops 536870912 | bytes 14680064 | tf_op jit(solution)/shard_map/outputs/pallas_call | solution.py:402
  106.9 5.3 %collective-permute-done.10.got_down = bf16[2,2,128,256]{3,2,1,0:T(8,128)(2,1)S(1)} collective-permute-done((bf16[2,2,128,256]{3,2,1,0:T(8,128)(2,1)S(1)}, bf16[2,2,128,256]{3,2,1,0:T(8,128)(2,1)S(1)}, u32[]{:S(2)}, u32[]{:S(2)}) %collective-permute-start.10) | collective-permute-done | bytes 262176 | tf_op jit(solution)/shard_map/ppermute | solution.py:29
  112.1 1.0 collective-permute-done.9.got_up
  113.9 2.7 %collective-permute-start.12 = (bf16[2,2,128,256]{3,2,1,0:T(8,128)(2,1)S(1)}, bf16[2,2,128,256]{3,2,1,0:T(8,128)(2,1)S(1)}, u32[]{:S(2)}, u32[]{:S(2)}) collective-permute-start(bf16[2,2,128,256]{3,2,1,0:T(8,128)(2,1)S(1)} %get-tuple-element.47), channel_id=1, source_target_pairs={{0,14},{1,15},{2,0},{3,1},{4,2},{5,3},{6,4},{7,5},{8,6},{9,7},{10,... | collective-permute-start | bytes 786440 | tf_op jit(solution)/shard_map/ppermute | solution.py:29
  116.6 5.2 %collective-permute-done.11.got_up = bf16[2,2,128,256]{3,2,1,0:T(8,128)(2,1)S(1)} collective-permute-done((bf16[2,2,128,256]{3,2,1,0:T(8,128)(2,1)S(1)}, bf16[2,2,128,256]{3,2,1,0:T(8,128)(2,1)S(1)}, u32[]{:S(2)}, u32[]{:S(2)}) %collective-permute-start.11) | collective-permute-done | bytes 262176 | tf_op jit(solution)/shard_map/ppermute | solution.py:29
  122.1 3.0 %collective-permute-start.18 = (bf16[2,2,128,256]{3,2,1,0:T(8,128)(2,1)S(1)}, bf16[2,2,128,256]{3,2,1,0:T(8,128)(2,1)S(1)}, u32[]{:S(2)}, u32[]{:S(2)}) collective-permute-start(bf16[2,2,128,256]{3,2,1,0:T(8,128)(2,1)S(1)} %get-tuple-element.49), channel_id=1, source_target_pairs={{0,14},{1,15},{2,0},{3,1},{4,2},{5,3},{6,4},{7,5},{8,6},{9,7},{10,... | collective-permute-start | bytes 786440 | tf_op jit(solution)/shard_map/ppermute | solution.py:29
  125.1 0.9 copy-done.7
  126.2 0.9 collective-permute-start.14
  127.1 1.3 collective-permute-start.13
  128.4 2.3 %collective-permute-start.16 = (bf16[4,8192]{1,0:T(4,128)(2,1)S(1)}, bf16[4,8192]{1,0:T(4,128)(2,1)S(1)}, u32[]{:S(2)}, u32[]{:S(2)}) collective-permute-start(bf16[4,8192]{1,0:T(4,128)(2,1)S(1)} %get-tuple-element.56), channel_id=1, source_target_pairs={{0,240},{1,241},{2,242},{3,243},{4,244},{5,245},{6,246},{7,247},{8... | collective-permute-start | bytes 196616 | tf_op jit(solution)/shard_map/ppermute | solution.py:44
  130.7 2.2 %collective-permute-done.14 = bf16[4,8192]{1,0:T(4,128)(2,1)S(1)} collective-permute-done((bf16[4,8192]{1,0:T(4,128)(2,1)S(1)}, bf16[4,8192]{1,0:T(4,128)(2,1)S(1)}, u32[]{:S(2)}, u32[]{:S(2)}) %collective-permute-start.14) | collective-permute-done | bytes 65568 | tf_op jit(solution)/shard_map/ppermute | solution.py:44
  133.0 3.0 %collective-permute-done.16 = bf16[4,8192]{1,0:T(4,128)(2,1)S(1)} collective-permute-done((bf16[4,8192]{1,0:T(4,128)(2,1)S(1)}, bf16[4,8192]{1,0:T(4,128)(2,1)S(1)}, u32[]{:S(2)}, u32[]{:S(2)}) %collective-permute-start.16) | collective-permute-done | bytes 65568 | tf_op jit(solution)/shard_map/ppermute | solution.py:44
  136.0 3.3 %collective-permute-done.15 = bf16[4,8192]{1,0:T(4,128)(2,1)S(1)} collective-permute-done((bf16[4,8192]{1,0:T(4,128)(2,1)S(1)}, bf16[4,8192]{1,0:T(4,128)(2,1)S(1)}, u32[]{:S(2)}, u32[]{:S(2)}) %collective-permute-start.15) | collective-permute-done | bytes 65568 | tf_op jit(solution)/shard_map/ppermute | solution.py:44
  139.4 2.2 %copy-done.1 = f32[8,2,2,128,256]{4,3,2,1,0:T(8,128)S(1)} copy-done((f32[8,2,2,128,256]{4,3,2,1,0:T(8,128)S(1)}, f32[8,2,2,128,256]{4,3,2,1,0:T(8,128)}, u32[]{:S(2)}) %copy-start.1) | copy-done | bytes 4194328
  141.7 1.6 %collective-permute-start.19 = (bf16[2,128,256]{2,1,0:T(8,128)(2,1)S(1)}, bf16[2,128,256]{2,1,0:T(8,128)(2,1)S(1)}, u32[]{:S(2)}, u32[]{:S(2)}) collective-permute-start(bf16[2,128,256]{2,1,0:T(8,128)(2,1)S(1)} %get-tuple-element.53), channel_id=1, source_target_pairs={{0,16},{1,17},{2,18},{3,19},{4,20},{5,21},{6,22},{7,23},{8,24},{9,... | collective-permute-start | bytes 393224 | tf_op jit(solution)/shard_map/ppermute | solution.py:29
  143.3 3.7 %extras.1 = (bf16[16,8192]{1,0:T(8,128)(2,1)S(1)}, bf16[16,8192]{1,0:T(8,128)(2,1)S(1)}) custom-call(f32[2,128,256]{2,1,0:T(8,128)S(1)} %get-tuple-element.50.token.own, s32[34]{0:T(128)S(1)} %compare_select_fusion.5.at, bf16[16,8192]{1,0:T(8,128)(2,1)S(1)} %pad.7.token_1.x_ref, bf16[16,8192]{1,0:T(8,128)(2,1)S(1)} %pad.8.token_2.g_ref, ...), custom_call_target="tpu_custom_call" | custom-call | flops 134217728 | bytes 6291456 | tf_op jit(solution)/shard_map/extras/pallas_call | solution.py:448
  (61 shorter events, 8.9 us)
Async XLA Ops:
  7.2 57.6 %all-gather.3.cloned.1.call-start = ((), (), s32[]{:S(2)}) async-start(), calls=%async_computation.2 | async-start | bytes 2359296 | tf_op jit(solution)/shard_map/all_gather | solution.py:316
  7.2 0.8 copy-start.8
  8.1 0.8 copy-start.9
  8.9 11.3 %collective-permute-start.3 = (bf16[2,128,256]{2,1,0:T(8,128)(2,1)S(1)}, bf16[2,128,256]{2,1,0:T(8,128)(2,1)S(1)}, u32[]{:S(2)}, u32[]{:S(2)}) collective-permute-start(bf16[2,128,256]{2,1,0:T(8,128)(2,1)S(1)} %pair.1.mine), channel_id=1, source_target_pairs={{0,16},{1,17},{2,18},{3,19},{4,20},{5,21},{6,22},{7,23},{8,24},{9,... | collective-permute-start | bytes 393224 | tf_op jit(solution)/shard_map/ppermute | solution.py:29
  20.2 1.6 %copy-start.4 = (bf16[128,8192]{1,0:T(8,128)(2,1)S(1)}, bf16[128,8192]{1,0:T(8,128)(2,1)}, u32[]{:S(2)}) copy-start(bf16[128,8192]{1,0:T(8,128)(2,1)} %get-tuple-element.31.a_ref.token) | copy-start | bytes 6291460
  22.6 102.5 %reduce-scatter.2.cloned.1.call-start = ((), (), s32[]{:S(2)}) async-start(), calls=%async_computation.1 | async-start | bytes 2359296 | tf_op jit(solution)/shard_map/reduce_scatter | solution.py:331
  22.6 42.1 %collective-permute-start.2 = (bf16[128,8192]{1,0:T(8,128)(2,1)}, bf16[128,8192]{1,0:T(8,128)(2,1)}, u32[]{:S(2)}, u32[]{:S(2)}) collective-permute-start(bf16[128,8192]{1,0:T(8,128)(2,1)} %get-tuple-element.32), channel_id=1, source_target_pairs={{0,1},{1,0},{2,3},{3,2},{4,5},{5,4},{6,7},{7,6},{8,9},{9,8},{10,11... | collective-permute-start | bytes 6291464 | tf_op jit(solution)/shard_map/ppermute | solution.py:29
  22.7 49.4 %collective-permute-start = (bf16[1,1,128,8192]{3,2,1,0:T(8,128)(2,1)}, bf16[1,1,128,8192]{3,2,1,0:T(8,128)(2,1)S(1)}, u32[]{:S(2)}, u32[]{:S(2)}) collective-permute-start(bf16[1,1,128,8192]{3,2,1,0:T(8,128)(2,1)} %param.7), channel_id=1, source_target_pairs={{0,32},{32,64},{64,96},{96,128},{128,160},{160,192},{192,224},{224... | collective-permute-start | bytes 6291464 | tf_op jit(solution)/shard_map/ppermute | solution.py:34
  23.4 50.1 %collective-permute-start.1 = (bf16[1,1,128,8192]{3,2,1,0:T(8,128)(2,1)}, bf16[1,1,128,8192]{3,2,1,0:T(8,128)(2,1)}, u32[]{:S(2)}, u32[]{:S(2)}) collective-permute-start(bf16[1,1,128,8192]{3,2,1,0:T(8,128)(2,1)} %param.8), channel_id=1, source_target_pairs={{0,224},{32,0},{64,32},{96,64},{128,96},{160,128},{192,160},{224,1... | collective-permute-start | bytes 6291464 | tf_op jit(solution)/shard_map/ppermute | solution.py:34
  64.7 9.4 %collective-permute-start.4 = (bf16[8,2,2,128,256]{4,3,2,1,0:T(8,128)(2,1)}, bf16[8,2,2,128,256]{4,3,2,1,0:T(8,128)(2,1)}, u32[]{:S(2)}, u32[]{:S(2)}) collective-permute-start(bf16[8,2,2,128,256]{4,3,2,1,0:T(8,128)(2,1)} %bitcast.15), channel_id=1, source_target_pairs={{0,1},{1,0},{2,3},{3,2},{4,5},{5,4},{6,7},{7,6},{8,9},{9,8},{10,11... | collective-permute-start | bytes 6291464 | tf_op jit(solution)/shard_map/ppermute | solution.py:29
  64.7 1.6 %copy-start.5 = (bf16[128,8192]{1,0:T(8,128)(2,1)S(1)}, bf16[128,8192]{1,0:T(8,128)(2,1)}, u32[]{:S(2)}) copy-start(bf16[128,8192]{1,0:T(8,128)(2,1)} %get-tuple-element.31.a_ref.token) | copy-start | bytes 6291460
  73.5 1.6 %copy-start.2 = (bf16[16,2,128,256]{3,2,1,0:T(8,128)(2,1)S(1)}, bf16[16,2,128,256]{3,2,1,0:T(8,128)(2,1)}, u32[]{:S(2)}) copy-start(bf16[16,2,128,256]{3,2,1,0:T(8,128)(2,1)} %all-gather.3.cloned.1.call-done) | copy-start | bytes 6291460
  73.5 1.6 %copy-start.6 = (f32[1,8192]{1,0:T(1,128)S(1)}, f32[1,8192]{1,0:T(1,128)}, u32[]{:S(2)}) copy-start(f32[1,8192]{1,0:T(1,128)} %gain_ref.5) | copy-start | bytes 98308
  80.0 41.9 %copy-start = (f32[8,2,2,128,256]{4,3,2,1,0:T(8,128)}, f32[8,2,2,128,256]{4,3,2,1,0:T(8,128)S(1)}, u32[]{:S(2)}) copy-start(f32[8,2,2,128,256]{4,3,2,1,0:T(8,128)S(1)} %get-tuple-element.33.keep.keep_up.keep_down) | copy-start | bytes 12582916
  80.0 2.4 %collective-permute-start.5 = (bf16[3,2,2,128,256]{4,3,2,1,0:T(8,128)(2,1)S(1)}, bf16[3,2,2,128,256]{4,3,2,1,0:T(8,128)(2,1)S(1)}, u32[]{:S(2)}, u32[]{:S(2)}) collective-permute-start(bf16[3,2,2,128,256]{4,3,2,1,0:T(8,128)(2,1)S(1)} %get-tuple-element.34), channel_id=1, source_target_pairs={{0,1},{1,0},{2,3},{3,2},{4,5},{5,4},{6,7},{7,6},{8,9},{9,8},{10,11... | collective-permute-start | bytes 2359304 | tf_op jit(solution)/shard_map/ppermute | solution.py:29
  82.5 30.6 %collective-permute-start.8 = (bf16[5,2,2,128,256]{4,3,2,1,0:T(8,128)(2,1)S(1)}, bf16[5,2,2,128,256]{4,3,2,1,0:T(8,128)(2,1)S(1)}, u32[]{:S(2)}, u32[]{:S(2)}) collective-permute-start(bf16[5,2,2,128,256]{4,3,2,1,0:T(8,128)(2,1)S(1)} %later.1), channel_id=1, source_target_pairs={{0,1},{1,0},{2,3},{3,2},{4,5},{5,4},{6,7},{7,6},{8,9},{9,8},{10,11... | collective-permute-start | bytes 3932168 | tf_op jit(solution)/shard_map/ppermute | solution.py:29
  82.7 12.0 %collective-permute-start.7 = (bf16[1,2,128,256]{3,2,1,0:T(8,128)(2,1)S(1)}, bf16[1,2,128,256]{3,2,1,0:T(8,128)(2,1)S(1)}, u32[]{:S(2)}, u32[]{:S(2)}) collective-permute-start(bf16[1,2,128,256]{3,2,1,0:T(8,128)(2,1)S(1)} %get-tuple-element.36), channel_id=1, source_target_pairs={{0,14},{1,15},{2,0},{3,1},{4,2},{5,3},{6,4},{7,5},{8,6},{9,7},{10,... | collective-permute-start | bytes 393224 | tf_op jit(solution)/shard_map/ppermute | solution.py:29
  88.6 9.7 %collective-permute-start.6 = (bf16[1,2,128,256]{3,2,1,0:T(8,128)(2,1)S(1)}, bf16[1,2,128,256]{3,2,1,0:T(8,128)(2,1)S(1)}, u32[]{:S(2)}, u32[]{:S(2)}) collective-permute-start(bf16[1,2,128,256]{3,2,1,0:T(8,128)(2,1)S(1)} %get-tuple-element.35.token), channel_id=1, source_target_pairs={{0,2},{1,3},{2,4},{3,5},{4,6},{5,7},{6,8},{7,9},{8,10},{9,11},{10,... | collective-permute-start | bytes 393224 | tf_op jit(solution)/shard_map/ppermute | solution.py:29
  98.4 13.7 %collective-permute-start.10 = (bf16[2,2,128,256]{3,2,1,0:T(8,128)(2,1)S(1)}, bf16[2,2,128,256]{3,2,1,0:T(8,128)(2,1)S(1)}, u32[]{:S(2)}, u32[]{:S(2)}) collective-permute-start(bf16[2,2,128,256]{3,2,1,0:T(8,128)(2,1)S(1)} %get-tuple-element.45), channel_id=1, source_target_pairs={{0,14},{1,15},{2,0},{3,1},{4,2},{5,3},{6,4},{7,5},{8,6},{9,7},{10,... | collective-permute-start | bytes 786440 | tf_op jit(solution)/shard_map/ppermute | solution.py:29
  98.7 14.5 %collective-permute-start.9 = (bf16[2,2,128,256]{3,2,1,0:T(8,128)(2,1)S(1)}, bf16[2,2,128,256]{3,2,1,0:T(8,128)(2,1)S(1)}, u32[]{:S(2)}, u32[]{:S(2)}) collective-permute-start(bf16[2,2,128,256]{3,2,1,0:T(8,128)(2,1)S(1)} %get-tuple-element.37.token), channel_id=1, source_target_pairs={{0,2},{1,3},{2,4},{3,5},{4,6},{5,7},{6,8},{7,9},{8,10},{9,11},{10,... | collective-permute-start | bytes 786440 | tf_op jit(solution)/shard_map/ppermute | solution.py:29
  113.3 8.6 %collective-permute-start.11 = (bf16[2,2,128,256]{3,2,1,0:T(8,128)(2,1)S(1)}, bf16[2,2,128,256]{3,2,1,0:T(8,128)(2,1)S(1)}, u32[]{:S(2)}, u32[]{:S(2)}) collective-permute-start(bf16[2,2,128,256]{3,2,1,0:T(8,128)(2,1)S(1)} %get-tuple-element.46), channel_id=1, source_target_pairs={{0,2},{1,3},{2,4},{3,5},{4,6},{5,7},{6,8},{7,9},{8,10},{9,11},{10,... | collective-permute-start | bytes 786440 | tf_op jit(solution)/shard_map/ppermute | solution.py:29
  113.9 8.0 %collective-permute-start.12 = (bf16[2,2,128,256]{3,2,1,0:T(8,128)(2,1)S(1)}, bf16[2,2,128,256]{3,2,1,0:T(8,128)(2,1)S(1)}, u32[]{:S(2)}, u32[]{:S(2)}) collective-permute-start(bf16[2,2,128,256]{3,2,1,0:T(8,128)(2,1)S(1)} %get-tuple-element.47), channel_id=1, source_target_pairs={{0,14},{1,15},{2,0},{3,1},{4,2},{5,3},{6,4},{7,5},{8,6},{9,7},{10,... | collective-permute-start | bytes 786440 | tf_op jit(solution)/shard_map/ppermute | solution.py:29
  122.1 17.3 %collective-permute-start.18 = (bf16[2,2,128,256]{3,2,1,0:T(8,128)(2,1)S(1)}, bf16[2,2,128,256]{3,2,1,0:T(8,128)(2,1)S(1)}, u32[]{:S(2)}, u32[]{:S(2)}) collective-permute-start(bf16[2,2,128,256]{3,2,1,0:T(8,128)(2,1)S(1)} %get-tuple-element.49), channel_id=1, source_target_pairs={{0,14},{1,15},{2,0},{3,1},{4,2},{5,3},{6,4},{7,5},{8,6},{9,7},{10,... | collective-permute-start | bytes 786440 | tf_op jit(solution)/shard_map/ppermute | solution.py:29
  125.1 14.3 %collective-permute-start.17 = (bf16[2,2,128,256]{3,2,1,0:T(8,128)(2,1)S(1)}, bf16[2,2,128,256]{3,2,1,0:T(8,128)(2,1)S(1)}, u32[]{:S(2)}, u32[]{:S(2)}) collective-permute-start(bf16[2,2,128,256]{3,2,1,0:T(8,128)(2,1)S(1)} %get-tuple-element.48.token), channel_id=1, source_target_pairs={{0,2},{1,3},{2,4},{3,5},{4,6},{5,7},{6,8},{7,9},{8,10},{9,11},{10,... | collective-permute-start | bytes 786440 | tf_op jit(solution)/shard_map/ppermute | solution.py:29
  125.1 1.0 copy-start.7
  126.2 6.7 %collective-permute-start.14 = (bf16[4,8192]{1,0:T(4,128)(2,1)S(1)}, bf16[4,8192]{1,0:T(4,128)(2,1)S(1)}, u32[]{:S(2)}, u32[]{:S(2)}) collective-permute-start(bf16[4,8192]{1,0:T(4,128)(2,1)S(1)} %get-tuple-element.58), channel_id=1, source_target_pairs={{0,48},{1,49},{2,50},{3,51},{4,52},{5,53},{6,54},{7,55},{8,56},{9,... | collective-permute-start | bytes 196616 | tf_op jit(solution)/shard_map/ppermute | solution.py:44
  127.1 5.8 %collective-permute-start.13 = (bf16[4,8192]{1,0:T(4,128)(2,1)S(1)}, bf16[4,8192]{1,0:T(4,128)(2,1)S(1)}, u32[]{:S(2)}, u32[]{:S(2)}) collective-permute-start(bf16[4,8192]{1,0:T(4,128)(2,1)S(1)} %get-tuple-element.59), channel_id=1, source_target_pairs={{0,32},{1,33},{2,34},{3,35},{4,36},{5,37},{6,38},{7,39},{8,40},{9,... | collective-permute-start | bytes 196616 | tf_op jit(solution)/shard_map/ppermute | solution.py:44
  128.4 7.6 %collective-permute-start.16 = (bf16[4,8192]{1,0:T(4,128)(2,1)S(1)}, bf16[4,8192]{1,0:T(4,128)(2,1)S(1)}, u32[]{:S(2)}, u32[]{:S(2)}) collective-permute-start(bf16[4,8192]{1,0:T(4,128)(2,1)S(1)} %get-tuple-element.56), channel_id=1, source_target_pairs={{0,240},{1,241},{2,242},{3,243},{4,244},{5,245},{6,246},{7,247},{8... | collective-permute-start | bytes 196616 | tf_op jit(solution)/shard_map/ppermute | solution.py:44
  132.9 6.4 %collective-permute-start.15 = (bf16[4,8192]{1,0:T(4,128)(2,1)S(1)}, bf16[4,8192]{1,0:T(4,128)(2,1)S(1)}, u32[]{:S(2)}, u32[]{:S(2)}) collective-permute-start(bf16[4,8192]{1,0:T(4,128)(2,1)S(1)} %get-tuple-element.57), channel_id=1, source_target_pairs={{0,224},{1,225},{2,226},{3,227},{4,228},{5,229},{6,230},{7,231},{8... | collective-permute-start | bytes 196616 | tf_op jit(solution)/shard_map/ppermute | solution.py:44
  139.4 2.2 %copy-start.1 = (f32[8,2,2,128,256]{4,3,2,1,0:T(8,128)S(1)}, f32[8,2,2,128,256]{4,3,2,1,0:T(8,128)}, u32[]{:S(2)}) copy-start(f32[8,2,2,128,256]{4,3,2,1,0:T(8,128)} %copy-done) | copy-start | bytes 12582916
  141.6 1.7 %copy-start.3 = (bf16[16,2,128,256]{3,2,1,0:T(8,128)(2,1)S(1)}, bf16[16,2,128,256]{3,2,1,0:T(8,128)(2,1)}, u32[]{:S(2)}) copy-start(bf16[16,2,128,256]{3,2,1,0:T(8,128)(2,1)} %all-gather.3.cloned.1.call-done) | copy-start | bytes 6291460
  141.7 6.6 %collective-permute-start.19 = (bf16[2,128,256]{2,1,0:T(8,128)(2,1)S(1)}, bf16[2,128,256]{2,1,0:T(8,128)(2,1)S(1)}, u32[]{:S(2)}, u32[]{:S(2)}) collective-permute-start(bf16[2,128,256]{2,1,0:T(8,128)(2,1)S(1)} %get-tuple-element.53), channel_id=1, source_target_pairs={{0,16},{1,17},{2,18},{3,19},{4,20},{5,21},{6,22},{7,23},{8,24},{9,... | collective-permute-start | bytes 393224 | tf_op jit(solution)/shard_map/ppermute | solution.py:29
  (1 other events, 0.7 us)
Sparse Core Ops, SparseCore 0:
  22.7 41.9 all-gather.2
  70.3 45.7 reduce-scatter.1
